TPU v7x, 512 devices: a whole 4x4x16 slice. The times are simulated.
512 devices in a mesh: dp: 32 (over z, core), adapter: 16 (over x, y).
Axes of the slice: x: 4, y: 4, z: 16, core: 2. Of those that a mesh axis runs over, the one named last changes fastest.
Arguments:
- activations: bfloat16 [32768, 8192], P('dp', 'adapter'), may hold values from -6 to 6
- cotangent: bfloat16 [32768, 8192], P('dp', 'adapter'), may hold values from -24 to 24
- adapter_down_weights: bfloat16 [64, 8192, 64], P('dp', 'adapter'), may hold values from -0.0625 to 0.0625
- adapter_up_weights: bfloat16 [64, 64, 8192], P('dp', None, 'adapter'), may hold values from -0.125 to 0.125
- adapter_of_block: int32 [256], replicated, may hold values from 0 to 63, as said below
Outputs:
- adapter_branch_output: bfloat16 [32768, 8192], P('dp', 'adapter')
- input_grad: bfloat16 [32768, 8192], P('dp', 'adapter')
- down_grad: float32 [64, 8192, 64], P('dp', 'adapter')
- up_grad: float32 [64, 64, 8192], P('dp', None, 'adapter')
Inputs may be any that keep to these rules, and one draw needn't show every extreme that they name: `adapter_of_block`: the blocks 8 * p to 8 * p + 8 - 1 (those of index p of dp) name adapters of distinct owners, where the owner of adapter a is a // 2. Every adapter is named by some block, and some owner is named by a block of every index of dp.
All inputs are finite; a program needn't handle non-finite values.
Results may differ from a plain program's by a relative error of at most 0.0049.
Values may be sent and summed in bfloat16 or wider, within the bound.
No kernel may reach another device: no remote copies, remote signals or barrier semaphores. Data moves between devices by JAX's collectives and lax.ppermute only.
A program may use at most 64 MiB of HBM per device.

v0:
```python
import jax
import jax.numpy as jnp
from jax import lax
from jax.sharding import PartitionSpec as P

BLOCK = 128


adapter_scale = 2.0


def local(activations, cotangent, adapter_down_weights, adapter_up_weights, adapter_of_block):
    groups = lax.axis_size("dp")
    position = lax.axis_index("dp")
    owner_share = adapter_down_weights.shape[0]
    feature_width = activations.shape[1]
    rank_extent = adapter_down_weights.shape[2]
    resident_tokens = activations.shape[0]
    local_blocks = resident_tokens // BLOCK
    table = adapter_of_block.reshape(groups, local_blocks)
    mine = lax.dynamic_slice_in_dim(adapter_of_block, position * local_blocks, local_blocks)
    mine_owner = mine // owner_share
    local_ids = position * owner_share + jnp.arange(owner_share, dtype=jnp.int32)
    usage = jnp.any(table[:, :, None] == local_ids[None, None, :], axis=1)
    all_down, all_up = (
        lax.all_gather(adapter_down_weights, "dp", axis=0, tiled=True),
        lax.all_gather(adapter_up_weights, "dp", axis=0, tiled=True),
    )
    down_sel = jnp.take(all_down, mine, axis=0)
    up_sel = jnp.take(all_up, mine, axis=0)
    rows_in = activations.reshape(local_blocks, BLOCK, feature_width)
    rows_companion = cotangent.reshape(local_blocks, BLOCK, feature_width)
    proj_part = jnp.einsum(
        "bnd,bdr->bnr", rows_in, down_sel, preferred_element_type=jnp.float32
    ).reshape(resident_tokens, rank_extent)
    backward_piece = adapter_scale * jnp.einsum(
        "bnd,brd->bnr", rows_companion, up_sel, preferred_element_type=jnp.float32
    ).reshape(resident_tokens, rank_extent)
    proj_total, back_total = lax.psum((proj_part, backward_piece), "adapter")
    projected = proj_total.astype(jnp.bfloat16)
    backward = back_total.astype(jnp.bfloat16)
    proj_blocks = projected.reshape(local_blocks, BLOCK, rank_extent)
    back_blocks = backward.reshape(local_blocks, BLOCK, rank_extent)
    adapter_branch_output = (
        adapter_scale
        * jnp.einsum("bnr,brd->bnd", proj_blocks, up_sel, preferred_element_type=jnp.float32)
    ).astype(jnp.bfloat16)
    input_grad = jnp.einsum(
        "bnr,bdr->bnd", back_blocks, down_sel, preferred_element_type=jnp.float32
    ).astype(jnp.bfloat16)
    down_part = jnp.einsum(
        "bnd,bnr->bdr", rows_in, back_blocks, preferred_element_type=jnp.float32
    ).astype(jnp.bfloat16)
    up_piece = (
        adapter_scale
        * jnp.einsum(
            "bnr,bnd->brd", proj_blocks, rows_companion, preferred_element_type=jnp.float32
        )
    ).astype(jnp.bfloat16)
    routing = (mine_owner[None, :] == jnp.arange(groups, dtype=jnp.int32)[:, None]).astype(
        jnp.bfloat16
    )
    slot_down = jnp.einsum(
        "sb,bdr->sdr", routing, down_part, preferred_element_type=jnp.float32
    ).astype(jnp.bfloat16)
    slot_up = jnp.einsum(
        "sb,brd->srd", routing, up_piece, preferred_element_type=jnp.float32
    ).astype(jnp.bfloat16)
    recv_down, recv_up = (
        lax.all_to_all(slot_down, "dp", split_axis=0, concat_axis=0, tiled=True),
        lax.all_to_all(slot_up, "dp", split_axis=0, concat_axis=0, tiled=True),
    )
    counts = (
        jnp.sum((adapter_of_block[:, None] == local_ids[None, :]).astype(jnp.float32), axis=0)
        * BLOCK
    )
    weighting = usage.astype(jnp.bfloat16)
    down_grad = (
        jnp.einsum("sk,sdr->kdr", weighting, recv_down, preferred_element_type=jnp.float32)
        / counts[:, None, None]
    )
    up_grad = (
        jnp.einsum("sk,srd->krd", weighting, recv_up, preferred_element_type=jnp.float32)
        / counts[:, None, None]
    )
    return (
        adapter_branch_output.reshape(resident_tokens, feature_width),
        input_grad.reshape(resident_tokens, feature_width),
        down_grad,
        up_grad,
    )


def solution(mesh):
    return jax.shard_map(
        local,
        mesh=mesh,
        in_specs=(
            P("dp", "adapter"),
            P("dp", "adapter"),
            P("dp", "adapter", None),
            P("dp", None, "adapter"),
            P(),
        ),
        out_specs=(
            P("dp", "adapter"),
            P("dp", "adapter"),
            P("dp", "adapter", None),
            P("dp", None, "adapter"),
        ),
        check_vma=False,
    )
```

profile of v0, /device:TPU:1, one launch (start us, length us, event | category | flops | bytes accessed | tf_op | source)
XLA Modules:
  0.0 474.8 jit_solution(8204605688675606517)
XLA Ops:
  8.7 0.8 and_select_fusion
  9.4 0.8 compare_and_fusion
  10.2 79.4 %all-gather.3.cloned.1.call-done = bf16[64,512,64]{1,2,0:T(8,128)(2,1)} async-done(((bf16[2,512,64]{1,2,0:T(8,128)(2,1)}), bf16[64,512,64]{1,2,0:T(8,128)(2,1)}) %all-gather.3.cloned.1.call-update) | async-done | bytes 4194320 | tf_op jit(solution)/shard_map/all_gather | solution.py:26
  89.6 2.8 gather_fusion
  92.4 1.2 convolution_bitcast_fusion
  93.6 69.0 %all-gather.5.cloned.1.call-done = bf16[64,64,512]{2,1,0:T(8,128)(2,1)} async-done(((bf16[2,64,512]{2,1,0:T(8,128)(2,1)}), bf16[64,64,512]{2,1,0:T(8,128)(2,1)}) %all-gather.5.cloned.1.call-update) | async-done | bytes 4194320 | tf_op jit(solution)/shard_map/all_gather | solution.py:27
  162.7 2.8 gather_fusion.1
  166.0 1.7 copy_bitcast_fusion
  167.7 66.7 %all-reduce.2 = (bf16[1024,64]{0,1:T(8,128)(2,1)S(1)}, bf16[1024,64]{0,1:T(8,128)(2,1)}) all-reduce(f32[1024,64]{0,1:T(8,128)} %get-tuple-element.25, f32[1024,64]{0,1:T(8,128)S(1)} %get-tuple-element.24), channel_id=1, replica_groups=mesh['dp'=32,'adapter'=16] {'adapter'}, use_global_device_ids=true, to_apply=%region_0.1 | all-reduce | flops 131072 | bytes 786432 | tf_op jit(solution)/shard_map/psum | solution.py:39
  234.4 1.2 fusion.5
  235.6 0.8 convolution_convert_fusion.1
  236.4 2.5 copy.38
  238.9 22.4 %all-to-all-start = ((bf16[32,512,64]{1,2,0:T(8,128)(2,1)}), bf16[32,512,64]{1,2,0:T(8,128)(2,1)}, u32[]{:S(2)}, u32[]{:S(2)}) async-start(bf16[32,512,64]{1,2,0:T(8,128)(2,1)} %copy.38), calls=%async_computation | async-start | bytes 4194304 | tf_op jit(solution)/shard_map/all_to_all | solution.py:70
  261.6 0.8 convolution_convert_fusion
  262.5 2.5 copy.42
  264.9 95.0 %all-to-all-done = bf16[32,512,64]{1,2,0:T(8,128)(2,1)} async-done(((bf16[32,512,64]{1,2,0:T(8,128)(2,1)}), bf16[32,512,64]{1,2,0:T(8,128)(2,1)}, u32[]{:S(2)}, u32[]{:S(2)}) %all-to-all-start) | async-done | bytes 2097184 | tf_op jit(solution)/shard_map/all_to_all | solution.py:70
  360.0 5.2 %all-to-all-start.1 = ((bf16[32,64,512]{2,1,0:T(8,128)(2,1)}), bf16[32,64,512]{2,1,0:T(8,128)(2,1)}, u32[]{:S(2)}, u32[]{:S(2)}) async-start(bf16[32,64,512]{2,1,0:T(8,128)(2,1)} %copy.42), calls=%async_computation.1 | async-start | bytes 4194304 | tf_op jit(solution)/shard_map/all_to_all | solution.py:71
  365.7 1.5 convolution_convert_fusion.2
  367.1 1.5 multiply_convert_fusion
  368.6 2.9 fusion.7
  371.5 0.8 copy.44
  372.2 92.1 %all-to-all-done.1 = bf16[32,64,512]{2,1,0:T(8,128)(2,1)} async-done(((bf16[32,64,512]{2,1,0:T(8,128)(2,1)}), bf16[32,64,512]{2,1,0:T(8,128)(2,1)}, u32[]{:S(2)}, u32[]{:S(2)}) %all-to-all-start.1) | async-done | bytes 2097184 | tf_op jit(solution)/shard_map/all_to_all | solution.py:71
  464.4 2.9 fusion.10
  467.2 0.8 copy.45
  (21 shorter events, 2.7 us)
Async XLA Ops:
  7.2 85.3 %copy-start = (bf16[1024,512]{1,0:T(8,128)(2,1)S(1)}, bf16[1024,512]{1,0:T(8,128)(2,1)}, u32[]{:S(2)}) copy-start(bf16[1024,512]{1,0:T(8,128)(2,1)} %param.5) | copy-start | bytes 3145732
  7.2 82.5 %all-gather.3.cloned.1.call-start = ((), (), s32[]{:S(2)}) async-start(), calls=%async_computation.2 | async-start | bytes 4325376 | tf_op jit(solution)/shard_map/all_gather | solution.py:26
  7.9 154.8 %all-gather.5.cloned.1.call-start = ((), (), s32[]{:S(2)}) async-start(), calls=%async_computation.3 | async-start | bytes 4325376 | tf_op jit(solution)/shard_map/all_gather | solution.py:27
  10.2 155.2 %copy-start.1 = (bf16[1024,512]{1,0:T(8,128)(2,1)S(1)}, bf16[1024,512]{1,0:T(8,128)(2,1)}, u32[]{:S(2)}) copy-start(bf16[1024,512]{1,0:T(8,128)(2,1)} %param.6) | copy-start | bytes 3145732
  238.9 121.0 %all-to-all-start = ((bf16[32,512,64]{1,2,0:T(8,128)(2,1)}), bf16[32,512,64]{1,2,0:T(8,128)(2,1)}, u32[]{:S(2)}, u32[]{:S(2)}) async-start(bf16[32,512,64]{1,2,0:T(8,128)(2,1)} %copy.38), calls=%async_computation | async-start | bytes 4194304 | tf_op jit(solution)/shard_map/all_to_all | solution.py:70
  264.9 100.3 %copy-start.3 = (s32[256]{0:T(256)S(1)}, s32[256]{0:T(256)}, u32[]{:S(2)}) copy-start(s32[256]{0:T(256)} %param.9) | copy-start | bytes 3076
  264.9 100.7 %copy-start.2 = (bf16[1024,64]{0,1:T(8,128)(2,1)S(1)}, bf16[1024,64]{0,1:T(8,128)(2,1)}, u32[]{:S(2)}) copy-start(bf16[1024,64]{0,1:T(8,128)(2,1)} %get-tuple-element.21) | copy-start | bytes 393220
  360.0 104.4 %all-to-all-start.1 = ((bf16[32,64,512]{2,1,0:T(8,128)(2,1)}), bf16[32,64,512]{2,1,0:T(8,128)(2,1)}, u32[]{:S(2)}, u32[]{:S(2)}) async-start(bf16[32,64,512]{2,1,0:T(8,128)(2,1)} %copy.42), calls=%async_computation.1 | async-start | bytes 4194304 | tf_op jit(solution)/shard_map/all_to_all | solution.py:71
Sparse Core Ops, SparseCore 0:
  10.1 79.4 all-gather.2
  91.8 70.8 all-gather.4
where the time goes:
time: 475 us
  waiting for transfers between devices  337 us (71%)
  blocking collectives  66.7 us (14%)
  starting transfers between devices  27.7 us (6%)
  between operations  14.2 us (3%)
  local copies, waits for them, and re-layouts  13.9 us (3%)
  matrix products  13.5 us (3%)
    all_to_all x1, waiting for transfers between devices, local(): lax.all_to_all(slot_down, 'dp', split_axis=0, concat_axis=0, tiled=True)  95 us
    all_to_all x1, waiting for transfers between devices, local(): lax.all_to_all(slot_up, 'dp', split_axis=0, concat_axis=0, tiled=True)  92.1 us
    all_gather x1, waiting for transfers between devices, local(): lax.all_gather(adapter_down_weights, 'dp', axis=0, tiled=True)  79.4 us
    all_gather x1, waiting for transfers between devices, local(): lax.all_gather(adapter_up_weights, 'dp', axis=0, tiled=True)  69 us
    psum x1, blocking collectives, local(): proj_total, back_total = lax.psum((proj_part, backward_piece), 'adapter')  66.7 us
    all_to_all x1, starting transfers between devices, local(): lax.all_to_all(slot_down, 'dp', split_axis=0, concat_axis=0, tiled=True)  22.4 us
  transfers between devices with their start and end apart: 4, of which 4 were waited for; matrix products, arithmetic and copies ran while one was open for 3% of the time, Pallas kernels for 0%

commit v1 on v0

v1 whole, which is shorter than its diff:
```python
import jax
import jax.numpy as jnp
from jax import lax
from jax.experimental import pallas as pl
from jax.experimental.pallas import tpu as pltpu
from jax.sharding import Mesh, PartitionSpec as P

BLOCK = 128
SCALE = 2.0
CORES = 2
PIECE = (16, 128)
F32, BF16 = jnp.float32, jnp.bfloat16

VMEM = pl.BlockSpec(memory_space=pltpu.VMEM)
SMEM = pl.BlockSpec(memory_space=pltpu.SMEM)
ANY = pl.BlockSpec(memory_space=pl.ANY)
NT = (((1,), (1,)), ((), ()))
NN = (((1,), (0,)), ((), ()))
TN = (((0,), (0,)), ((), ()))


def dot(a, b, dims):
    return lax.dot_general(a, b, dims, preferred_element_type=F32)


def call(body, outs, ins, in_specs, scratch=(), out_specs=None):
    return pl.pallas_call(
        body,
        out_shape=outs,
        in_specs=in_specs,
        out_specs=out_specs or jax.tree.map(lambda _: VMEM, outs),
        scratch_shapes=list(scratch),
        compiler_params=pltpu.CompilerParams(vmem_limit_bytes=40 * 2**20),
    )(*ins)


def shape(dims, kind):
    return jax.ShapeDtypeStruct(dims, kind)


def named(table, where, dev_z, core, block, blocks):
    adapter = table[(dev_z * CORES + core) * blocks + block]
    owner = adapter // 2
    return owner % 2, (owner // 2) * 2 + adapter % 2


def pick_pieces(table, where, mine, other, out):
    nz, blocks = out.shape[0], out.shape[1]
    core = where[1]

    def step(i, _):
        z, b = i // blocks, i % blocks
        par, row = named(table, where, z, core, b, blocks)
        out[z, b] = jnp.where(par == core, mine[row], other[row])
        return 0

    lax.fori_loop(0, nz * blocks, step, 0, unroll=8)


def assemble(pieces, b, per_row):
    rows = []
    for i in range(pieces.shape[0] // per_row):
        rows.append(jnp.concatenate([pieces[i * per_row + j, b] for j in range(per_row)], axis=1))
    return jnp.concatenate(rows, axis=0)


def pad_low(w):
    return jnp.concatenate([w, jnp.zeros_like(w)], axis=0)


def pad_high(w):
    return jnp.concatenate([jnp.zeros_like(w), w], axis=0)


def rows_of(ref, b):
    return ref[b * BLOCK:(b + 1) * BLOCK, :]


def back_partial(cot, pieces, out):
    half = pieces.shape[1] // 2
    per_row = cot.shape[1] // PIECE[1]
    for j in range(half):
        low = dot(rows_of(cot, j), pad_low(assemble(pieces, j, per_row)), NT)
        high = dot(rows_of(cot, j + half), pad_high(assemble(pieces, j + half, per_row)), NT)
        out[j * BLOCK:(j + 1) * BLOCK, :] = SCALE * (low + high)


def grads_down(acts, back, out):
    half = out.shape[0] // 2
    rank = out.shape[1]
    for j in range(half):
        b = rows_of(back, j)
        out[j] = dot(b, rows_of(acts, j), TN)[:rank].astype(BF16)
        out[j + half] = dot(b, rows_of(acts, j + half), TN)[rank:].astype(BF16)


def grads_up(cot, proj, out):
    half = out.shape[1] // 2
    per_row = cot.shape[1] // PIECE[1]
    rank = out.shape[0] // per_row * PIECE[0]

    def put(b, g):
        g = (SCALE * g).astype(BF16)
        for i in range(rank // PIECE[0]):
            for j in range(per_row):
                out[i * per_row + j, b] = g[i * PIECE[0]:(i + 1) * PIECE[0], j * PIECE[1]:(j + 1) * PIECE[1]]

    for j in range(half):
        p = rows_of(proj, j)
        put(j, dot(p, rows_of(cot, j), TN)[:rank])
        put(j + half, dot(p, rows_of(cot, j + half), TN)[rank:])


def sum_pieces(table, where, got, keep, send, acc):
    nz, blocks = got.shape[0], got.shape[1]
    core = where[1]
    half = keep.shape[0]
    acc[...] = jnp.zeros_like(acc)

    def step(i, _):
        z, b = i // blocks, i % blocks
        par, row = named(table, where, z, core, b, blocks)
        at = par * half + row
        acc[at] = acc[at] + got[z, b].astype(F32)
        return 0

    lax.fori_loop(0, nz * blocks, step, 0, unroll=8)
    keep[...] = acc[pl.ds(core * half, half)]
    send[...] = acc[pl.ds((1 - core) * half, half)]


def pick_for_other(table, where, gathered, out, sems):
    blocks = out.shape[0]
    copies = []
    for b in range(blocks):
        _, row = named(table, where, where[0], 1 - where[1], b, blocks)
        copies.append(pltpu.make_async_copy(gathered.at[row], out.at[b], sems.at[b]))
    for c in copies:
        c.start()
    for c in copies:
        c.wait()


def proj_partial(table, where, acts, gathered, other, out, chosen, sems):
    blocks = chosen.shape[0]
    half = blocks // 2
    core = where[1]
    copies, pars = [], []
    for b in range(blocks):
        par, row = named(table, where, where[0], core, b, blocks)
        copies.append(pltpu.make_async_copy(gathered.at[row], chosen.at[b], sems.at[b]))
        pars.append(par)
    for c in copies:
        c.start()
    for b in range(blocks):
        copies[b].wait()
        chosen[b] = jnp.where(pars[b] == core, chosen[b], other[b])
    for j in range(half):
        low = dot(rows_of(acts, j), pad_low(chosen[j]), NT)
        high = dot(rows_of(acts, j + half), pad_high(chosen[j + half]), NT)
        out[j * BLOCK:(j + 1) * BLOCK, :] = low + high


def place_parts(table, where, mine, other, out):
    blocks = mine.shape[0]
    core = where[1]
    out[...] = jnp.zeros_like(out)
    for b in range(blocks):
        par, row = named(table, where, where[0], core, b, blocks)

        @pl.when(par == core)
        def _():
            out[row] = mine[b]

    for b in range(blocks):
        par, row = named(table, where, where[0], 1 - core, b, blocks)

        @pl.when(par == core)
        def _():
            out[row] = (out[row].astype(F32) + other[b].astype(F32)).astype(BF16)


def outputs(proj, back, pieces, chosen, out, grad):
    half = chosen.shape[0] // 2
    per_row = out.shape[1] // PIECE[1]
    for b in range(2 * half):
        pad = pad_low if b < half else pad_high
        p, k = rows_of(proj, b % half), rows_of(back, b % half)
        out[b * BLOCK:(b + 1) * BLOCK, :] = (SCALE * dot(p, pad(assemble(pieces, b, per_row)), NN)).astype(BF16)
        grad[b * BLOCK:(b + 1) * BLOCK, :] = dot(k, pad(chosen[b]), NN).astype(BF16)


def local(activations, cotangent, adapter_down_weights, adapter_up_weights, table):
    nz, nxy = lax.axis_size("z"), lax.axis_size("xy")
    share, width, rank = adapter_down_weights.shape
    tokens = activations.shape[0]
    blocks = tokens // BLOCK
    across, along = rank // PIECE[0], width // PIECE[1]
    where = jnp.stack([lax.axis_index("z"), lax.axis_index("core")]).astype(jnp.int32)
    swap = [(0, 1), (1, 0)]
    own = nz * share

    def over_z(x):
        return lax.all_to_all(x, "z", 0, 0, tiled=True)

    def total(part):
        rows = part.shape[0] // nxy
        got = lax.all_to_all(part.reshape(nxy, rows, part.shape[1]), "xy", 0, 0, tiled=True)
        mine = jnp.sum(got, axis=0).astype(BF16)
        spread = jnp.broadcast_to(mine[None], (nxy,) + mine.shape)
        return lax.all_to_all(spread, "xy", 0, 0, tiled=True).reshape(part.shape)

    gathered = lax.all_gather(jnp.swapaxes(adapter_down_weights, 1, 2), "z", tiled=True)

    cut = adapter_up_weights.reshape(share, across, PIECE[0], along, PIECE[1])
    cut = cut.transpose(1, 3, 0, 2, 4).reshape(nz, share, *PIECE)
    held = over_z(cut).reshape(own, *PIECE)
    held_other = lax.ppermute(held, "core", swap)
    wanted = call(pick_pieces, shape((nz, blocks) + PIECE, BF16), (table, where, held, held_other), [SMEM, SMEM, VMEM, VMEM])
    pieces = over_z(wanted)
    back = total(call(back_partial, shape((tokens // 2, 2 * rank), F32), (cotangent, pieces), [VMEM, VMEM]))

    part_down = call(grads_down, shape((blocks, rank, width), BF16), (activations, back), [VMEM, VMEM])
    part_other = lax.ppermute(part_down, "core", swap)
    placed = call(place_parts, shape((own, rank, width), BF16), (table, where, part_down, part_other), [SMEM, SMEM, VMEM, VMEM])
    summed = lax.psum_scatter(placed, "z", scatter_dimension=0, tiled=True)

    gathered, _ = lax.optimization_barrier((gathered, back))
    for_other = call(
        pick_for_other, shape((blocks, rank, width), BF16), (table, where, gathered), [SMEM, SMEM, ANY],
        [pltpu.SemaphoreType.DMA((blocks,))],
    )
    from_other = lax.ppermute(for_other, "core", swap)
    proj_part, chosen = call(
        proj_partial,
        (shape((tokens // 2, 2 * rank), F32), shape((blocks, rank, width), BF16)),
        (table, where, activations, gathered, from_other),
        [SMEM, SMEM, VMEM, ANY, VMEM],
        [pltpu.SemaphoreType.DMA((blocks,))],
    )
    proj = total(proj_part)
    part_up = call(grads_up, shape((nz, blocks) + PIECE, BF16), (cotangent, proj), [VMEM, VMEM])
    got = over_z(part_up)
    keep, send = call(
        sum_pieces, (shape((own,) + PIECE, F32),) * 2, (table, where, got), [SMEM, SMEM, VMEM],
        [pltpu.VMEM((CORES * own,) + PIECE, F32)],
    )
    merged = (keep + lax.ppermute(send, "core", swap)).astype(BF16)
    owned = over_z(merged.reshape(nz, share, *PIECE))

    out, grad = call(
        outputs, (shape((tokens, width), BF16),) * 2, (proj, back, pieces, chosen), [VMEM] * 4,
    )

    ids = (where[0] * CORES + where[1]) * share + jnp.arange(share, dtype=jnp.int32)
    counts = jnp.sum((table[:, None] == ids[None, :]).astype(F32), axis=0) * BLOCK
    counts = counts[:, None, None]
    down_grad = jnp.swapaxes(summed.astype(F32) / counts, 1, 2)
    up_grad = owned.reshape(across, along, share, *PIECE).transpose(2, 0, 3, 1, 4)
    up_grad = up_grad.reshape(share, rank, width).astype(F32) / counts
    return out, grad, down_grad, up_grad


def solution(mesh):
    nxy = mesh.shape["adapter"]
    grid = Mesh(mesh.devices.reshape(-1, CORES, nxy), ("z", "core", "xy"))
    dp = ("z", "core")
    specs = (P(dp, "xy"), P(dp, "xy"), P(dp, "xy", None), P(dp, None, "xy"))
    return jax.shard_map(
        local, mesh=grid, in_specs=specs + (P(),), out_specs=specs, check_vma=False
    )
```

time: 475 us -> 228 us (0.48)
  the two profiles are of different devices: /device:TPU:1 before, /device:TPU:32 now
where the time goes in v1:
time: 228 us; the launch traced here: 227 us
  blocking collectives  157 us (69%)
  waiting for transfers between devices  18.9 us (8%)
  Pallas kernels  15.5 us (7%)
  starting transfers between devices  14.9 us (7%)
  between operations  14.2 us (6%)
  local copies, waits for them, and re-layouts  3.45 us (2%)
  other arithmetic  2.83 us (1%)
    all_to_all x3, blocking collectives, over_z(): return lax.all_to_all(x, 'z', 0, 0, tiled=True)  108 us
    all_to_all x2, blocking collectives, total(): lax.all_to_all(part.reshape(nxy, rows, part.shape[1]), 'xy', 0, 0, tiled=...  26.3 us
    all_to_all x2, blocking collectives, total(): return lax.all_to_all(spread, 'xy', 0, 0, tiled=True).reshape(part.shape)  22.6 us
    pallas_call x9, Pallas kernels, call(): pl.pallas_call(body, out_shape=outs, in_specs=in_specs, out_specs=out_spe...  15.5 us
    all_to_all x1, waiting for transfers between devices, over_z(): return lax.all_to_all(x, 'z', 0, 0, tiled=True)  11.8 us
    all_to_all x1, starting transfers between devices, over_z(): return lax.all_to_all(x, 'z', 0, 0, tiled=True)  6.98 us
  transfers between devices with their start and end apart: 7, of which 5 were waited for; matrix products, arithmetic and copies ran while one was open for 1% of the time, Pallas kernels for 7%

profile of v1, /device:TPU:32, one launch (start us, length us, event | category | flops | bytes accessed | tf_op | source)
XLA Modules:
  0.0 227.0 jit_solution(4006676012782252368)
XLA Ops:
  8.9 29.2 %all_to_all.40 = bf16[16,2,16,128]{3,2,1,0:T(8,128)(2,1)S(1)} all-to-all(bf16[16,2,16,128]{3,2,1,0:T(8,128)(2,1)S(1)} %bitcast.28), channel_id=1, replica_groups=mesh['z'=16,'core'=2,'xy'=16] {'z'}, dimensions={0} | all-to-all | bytes 262144 | tf_op jit(solution)/shard_map/all_to_all | solution.py:204
  38.1 1.9 collective-permute-start
  42.1 3.2 %shard_map.84 = bf16[16,8,16,128]{3,2,1,0:T(8,128)(2,1)S(1)} custom-call(s32[256]{0:T(256)S(1)} %copy-done.3, s32[2]{0:T(128)S(1)} %pad_add_fusion.where, bf16[32,16,128]{2,1,0:T(8,128)(2,1)S(1)} %bitcast.24, bf16[32,16,128]{2,1,0:T(8,128)(2,1)S(1)} %collective-permute-done.other), custom_call_target="tpu_custom_call" | custom-call | tf_op jit(solution)/shard_map/pallas_call | solution.py:27
  45.3 37.0 %all_to_all.41.pieces = bf16[16,8,16,128]{3,2,1,0:T(8,128)(2,1)S(1)} all-to-all(bf16[16,8,16,128]{3,2,1,0:T(8,128)(2,1)S(1)} %shard_map.84), channel_id=1, replica_groups=mesh['z'=16,'core'=2,'xy'=16] {'z'}, dimensions={0} | all-to-all | bytes 1048576 | tf_op jit(solution)/shard_map/all_to_all | solution.py:204
  82.8 14.1 %all_to_all.42 = f32[16,32,128]{2,1,0:T(8,128)S(1)} all-to-all(f32[16,32,128]{2,1,0:T(8,128)S(1)} %bitcast.22), channel_id=1, replica_groups=mesh['z'=16,'core'=2,'xy'=16] {'xy'}, dimensions={0} | all-to-all | bytes 524288 | tf_op jit(solution)/shard_map/all_to_all | solution.py:208
  96.9 11.3 %all_to_all.43 = bf16[16,32,128]{2,1,0:T(8,128)(2,1)S(1)} all-to-all(bf16[16,32,128]{2,1,0:T(8,128)(2,1)S(1)} %broadcast_in_dim.4), channel_id=1, replica_groups=mesh['z'=16,'core'=2,'xy'=16] {'xy'}, dimensions={0} | all-to-all | bytes 262144 | tf_op jit(solution)/shard_map/all_to_all | solution.py:211
  108.6 1.9 collective-permute-start.2
  110.6 1.9 collective-permute-done.2.other
  112.5 2.4 %shard_map.90 = bf16[32,64,512]{2,1,0:T(8,128)(2,1)} custom-call(s32[256]{0:T(256)S(1)} %copy-done.4, s32[2]{0:T(128)S(1)} %pad_add_fusion.where, bf16[8,64,512]{2,1,0:T(8,128)(2,1)S(1)} %shard_map.89.mine, bf16[8,64,512]{2,1,0:T(8,128)(2,1)S(1)} %collective-permute-done.2.other), custom_call_target="tpu_custom_call" | custom-call | tf_op jit(solution)/shard_map/pallas_call | solution.py:27
  114.9 1.6 copy-done
  116.5 1.4 shard_map.86
  117.9 2.1 collective-permute-start.1
  120.0 1.7 collective-permute-done.1.other
  121.7 1.9 shard_map.87
  123.7 12.2 %all_to_all.44 = f32[16,32,128]{2,1,0:T(8,128)S(1)} all-to-all(f32[16,32,128]{2,1,0:T(8,128)S(1)} %bitcast.25), channel_id=1, replica_groups=mesh['z'=16,'core'=2,'xy'=16] {'xy'}, dimensions={0} | all-to-all | bytes 524288 | tf_op jit(solution)/shard_map/all_to_all | solution.py:208
  136.0 11.3 %all_to_all.45 = bf16[16,32,128]{2,1,0:T(8,128)(2,1)S(1)} all-to-all(bf16[16,32,128]{2,1,0:T(8,128)(2,1)S(1)} %broadcast_in_dim.5), channel_id=1, replica_groups=mesh['z'=16,'core'=2,'xy'=16] {'xy'}, dimensions={0} | all-to-all | bytes 262144 | tf_op jit(solution)/shard_map/all_to_all | solution.py:211
  147.7 42.1 %all_to_all.46.got = bf16[16,8,16,128]{3,2,1,0:T(8,128)(2,1)S(1)} all-to-all(bf16[16,8,16,128]{3,2,1,0:T(8,128)(2,1)S(1)} %shard_map.91), channel_id=1, replica_groups=mesh['z'=16,'core'=2,'xy'=16] {'z'}, dimensions={0} | all-to-all | bytes 1048576 | tf_op jit(solution)/shard_map/all_to_all | solution.py:204
  189.8 3.2 %shard_map.92 = (f32[32,16,128]{2,1,0:T(8,128)S(1)}, f32[32,16,128]{2,1,0:T(8,128)S(1)}) custom-call(s32[256]{0:T(256)S(1)} %copy-done.4, s32[2]{0:T(128)S(1)} %pad_add_fusion.where, bf16[16,8,16,128]{3,2,1,0:T(8,128)(2,1)S(1)} %all_to_all.46.got), custom_call_target="tpu_custom_call" | custom-call | tf_op jit(solution)/shard_map/pallas_call | solution.py:27
  193.0 1.9 collective-permute-start.3
  195.0 1.5 collective-permute-done.3
  197.1 7.0 %all-to-all-start.7 = ((bf16[16,2,16,128]{3,2,1,0:T(8,128)(2,1)}), bf16[16,2,16,128]{3,2,1,0:T(8,128)(2,1)S(1)}, u32[]{:S(2)}, u32[]{:S(2)}) async-start(bf16[16,2,16,128]{3,2,1,0:T(8,128)(2,1)} %bitcast.11), calls=%async_computation.8 | async-start | bytes 262144 | tf_op jit(solution)/shard_map/all_to_all | solution.py:204
  204.3 2.0 shard_map.88
  206.3 11.8 %all-to-all-done.7 = bf16[16,2,16,128]{3,2,1,0:T(8,128)(2,1)S(1)} async-done(((bf16[16,2,16,128]{3,2,1,0:T(8,128)(2,1)}), bf16[16,2,16,128]{3,2,1,0:T(8,128)(2,1)S(1)}, u32[]{:S(2)}, u32[]{:S(2)}) %all-to-all-start.7) | async-done | bytes 131104 | tf_op jit(solution)/shard_map/all_to_all | solution.py:204
  218.3 1.8 broadcast_divide_fusion
  (32 shorter events, 6.3 us)
Async XLA Ops:
  7.2 75.2 %copy-start.2 = (bf16[1024,512]{1,0:T(8,128)(2,1)S(1)}, bf16[1024,512]{1,0:T(8,128)(2,1)}, u32[]{:S(2)}) copy-start(bf16[1024,512]{1,0:T(8,128)(2,1)} %cot.3) | copy-start | bytes 3145732
  7.2 107.7 %all-gather.2.cloned.1.call-start = ((), (), s32[]{:S(2)}) async-start(), calls=%async_computation.9 | async-start | bytes 2228224 | tf_op jit(solution)/shard_map/all_gather | solution.py:213
  7.9 210.4 %reduce-scatter.2.cloned.1.call-start = ((), (), s32[]{:S(2)}) async-start(), calls=%async_computation.10 | async-start | bytes 2228224 | tf_op jit(solution)/shard_map/reduce_scatter | solution.py:226
  38.1 3.2 %collective-permute-start = (bf16[32,16,128]{2,1,0:T(8,128)(2,1)S(1)}, bf16[32,16,128]{2,1,0:T(8,128)(2,1)S(1)}, u32[]{:S(2)}, u32[]{:S(2)}) collective-permute-start(bf16[32,16,128]{2,1,0:T(8,128)(2,1)S(1)} %bitcast.23), channel_id=1, source_target_pairs={{0,16},{16,0},{1,17},{17,1},{2,18},{18,2},{3,19},{19,3},{4,20},{20... | collective-permute-start | bytes 393224 | tf_op jit(solution)/shard_map/ppermute | solution.py:218
  41.4 0.7 copy-start.3
  45.3 62.9 %copy-start.1 = (bf16[1024,512]{1,0:T(8,128)(2,1)S(1)}, bf16[1024,512]{1,0:T(8,128)(2,1)}, u32[]{:S(2)}) copy-start(bf16[1024,512]{1,0:T(8,128)(2,1)} %acts.3) | copy-start | bytes 3145732
  82.3 30.1 %copy-start.4 = (s32[256]{0:T(256)S(1)}, s32[256]{0:T(256)}, u32[]{:S(2)}) copy-start(s32[256]{0:T(256)} %table.9) | copy-start | bytes 3076
  108.6 3.8 %collective-permute-start.2 = (bf16[8,64,512]{2,1,0:T(8,128)(2,1)S(1)}, bf16[8,64,512]{2,1,0:T(8,128)(2,1)S(1)}, u32[]{:S(2)}, u32[]{:S(2)}) collective-permute-start(bf16[8,64,512]{2,1,0:T(8,128)(2,1)S(1)} %shard_map.89.mine), channel_id=1, source_target_pairs={{0,16},{16,0},{1,17},{17,1},{2,18},{18,2},{3,19},{19,3},{4,20},{20... | collective-permute-start | bytes 1572872 | tf_op jit(solution)/shard_map/ppermute | solution.py:224
  114.9 1.6 copy-start
  117.9 3.8 %collective-permute-start.1 = (bf16[8,64,512]{2,1,0:T(8,128)(2,1)S(1)}, bf16[8,64,512]{2,1,0:T(8,128)(2,1)S(1)}, u32[]{:S(2)}, u32[]{:S(2)}) collective-permute-start(bf16[8,64,512]{2,1,0:T(8,128)(2,1)S(1)} %shard_map.86), channel_id=1, source_target_pairs={{0,16},{16,0},{1,17},{17,1},{2,18},{18,2},{3,19},{19,3},{4,20},{20... | collective-permute-start | bytes 1572872 | tf_op jit(solution)/shard_map/ppermute | solution.py:233
  193.0 3.4 %collective-permute-start.3 = (f32[32,16,128]{2,1,0:T(8,128)S(1)}, f32[32,16,128]{2,1,0:T(8,128)S(1)}, u32[]{:S(2)}, u32[]{:S(2)}) collective-permute-start(f32[32,16,128]{2,1,0:T(8,128)S(1)} %get-tuple-element.17), channel_id=1, source_target_pairs={{0,16},{16,0},{1,17},{17,1},{2,18},{18,2},{3,19},{19,3},{4,20},{20... | collective-permute-start | bytes 786440 | tf_op jit(solution)/shard_map/ppermute | solution.py:248
  197.1 20.9 %all-to-all-start.7 = ((bf16[16,2,16,128]{3,2,1,0:T(8,128)(2,1)}), bf16[16,2,16,128]{3,2,1,0:T(8,128)(2,1)S(1)}, u32[]{:S(2)}, u32[]{:S(2)}) async-start(bf16[16,2,16,128]{3,2,1,0:T(8,128)(2,1)} %bitcast.11), calls=%async_computation.8 | async-start | bytes 262144 | tf_op jit(solution)/shard_map/all_to_all | solution.py:204
Sparse Core Ops, SparseCore 0:
  10.1 92.0 all-gather.1
  115.0 81.8 reduce-scatter.1

commit v2 on v1

v2 whole, which is shorter than its diff:
```python
import jax
import jax.numpy as jnp
from jax import lax
from jax.experimental import pallas as pl
from jax.experimental.pallas import tpu as pltpu
from jax.sharding import Mesh, PartitionSpec as P

BLOCK = 128
SCALE = 2.0
CORES = 2
HALF = 16
PIECE = (2 * HALF, 128)
F32, BF16 = jnp.float32, jnp.bfloat16

VMEM = pl.BlockSpec(memory_space=pltpu.VMEM)
SMEM = pl.BlockSpec(memory_space=pltpu.SMEM)
NT = (((1,), (1,)), ((), ()))
NN = (((1,), (0,)), ((), ()))
TN = (((0,), (0,)), ((), ()))


def dot(a, b, dims):
    return lax.dot_general(a, b, dims, preferred_element_type=F32)


def call(body, outs, ins, in_specs, scratch=()):
    return pl.pallas_call(
        body,
        out_shape=outs,
        in_specs=in_specs,
        out_specs=jax.tree.map(lambda _: VMEM, outs),
        scratch_shapes=list(scratch),
        compiler_params=pltpu.CompilerParams(vmem_limit_bytes=40 * 2**20),
    )(*ins)


def shape(dims, kind):
    return jax.ShapeDtypeStruct(dims, kind)


def named(table, z, core, block, blocks):
    adapter = table[(z * CORES + core) * blocks + block]
    owner = adapter // 2
    return owner % 2, (owner // 2) * 2 + adapter % 2


def pieces_of(matrix):
    across, along = matrix[0] // HALF, matrix[1] // PIECE[1]
    for i in range(across):
        for j in range(along):
            yield i * along + j, slice(i * HALF, (i + 1) * HALF), slice(j * PIECE[1], (j + 1) * PIECE[1])


def cut(down, up, out):
    for k in range(down.shape[0]):
        for h, r, c in pieces_of(down.shape[1:]):
            out[h, k, :HALF] = down[k, r, c]
            out[h, k, HALF:] = up[k, r, c]


def means(counts, owned, down, up):
    for k in range(down.shape[0]):
        for h, r, c in pieces_of(down.shape[1:]):
            mean = owned[h, k].astype(F32) / counts[k]
            down[k, r, c] = mean[:HALF]
            up[k, r, c] = mean[HALF:]


def pick_pieces(table, where, mine, other, out, held):
    nz, blocks = out.shape[0], out.shape[1]
    half = mine.shape[0]
    core = where[1]
    held[:half] = mine[...]
    held[half:] = other[...]

    def step(z, _):
        for b in range(blocks):
            par, row = named(table, z, core, b, blocks)
            out[z, b] = held[jnp.where(par == core, row, row + half)]
        return 0

    lax.fori_loop(0, nz, step, 0, unroll=2)


def assemble(pieces, b, which, per_row):
    rows = []
    for i in range(pieces.shape[0] // per_row):
        parts = [pieces[i * per_row + j, b, which * HALF:(which + 1) * HALF] for j in range(per_row)]
        rows.append(jnp.concatenate(parts, axis=1))
    return jnp.concatenate(rows, axis=0)


def low(w):
    return jnp.concatenate([w, jnp.zeros_like(w)], axis=0)


def high(w):
    return jnp.concatenate([jnp.zeros_like(w), w], axis=0)


def rows_of(ref, b):
    return ref[b * BLOCK:(b + 1) * BLOCK, :]


def partial_sums(acts, cot, pieces, out):
    per_row = acts.shape[1] // PIECE[1]
    for b in range(pieces.shape[1]):
        proj = dot(rows_of(acts, b), low(assemble(pieces, b, 0, per_row)), NT)
        back = dot(rows_of(cot, b), high(assemble(pieces, b, 1, per_row)), NT)
        out[b * BLOCK:(b + 1) * BLOCK, :] = proj + SCALE * back


def block_grads(acts, cot, sums, out):
    rank = sums.shape[1] // 2
    for b in range(out.shape[1]):
        p = rows_of(sums, b)
        down = dot(p, rows_of(acts, b), TN)[rank:].astype(BF16)
        up = (SCALE * dot(p, rows_of(cot, b), TN)[:rank]).astype(BF16)
        for which, g in enumerate((down, up)):
            for h, r, c in pieces_of(g.shape):
                out[h, b, which * HALF:(which + 1) * HALF] = g[r, c]


def sum_pieces(table, where, got, keep, send, acc):
    nz, blocks = got.shape[0], got.shape[1]
    core = where[1]
    half = keep.shape[0]
    acc[...] = jnp.zeros_like(acc)

    def step(z, _):
        for b in range(blocks):
            par, row = named(table, z, core, b, blocks)
            at = par * half + row
            acc[at] = acc[at] + got[z, b].astype(F32)
        return 0

    lax.fori_loop(0, nz, step, 0, unroll=2)
    keep[...] = acc[pl.ds(core * half, half)]
    send[...] = acc[pl.ds((1 - core) * half, half)]


def outputs(sums, pieces, out, grad):
    per_row = out.shape[1] // PIECE[1]
    for b in range(pieces.shape[1]):
        p = rows_of(sums, b)
        at = slice(b * BLOCK, (b + 1) * BLOCK)
        out[at, :] = (SCALE * dot(p, low(assemble(pieces, b, 1, per_row)), NN)).astype(BF16)
        grad[at, :] = dot(p, high(assemble(pieces, b, 0, per_row)), NN).astype(BF16)


def local(activations, cotangent, adapter_down_weights, adapter_up_weights, table):
    nz, nxy = lax.axis_size("z"), lax.axis_size("xy")
    share, width, rank = adapter_down_weights.shape
    tokens = activations.shape[0]
    blocks = tokens // BLOCK
    where = jnp.stack([lax.axis_index("z"), lax.axis_index("core")]).astype(jnp.int32)
    swap = [(0, 1), (1, 0)]
    own = nz * share

    def over_z(x):
        return lax.all_to_all(x, "z", 0, 0, tiled=True)

    def total(part):
        rows = part.shape[0] // nxy
        got = lax.all_to_all(part.reshape(nxy, rows, part.shape[1]), "xy", 0, 0, tiled=True)
        mine = jnp.sum(got, axis=0).astype(BF16)
        spread = jnp.broadcast_to(mine[None], (nxy,) + mine.shape)
        return lax.all_to_all(spread, "xy", 0, 0, tiled=True).reshape(part.shape)

    down = jnp.swapaxes(adapter_down_weights, 1, 2)
    pieces = call(cut, shape((nz, share) + PIECE, BF16), (down, adapter_up_weights), [VMEM] * 2)
    held = over_z(pieces).reshape(own, *PIECE)
    held_other = lax.ppermute(held, "core", swap)
    wanted = call(
        pick_pieces, shape((nz, blocks) + PIECE, BF16), (table, where, held, held_other), [SMEM, SMEM, VMEM, VMEM],
        [pltpu.VMEM((CORES * own,) + PIECE, BF16)],
    )
    pieces = over_z(wanted)
    sums = total(
        call(partial_sums, shape((tokens, 2 * rank), F32), (activations, cotangent, pieces), [VMEM] * 3)
    )
    parts = call(
        block_grads, shape((nz, blocks) + PIECE, BF16), (activations, cotangent, sums), [VMEM] * 3
    )
    got = over_z(parts)
    keep, send = call(
        sum_pieces, (shape((own,) + PIECE, F32),) * 2, (table, where, got), [SMEM, SMEM, VMEM],
        [pltpu.VMEM((CORES * own,) + PIECE, F32)],
    )
    merged = (keep + lax.ppermute(send, "core", swap)).astype(BF16)
    owned = over_z(merged.reshape(nz, share, *PIECE))

    out, grad = call(outputs, (shape((tokens, width), BF16),) * 2, (sums, pieces), [VMEM] * 2)

    ids = (where[0] * CORES + where[1]) * share + jnp.arange(share, dtype=jnp.int32)
    counts = jnp.sum((table[:, None] == ids[None, :]).astype(F32), axis=0) * BLOCK
    down_grad, up_grad = call(means, (shape((share, rank, width), F32),) * 2, (counts, owned), [SMEM, VMEM])
    return out, grad, jnp.swapaxes(down_grad, 1, 2), up_grad


def solution(mesh):
    nxy = mesh.shape["adapter"]
    grid = Mesh(mesh.devices.reshape(-1, CORES, nxy), ("z", "core", "xy"))
    dp = ("z", "core")
    specs = (P(dp, "xy"), P(dp, "xy"), P(dp, "xy", None), P(dp, None, "xy"))
    return jax.shard_map(
        local, mesh=grid, in_specs=specs + (P(),), out_specs=specs, check_vma=False
    )
```

time: 228 us -> 221 us (0.969)
  blocking collectives: 157 us -> 175 us
  between operations: 14.2 us -> 0.74 us
  Pallas kernels: 15.5 us -> 9.35 us
  starting transfers between devices: 14.9 us -> 11.5 us
    all_to_all x3, blocking collectives: 108 us -> 146 us  [over_z(): return lax.all_to_all(x, 'z', 0, 0, tiled=True)]
    all_to_all x2 -> x1, blocking collectives: 22.6 us -> 11.7 us  [total(): return lax.all_to_all(spread, 'xy', 0, 0, tiled=True).reshape(part.shape)]
    all_to_all x2 -> x1, blocking collectives: 26.3 us -> 17 us  [total(): lax.all_to_all(part.reshape(nxy, rows, part.shape[1]), 'xy', 0, 0, tiled=...]
    pallas_call x9 -> x7, Pallas kernels: 15.5 us -> 9.35 us  [call(): pl.pallas_call(body, out_shape=outs, in_specs=in_specs, out_specs=jax.tre...]
    all_to_all x1, waiting for transfers between devices: 11.8 us -> 16.2 us  [over_z(): return lax.all_to_all(x, 'z', 0, 0, tiled=True)]
    ppermute x2 -> x0, starting transfers between devices: 3.98 us -> none  [the longest x1 2.06 us: local(): from_other = lax.ppermute(for_other, 'core', swap)]
    ppermute x2 -> x0, waiting for transfers between devices: 3.61 us -> none  [the longest x1 1.88 us: local(): part_other = lax.ppermute(part_down, 'core', swap)]
  transfers between devices with their start and end apart: 7 -> 3, of which waited for: 5 -> 3; matrix products, arithmetic and copies ran while one was open for 1% -> 0% of each run, Pallas kernels for 7% -> 1%
where the time goes in v2:
time: 221 us; the launch traced here: 220 us
  blocking collectives  175 us (79%)
  waiting for transfers between devices  19.5 us (9%)
  starting transfers between devices  11.5 us (5%)
  Pallas kernels  9.35 us (4%)
    all_to_all x3, blocking collectives, over_z(): return lax.all_to_all(x, 'z', 0, 0, tiled=True)  146 us
    all_to_all x1, blocking collectives, total(): lax.all_to_all(part.reshape(nxy, rows, part.shape[1]), 'xy', 0, 0, tiled=...  17 us
    all_to_all x1, waiting for transfers between devices, over_z(): return lax.all_to_all(x, 'z', 0, 0, tiled=True)  16.2 us
    all_to_all x1, blocking collectives, total(): return lax.all_to_all(spread, 'xy', 0, 0, tiled=True).reshape(part.shape)  11.7 us
    pallas_call x7, Pallas kernels, call(): pl.pallas_call(body, out_shape=outs, in_specs=in_specs, out_specs=jax.tre...  9.35 us
    all_to_all x1, starting transfers between devices, over_z(): return lax.all_to_all(x, 'z', 0, 0, tiled=True)  7.71 us
  transfers between devices with their start and end apart: 3, of which 3 were waited for; matrix products, arithmetic and copies ran while one was open for 0% of the time, Pallas kernels for 1%

profile of v2, /device:TPU:32, one launch (start us, length us, event | category | flops | bytes accessed | tf_op | source)
XLA Modules:
  0.0 220.2 jit_solution(14409440851943025426)
XLA Ops:
  0.6 0.9 copy-done.2
  1.5 0.9 copy-done.3
  2.5 32.9 %all_to_all.30 = bf16[16,2,32,128]{3,2,1,0:T(8,128)(2,1)S(1)} all-to-all(bf16[16,2,32,128]{3,2,1,0:T(8,128)(2,1)S(1)} %shard_map.84), channel_id=1, replica_groups=mesh['z'=16,'core'=2,'xy'=16] {'z'}, dimensions={0} | all-to-all | bytes 524288 | tf_op jit(solution)/shard_map/all_to_all | solution.py:161
  35.4 1.9 collective-permute-start
  37.3 0.0 copy-start.4
  37.3 0.1 pad_add_fusion.where
  37.4 1.4 collective-permute-done.other
  38.8 2.2 %shard_map.85 = bf16[16,8,32,128]{3,2,1,0:T(8,128)(2,1)S(1)} custom-call(s32[256]{0:T(256)S(1)} %copy-done.4, s32[2]{0:T(128)S(1)} %pad_add_fusion.where, bf16[32,32,128]{2,1,0:T(8,128)(2,1)S(1)} %bitcast.12, bf16[32,32,128]{2,1,0:T(8,128)(2,1)S(1)} %collective-permute-done.other), custom_call_target="tpu_custom_call" | custom-call | tf_op jit(solution)/shard_map/pallas_call | solution.py:27
  41.1 57.6 %all_to_all.31.pieces = bf16[16,8,32,128]{3,2,1,0:T(8,128)(2,1)S(1)} all-to-all(bf16[16,8,32,128]{3,2,1,0:T(8,128)(2,1)S(1)} %shard_map.85), channel_id=1, replica_groups=mesh['z'=16,'core'=2,'xy'=16] {'z'}, dimensions={0} | all-to-all | bytes 2097152 | tf_op jit(solution)/shard_map/all_to_all | solution.py:161
  98.7 0.7 shard_map.86
  99.4 17.0 %all_to_all.32 = f32[16,64,128]{2,1,0:T(8,128)} all-to-all(f32[16,64,128]{2,1,0:T(8,128)S(1)} %bitcast.10), channel_id=1, replica_groups=mesh['z'=16,'core'=2,'xy'=16] {'xy'}, dimensions={0} | all-to-all | bytes 1048576 | tf_op jit(solution)/shard_map/all_to_all | solution.py:165
  116.5 1.1 reduce_sum.18
  117.6 11.7 %all_to_all.33 = bf16[16,64,128]{2,1,0:T(8,128)(2,1)S(1)} all-to-all(bf16[16,64,128]{2,1,0:T(8,128)(2,1)S(1)} %broadcast_in_dim.2), channel_id=1, replica_groups=mesh['z'=16,'core'=2,'xy'=16] {'xy'}, dimensions={0} | all-to-all | bytes 524288 | tf_op jit(solution)/shard_map/all_to_all | solution.py:168
  129.3 0.7 shard_map.88
  130.0 55.9 %all_to_all.34.got = bf16[16,8,32,128]{3,2,1,0:T(8,128)(2,1)S(1)} all-to-all(bf16[16,8,32,128]{3,2,1,0:T(8,128)(2,1)S(1)} %shard_map.88), channel_id=1, replica_groups=mesh['z'=16,'core'=2,'xy'=16] {'z'}, dimensions={0} | all-to-all | bytes 2097152 | tf_op jit(solution)/shard_map/all_to_all | solution.py:161
  185.9 2.3 %shard_map.89 = (f32[32,32,128]{2,1,0:T(8,128)S(1)}, f32[32,32,128]{2,1,0:T(8,128)S(1)}) custom-call(s32[256]{0:T(256)S(1)} %copy-done.4, s32[2]{0:T(128)S(1)} %pad_add_fusion.where, bf16[16,8,32,128]{3,2,1,0:T(8,128)(2,1)S(1)} %all_to_all.34.got), custom_call_target="tpu_custom_call" | custom-call | tf_op jit(solution)/shard_map/pallas_call | solution.py:27
  188.2 1.9 collective-permute-start.1
  190.1 1.9 collective-permute-done.1
  192.0 0.8 add_convert_fusion
  192.8 7.7 %all-to-all-start.5 = ((bf16[16,2,32,128]{3,2,1,0:T(8,128)(2,1)}), bf16[16,2,32,128]{3,2,1,0:T(8,128)(2,1)S(1)}, u32[]{:S(2)}, u32[]{:S(2)}) async-start(bf16[16,2,32,128]{3,2,1,0:T(8,128)(2,1)} %bitcast.6), calls=%async_computation.5 | async-start | bytes 524288 | tf_op jit(solution)/shard_map/all_to_all | solution.py:161
  200.5 0.2 fusion
  200.7 2.0 shard_map.87
  202.7 16.2 %all-to-all-done.5.owned = bf16[16,2,32,128]{3,2,1,0:T(8,128)(2,1)S(1)} async-done(((bf16[16,2,32,128]{3,2,1,0:T(8,128)(2,1)}), bf16[16,2,32,128]{3,2,1,0:T(8,128)(2,1)S(1)}, u32[]{:S(2)}, u32[]{:S(2)}) %all-to-all-start.5) | async-done | bytes 262176 | tf_op jit(solution)/shard_map/all_to_all | solution.py:161
  218.9 1.4 shard_map.90
  (11 shorter events, 0.1 us)
Async XLA Ops:
  0.6 0.9 copy-start.2
  1.5 0.9 copy-start.3
  35.4 3.4 %collective-permute-start = (bf16[32,32,128]{2,1,0:T(8,128)(2,1)S(1)}, bf16[32,32,128]{2,1,0:T(8,128)(2,1)S(1)}, u32[]{:S(2)}, u32[]{:S(2)}) collective-permute-start(bf16[32,32,128]{2,1,0:T(8,128)(2,1)S(1)} %bitcast.11), channel_id=1, source_target_pairs={{0,16},{16,0},{1,17},{17,1},{2,18},{18,2},{3,19},{19,3},{4,20},{20... | collective-permute-start | bytes 786440 | tf_op jit(solution)/shard_map/ppermute | solution.py:173
  37.3 1.5 copy-start.4
  41.1 57.7 %copy-start = (bf16[1024,512]{1,0:T(8,128)(2,1)S(1)}, bf16[1024,512]{1,0:T(8,128)(2,1)}, u32[]{:S(2)}) copy-start(bf16[1024,512]{1,0:T(8,128)(2,1)} %acts.3) | copy-start | bytes 3145732
  41.1 57.6 %copy-start.1 = (bf16[1024,512]{1,0:T(8,128)(2,1)S(1)}, bf16[1024,512]{1,0:T(8,128)(2,1)}, u32[]{:S(2)}) copy-start(bf16[1024,512]{1,0:T(8,128)(2,1)} %cot.3) | copy-start | bytes 3145732
  188.2 3.8 %collective-permute-start.1 = (f32[32,32,128]{2,1,0:T(8,128)S(1)}, f32[32,32,128]{2,1,0:T(8,128)S(1)}, u32[]{:S(2)}, u32[]{:S(2)}) collective-permute-start(f32[32,32,128]{2,1,0:T(8,128)S(1)} %get-tuple-element.13), channel_id=1, source_target_pairs={{0,16},{16,0},{1,17},{17,1},{2,18},{18,2},{3,19},{19,3},{4,20},{20... | collective-permute-start | bytes 1572872 | tf_op jit(solution)/shard_map/ppermute | solution.py:190
  192.8 26.1 %all-to-all-start.5 = ((bf16[16,2,32,128]{3,2,1,0:T(8,128)(2,1)}), bf16[16,2,32,128]{3,2,1,0:T(8,128)(2,1)S(1)}, u32[]{:S(2)}, u32[]{:S(2)}) async-start(bf16[16,2,32,128]{3,2,1,0:T(8,128)(2,1)} %bitcast.6), calls=%async_computation.5 | async-start | bytes 524288 | tf_op jit(solution)/shard_map/all_to_all | solution.py:161

commit v3 on v2

v3 whole, which is shorter than its diff:
```python
import functools

import jax
import jax.numpy as jnp
from jax import lax
from jax.experimental import pallas as pl
from jax.experimental.pallas import tpu as pltpu
from jax.sharding import Mesh, PartitionSpec as P

BLOCK = 128
SCALE = 2.0
CORES = 2
COPIES = 2
GROUP = 8
STEPS = (0, 4, 1, -1, 2, -2, 3, -3)
F32, BF16 = jnp.float32, jnp.bfloat16

VMEM = pl.BlockSpec(memory_space=pltpu.VMEM)
SMEM = pl.BlockSpec(memory_space=pltpu.SMEM)
NT = (((1,), (1,)), ((), ()))
NN = (((1,), (0,)), ((), ()))
TN = (((0,), (0,)), ((), ()))


def dot(a, b, dims):
    return lax.dot_general(a, b, dims, preferred_element_type=F32)


def call(body, outs, ins, in_specs, scratch=()):
    return pl.pallas_call(
        body,
        out_shape=outs,
        in_specs=in_specs,
        out_specs=jax.tree.map(lambda _: VMEM, outs),
        scratch_shapes=list(scratch),
        compiler_params=pltpu.CompilerParams(vmem_limit_bytes=40 * 2**20),
    )(*ins)


def shape(dims, kind):
    return jax.ShapeDtypeStruct(dims, kind)


def named(table, z, core, block, blocks):
    adapter = table[(z * CORES + core) * blocks + block]
    owner = adapter // 2
    return owner % 2, (owner // 2) * 2 + adapter % 2


def cut(down, up, out):
    parts = out.shape[0] // COPIES
    for k in range(down.shape[0]):
        d, u = down[k].astype(F32), up[k].astype(F32)
        for i in range(parts):
            at = slice(i * GROUP, (i + 1) * GROUP)
            piece = jnp.concatenate([d[at], u[at]], axis=0).astype(BF16)
            for copy in range(COPIES):
                out[copy * parts + i, k] = piece


def means(counts, owned, down, up):
    parts = owned.shape[0] // COPIES
    for k in range(down.shape[0]):
        for i in range(parts):
            piece = owned[i, k].astype(F32)
            for copy in range(1, COPIES):
                piece = piece + owned[copy * parts + i, k].astype(F32)
            piece = piece / counts[k]
            down[k, i * GROUP:(i + 1) * GROUP] = piece[:GROUP]
            up[k, i * GROUP:(i + 1) * GROUP] = piece[GROUP:]


def partner(where, nz, step):
    return lax.rem(where[0] + (1 - 2 * where[1]) * step + nz, nz)


def pick_pieces(nz, table, where, mine, other, *outs):
    core = where[1]
    blocks = outs[0].shape[0]
    for step, out in zip(STEPS, outs):
        z = partner(where, nz, step)
        for b in range(blocks):
            par, row = named(table, z, core, b, blocks)

            @pl.when(par == core)
            def _():
                out[b] = mine[row]

            @pl.when(par != core)
            def _():
                out[b] = other[row]


def is_first(dims, axis):
    return lax.broadcasted_iota(jnp.int32, dims, axis) % (2 * GROUP) < GROUP


def rows_of(ref, b):
    return ref[b * BLOCK:(b + 1) * BLOCK, :]


def matrix(pieces, b):
    return jnp.concatenate([p[b] for p in pieces], axis=0)


def partial_sums(acts, cot, *refs):
    pieces, out = refs[:-1], refs[-1]
    lanes = out.shape[1]
    first = is_first((BLOCK, lanes), 1)
    for b in range(pieces[0].shape[0]):
        w = matrix(pieces, b)
        proj, back = dot(rows_of(acts, b), w, NT), dot(rows_of(cot, b), w, NT)
        out[b * BLOCK:(b + 1) * BLOCK, :] = jnp.where(first, proj, SCALE * back)


def swapped(sums, b):
    lanes = sums.shape[1]
    row = lax.broadcasted_iota(jnp.int32, (lanes, lanes), 0)
    col = lax.broadcasted_iota(jnp.int32, (lanes, lanes), 1)
    place = row == jnp.where(is_first((lanes, lanes), 1), col + GROUP, col - GROUP)
    return dot(rows_of(sums, b), place.astype(BF16), NN).astype(BF16)


def block_grads(acts, cot, sums, *outs):
    lanes = sums.shape[1]
    first = is_first((lanes, acts.shape[1]), 0)
    for b in range(outs[0].shape[0]):
        q = swapped(sums, b)
        down, up = dot(q, rows_of(acts, b), TN), dot(q, rows_of(cot, b), TN)
        g = jnp.where(first, down, SCALE * up).astype(BF16)
        for i, out in enumerate(outs):
            out[b] = g[i * 2 * GROUP:(i + 1) * 2 * GROUP]


def outputs(sums, *refs):
    pieces, out, grad = refs[:-2], refs[-2], refs[-1]
    first = is_first((BLOCK, sums.shape[1]), 1)
    for b in range(pieces[0].shape[0]):
        q, w = swapped(sums, b), matrix(pieces, b)
        zero = jnp.zeros_like(q)
        at = slice(b * BLOCK, (b + 1) * BLOCK)
        out[at, :] = (SCALE * dot(jnp.where(first, zero, q), w, NN)).astype(BF16)
        grad[at, :] = dot(jnp.where(first, q, zero), w, NN).astype(BF16)


def sum_pieces(nz, table, where, *refs):
    gots, (keep, send, acc) = refs[:-3], refs[-3:]
    core = where[1]
    half = keep.shape[0]
    blocks = gots[0].shape[0]
    acc[...] = jnp.zeros_like(acc)
    for step, got in zip(STEPS, gots):
        z = partner(where, nz, step)
        for b in range(blocks):
            par, row = named(table, z, core, b, blocks)
            at = par * half + row
            acc[at] = acc[at] + got[b].astype(F32)
    keep[...] = acc[pl.ds(core * half, half)]
    send[...] = acc[pl.ds((1 - core) * half, half)].astype(BF16)


def local(activations, cotangent, adapter_down_weights, adapter_up_weights, table):
    nz, nxy = lax.axis_size("z"), lax.axis_size("xy")
    share, width, rank = adapter_down_weights.shape
    tokens = activations.shape[0]
    blocks = tokens // BLOCK
    piece = (2 * GROUP, width)
    where = jnp.stack([lax.axis_index("z"), lax.axis_index("core")]).astype(jnp.int32)
    swap = [(0, 1), (1, 0)]
    own = nz * share
    slots = (shape((blocks,) + piece, BF16),) * len(STEPS)

    def over_z(x):
        return lax.all_to_all(x, "z", 0, 0, tiled=True)

    def shift(x, step):
        if step == 0:
            return x
        pairs = [(z * CORES + c, (z + (step, -step)[c]) % nz * CORES + c) for z in range(nz) for c in range(CORES)]
        return lax.ppermute(x, ("z", "core"), pairs)

    def total(part):
        rows = part.shape[0] // nxy
        got = lax.all_to_all(part.reshape(nxy, rows, part.shape[1]), "xy", 0, 0, tiled=True)
        mine = jnp.sum(got, axis=0).astype(BF16)
        spread = jnp.broadcast_to(mine[None], (nxy,) + mine.shape)
        return lax.all_to_all(spread, "xy", 0, 0, tiled=True).reshape(part.shape)

    down = jnp.swapaxes(adapter_down_weights, 1, 2)
    spread = call(cut, shape((nz, share) + piece, BF16), (down, adapter_up_weights), [VMEM] * 2)
    held = over_z(spread).reshape(own, *piece)
    held_other = lax.ppermute(held, "core", swap)
    wanted = call(
        functools.partial(pick_pieces, nz), slots, (table, where, held, held_other), [SMEM, SMEM, VMEM, VMEM]
    )
    pieces = [shift(w, step) for w, step in zip(wanted, STEPS)]
    sums = total(
        call(
            partial_sums, shape((tokens, 2 * rank), F32), (activations, cotangent, *pieces), [VMEM] * (2 + len(STEPS))
        )
    )
    parts = call(block_grads, slots, (activations, cotangent, sums), [VMEM] * 3)
    gots = [shift(g, -step) for g, step in zip(parts, STEPS)]
    keep, send = call(
        functools.partial(sum_pieces, nz), (shape((own,) + piece, F32), shape((own,) + piece, BF16)),
        (table, where, *gots), [SMEM, SMEM] + [VMEM] * len(STEPS), [pltpu.VMEM((CORES * own,) + piece, F32)],
    )
    merged = (keep + lax.ppermute(send, "core", swap).astype(F32)).astype(BF16)
    owned = over_z(merged.reshape(nz, share, *piece))

    out, grad = call(outputs, (shape((tokens, width), BF16),) * 2, (sums, *pieces), [VMEM] * (1 + len(STEPS)))

    ids = (where[0] * CORES + where[1]) * share + jnp.arange(share, dtype=jnp.int32)
    counts = jnp.sum((table[:, None] == ids[None, :]).astype(F32), axis=0) * BLOCK
    down_grad, up_grad = call(means, (shape((share, rank, width), F32),) * 2, (counts, owned), [SMEM, VMEM])
    return out, grad, jnp.swapaxes(down_grad, 1, 2), up_grad


def solution(mesh):
    nxy = mesh.shape["adapter"]
    grid = Mesh(mesh.devices.reshape(-1, CORES, nxy), ("z", "core", "xy"))
    dp = ("z", "core")
    specs = (P(dp, "xy"), P(dp, "xy"), P(dp, "xy", None), P(dp, None, "xy"))
    return jax.shard_map(
        local, mesh=grid, in_specs=specs + (P(),), out_specs=specs, check_vma=False
    )
```

time: 221 us -> 202 us (0.914)
  blocking collectives: 175 us -> 73.5 us
  starting transfers between devices: 11.5 us -> 65.6 us
  waiting for transfers between devices: 19.5 us -> 45.8 us
    all_to_all x3 -> x1, blocking collectives: 146 us -> 43.4 us  [over_z(): return lax.all_to_all(x, 'z', 0, 0, tiled=True)]
    ppermute x1 -> x15, starting transfers between devices: 1.92 us -> 56.4 us  [the longest x14 54.5 us: shift(): return lax.ppermute(x, ('z', 'core'), pairs)]
    ppermute x1 -> x15, waiting for transfers between devices: 1.88 us -> 17.9 us  [the longest x14 16 us: shift(): return lax.ppermute(x, ('z', 'core'), pairs)]
    all_to_all x1, waiting for transfers between devices: 16.2 us -> 26.1 us  [over_z(): return lax.all_to_all(x, 'z', 0, 0, tiled=True)]
  transfers between devices with their start and end apart: 3 -> 17, of which waited for: 3 -> 8; matrix products, arithmetic and copies ran while one was open for 0% -> 0% of each run, Pallas kernels for 1% -> 2%
where the time goes in v3:
time: 202 us; the launch traced here: 201 us
  blocking collectives  73.5 us (36%)
  starting transfers between devices  65.6 us (32%)
  waiting for transfers between devices  45.8 us (23%)
  Pallas kernels  11.2 us (6%)
  other arithmetic  2.33 us (1%)
    ppermute x14, starting transfers between devices, shift(): return lax.ppermute(x, ('z', 'core'), pairs)  54.5 us
    all_to_all x1, blocking collectives, over_z(): return lax.all_to_all(x, 'z', 0, 0, tiled=True)  43.4 us
    all_to_all x1, waiting for transfers between devices, over_z(): return lax.all_to_all(x, 'z', 0, 0, tiled=True)  26.1 us
    all_to_all x1, blocking collectives, total(): lax.all_to_all(part.reshape(nxy, rows, part.shape[1]), 'xy', 0, 0, tiled=...  18.4 us
    ppermute x14, waiting for transfers between devices, shift(): return lax.ppermute(x, ('z', 'core'), pairs)  16 us
    all_to_all x1, blocking collectives, total(): return lax.all_to_all(spread, 'xy', 0, 0, tiled=True).reshape(part.shape)  11.8 us
    pallas_call x7, Pallas kernels, call(): pl.pallas_call(body, out_shape=outs, in_specs=in_specs, out_specs=jax.tre...  11.2 us
    all_to_all x1, starting transfers between devices, over_z(): return lax.all_to_all(x, 'z', 0, 0, tiled=True)  7.23 us
  transfers between devices with their start and end apart: 17, of which 8 were waited for; matrix products, arithmetic and copies ran while one was open for 0% of the time, Pallas kernels for 2%

profile of v3, /device:TPU:32, one launch (start us, length us, event | category | flops | bytes accessed | tf_op | source)
XLA Modules:
  0.0 201.2 jit_solution(3787481040163606005)
XLA Ops:
  2.5 43.4 %all_to_all.20 = bf16[16,2,16,512]{3,2,1,0:T(8,128)(2,1)S(1)} all-to-all(bf16[16,2,16,512]{3,2,1,0:T(8,128)(2,1)S(1)} %shard_map.84), channel_id=1, replica_groups=mesh['z'=16,'core'=2,'xy'=16] {'z'}, dimensions={0} | all-to-all | bytes 1048576 | tf_op jit(solution)/shard_map/all_to_all | solution.py:174
  49.7 2.2 %shard_map.85 = (bf16[8,16,512]{2,1,0:T(8,128)(2,1)S(1)}, bf16[8,16,512]{2,1,0:T(8,128)(2,1)S(1)}, bf16[8,16,512]{2,1,0:T(8,128)(2,1)S(1)}, bf16[8,16,512]{2,1,0...) custom-call(s32[256]{0:T(256)S(1)} %copy-done.4, ...), custom_call_target="tpu_custom_call" | custom-call | tf_op jit(solution)/shard_map/pallas_call | solution.py:30
  51.9 6.0 %collective-permute-start.1 = (bf16[8,16,512]{2,1,0:T(8,128)(2,1)S(1)}, bf16[8,16,512]{2,1,0:T(8,128)(2,1)S(1)}, u32[]{:S(2)}, u32[]{:S(2)}) collective-permute-start(bf16[8,16,512]{2,1,0:T(8,128)(2,1)S(1)} %get-tuple-element.27), channel_id=1, source_target_pairs={{0,128},{16,400},{32,160},{48,432},{64,192},{80,464},{96,224},{112... | collective-permute-start | bytes 393224 | tf_op jit(solution)/shard_map/ppermute | solution.py:180
  57.9 2.4 %collective-permute-start.2 = (bf16[8,16,512]{2,1,0:T(8,128)(2,1)S(1)}, bf16[8,16,512]{2,1,0:T(8,128)(2,1)S(1)}, u32[]{:S(2)}, u32[]{:S(2)}) collective-permute-start(bf16[8,16,512]{2,1,0:T(8,128)(2,1)S(1)} %get-tuple-element.28), channel_id=1, source_target_pairs={{0,32},{16,496},{32,64},{48,16},{64,96},{80,48},{96,128},{112,80},... | collective-permute-start | bytes 393224 | tf_op jit(solution)/shard_map/ppermute | solution.py:180
  60.3 3.5 %collective-permute-start.3 = (bf16[8,16,512]{2,1,0:T(8,128)(2,1)S(1)}, bf16[8,16,512]{2,1,0:T(8,128)(2,1)S(1)}, u32[]{:S(2)}, u32[]{:S(2)}) collective-permute-start(bf16[8,16,512]{2,1,0:T(8,128)(2,1)S(1)} %get-tuple-element.29), channel_id=1, source_target_pairs={{0,480},{16,48},{32,0},{48,80},{64,32},{80,112},{96,64},{112,144},... | collective-permute-start | bytes 393224 | tf_op jit(solution)/shard_map/ppermute | solution.py:180
  63.7 2.8 %collective-permute-start.4 = (bf16[8,16,512]{2,1,0:T(8,128)(2,1)S(1)}, bf16[8,16,512]{2,1,0:T(8,128)(2,1)S(1)}, u32[]{:S(2)}, u32[]{:S(2)}) collective-permute-start(bf16[8,16,512]{2,1,0:T(8,128)(2,1)S(1)} %get-tuple-element.30), channel_id=1, source_target_pairs={{0,64},{16,464},{32,96},{48,496},{64,128},{80,16},{96,160},{112,48... | collective-permute-start | bytes 393224 | tf_op jit(solution)/shard_map/ppermute | solution.py:180
  66.6 5.1 %collective-permute-start.5 = (bf16[8,16,512]{2,1,0:T(8,128)(2,1)S(1)}, bf16[8,16,512]{2,1,0:T(8,128)(2,1)S(1)}, u32[]{:S(2)}, u32[]{:S(2)}) collective-permute-start(bf16[8,16,512]{2,1,0:T(8,128)(2,1)S(1)} %get-tuple-element.31), channel_id=1, source_target_pairs={{0,448},{16,80},{32,480},{48,112},{64,0},{80,144},{96,32},{112,176... | collective-permute-start | bytes 393224 | tf_op jit(solution)/shard_map/ppermute | solution.py:180
  71.7 4.0 %collective-permute-start.6 = (bf16[8,16,512]{2,1,0:T(8,128)(2,1)S(1)}, bf16[8,16,512]{2,1,0:T(8,128)(2,1)S(1)}, u32[]{:S(2)}, u32[]{:S(2)}) collective-permute-start(bf16[8,16,512]{2,1,0:T(8,128)(2,1)S(1)} %get-tuple-element.32), channel_id=1, source_target_pairs={{0,96},{16,432},{32,128},{48,464},{64,160},{80,496},{96,192},{112,... | collective-permute-start | bytes 393224 | tf_op jit(solution)/shard_map/ppermute | solution.py:180
  75.8 4.8 %collective-permute-start.7 = (bf16[8,16,512]{2,1,0:T(8,128)(2,1)S(1)}, bf16[8,16,512]{2,1,0:T(8,128)(2,1)S(1)}, u32[]{:S(2)}, u32[]{:S(2)}) collective-permute-start(bf16[8,16,512]{2,1,0:T(8,128)(2,1)S(1)} %get-tuple-element.33), channel_id=1, source_target_pairs={{0,416},{16,112},{32,448},{48,144},{64,480},{80,176},{96,0},{112,2... | collective-permute-start | bytes 393224 | tf_op jit(solution)/shard_map/ppermute | solution.py:180
  80.6 6.2 %collective-permute-done.6.refs_6_ = bf16[8,16,512]{2,1,0:T(8,128)(2,1)S(1)} collective-permute-done((bf16[8,16,512]{2,1,0:T(8,128)(2,1)S(1)}, bf16[8,16,512]{2,1,0:T(8,128)(2,1)S(1)}, u32[]{:S(2)}, u32[]{:S(2)}) %collective-permute-start.6) | collective-permute-done | bytes 131104 | tf_op jit(solution)/shard_map/ppermute | solution.py:180
  89.3 18.4 %all_to_all.21 = f32[16,64,128]{2,1,0:T(8,128)} all-to-all(f32[16,64,128]{2,1,0:T(8,128)S(1)} %bitcast.10), channel_id=1, replica_groups=mesh['z'=16,'core'=2,'xy'=16] {'xy'}, dimensions={0} | all-to-all | bytes 1048576 | tf_op jit(solution)/shard_map/all_to_all | solution.py:184
  108.8 11.8 %all_to_all.22 = bf16[16,64,128]{2,1,0:T(8,128)(2,1)S(1)} all-to-all(bf16[16,64,128]{2,1,0:T(8,128)(2,1)S(1)} %broadcast_in_dim.2), channel_id=1, replica_groups=mesh['z'=16,'core'=2,'xy'=16] {'xy'}, dimensions={0} | all-to-all | bytes 524288 | tf_op jit(solution)/shard_map/all_to_all | solution.py:187
  120.6 2.2 %shard_map.88 = (bf16[8,16,512]{2,1,0:T(8,128)(2,1)S(1)}, bf16[8,16,512]{2,1,0:T(8,128)(2,1)S(1)}, bf16[8,16,512]{2,1,0:T(8,128)(2,1)S(1)}, bf16[8,16,512]{2,1,0...) custom-call(bf16[1024,512]{1,0:T(8,128)(2,1)S(1)} %copy-done, ...), custom_call_target="tpu_custom_call" | custom-call | tf_op jit(solution)/shard_map/pallas_call | solution.py:30
  122.8 2.6 %collective-permute-start.8 = (bf16[8,16,512]{2,1,0:T(8,128)(2,1)S(1)}, bf16[8,16,512]{2,1,0:T(8,128)(2,1)S(1)}, u32[]{:S(2)}, u32[]{:S(2)}) collective-permute-start(bf16[8,16,512]{2,1,0:T(8,128)(2,1)S(1)} %get-tuple-element.37), channel_id=1, source_target_pairs={{0,384},{16,144},{32,416},{48,176},{64,448},{80,208},{96,480},{112... | collective-permute-start | bytes 393224 | tf_op jit(solution)/shard_map/ppermute | solution.py:180
  125.4 5.7 %collective-permute-start.9 = (bf16[8,16,512]{2,1,0:T(8,128)(2,1)S(1)}, bf16[8,16,512]{2,1,0:T(8,128)(2,1)S(1)}, u32[]{:S(2)}, u32[]{:S(2)}) collective-permute-start(bf16[8,16,512]{2,1,0:T(8,128)(2,1)S(1)} %get-tuple-element.38), channel_id=1, source_target_pairs={{0,480},{16,48},{32,0},{48,80},{64,32},{80,112},{96,64},{112,144},... | collective-permute-start | bytes 393224 | tf_op jit(solution)/shard_map/ppermute | solution.py:180
  131.1 1.9 collective-permute-start.10
  133.1 4.6 %collective-permute-start.11 = (bf16[8,16,512]{2,1,0:T(8,128)(2,1)S(1)}, bf16[8,16,512]{2,1,0:T(8,128)(2,1)S(1)}, u32[]{:S(2)}, u32[]{:S(2)}) collective-permute-start(bf16[8,16,512]{2,1,0:T(8,128)(2,1)S(1)} %get-tuple-element.40), channel_id=1, source_target_pairs={{0,448},{16,80},{32,480},{48,112},{64,0},{80,144},{96,32},{112,176... | collective-permute-start | bytes 393224 | tf_op jit(solution)/shard_map/ppermute | solution.py:180
  137.7 2.2 %collective-permute-start.12 = (bf16[8,16,512]{2,1,0:T(8,128)(2,1)S(1)}, bf16[8,16,512]{2,1,0:T(8,128)(2,1)S(1)}, u32[]{:S(2)}, u32[]{:S(2)}) collective-permute-start(bf16[8,16,512]{2,1,0:T(8,128)(2,1)S(1)} %get-tuple-element.41), channel_id=1, source_target_pairs={{0,64},{16,464},{32,96},{48,496},{64,128},{80,16},{96,160},{112,48... | collective-permute-start | bytes 393224 | tf_op jit(solution)/shard_map/ppermute | solution.py:180
  139.8 5.5 %collective-permute-start.13 = (bf16[8,16,512]{2,1,0:T(8,128)(2,1)S(1)}, bf16[8,16,512]{2,1,0:T(8,128)(2,1)S(1)}, u32[]{:S(2)}, u32[]{:S(2)}) collective-permute-start(bf16[8,16,512]{2,1,0:T(8,128)(2,1)S(1)} %get-tuple-element.42), channel_id=1, source_target_pairs={{0,416},{16,112},{32,448},{48,144},{64,480},{80,176},{96,0},{112,2... | collective-permute-start | bytes 393224 | tf_op jit(solution)/shard_map/ppermute | solution.py:180
  145.3 3.4 %collective-permute-start.14 = (bf16[8,16,512]{2,1,0:T(8,128)(2,1)S(1)}, bf16[8,16,512]{2,1,0:T(8,128)(2,1)S(1)}, u32[]{:S(2)}, u32[]{:S(2)}) collective-permute-start(bf16[8,16,512]{2,1,0:T(8,128)(2,1)S(1)} %get-tuple-element.43), channel_id=1, source_target_pairs={{0,96},{16,432},{32,128},{48,464},{64,160},{80,496},{96,192},{112,... | collective-permute-start | bytes 393224 | tf_op jit(solution)/shard_map/ppermute | solution.py:180
  150.3 6.5 %collective-permute-done.14.refs_7_ = bf16[8,16,512]{2,1,0:T(8,128)(2,1)S(1)} collective-permute-done((bf16[8,16,512]{2,1,0:T(8,128)(2,1)S(1)}, bf16[8,16,512]{2,1,0:T(8,128)(2,1)S(1)}, u32[]{:S(2)}, u32[]{:S(2)}) %collective-permute-start.14) | collective-permute-done | bytes 131104 | tf_op jit(solution)/shard_map/ppermute | solution.py:180
  163.2 7.2 %all-to-all-start.3 = ((bf16[16,2,16,512]{3,2,1,0:T(8,128)(2,1)}), bf16[16,2,16,512]{3,2,1,0:T(8,128)(2,1)S(1)}, u32[]{:S(2)}, u32[]{:S(2)}) async-start(bf16[16,2,16,512]{3,2,1,0:T(8,128)(2,1)} %bitcast.6), calls=%async_computation.3 | async-start | bytes 1048576 | tf_op jit(solution)/shard_map/all_to_all | solution.py:174
  170.6 3.0 %shard_map.87 = (bf16[1024,512]{1,0:T(8,128)(2,1)}, bf16[1024,512]{1,0:T(8,128)(2,1)}) custom-call(bf16[1024,128]{1,0:T(8,128)(2,1)S(1)} %bitcast.9, bf16[8,16,512]{2,1,0:T(8,128)(2,1)S(1)} %get-tuple-element.26.refs_0_, bf16[8,16,512]{2,1,0:T(8,128)(2,1)S(1)} %collective-permute-done.1.refs_1_, bf16[8,16,512]{2,1,0:T(8,128)(2,1)S(1)} %collective-permute-done.2.refs_2_, ...), custom_call_target="tpu_custom_call" | custom-call | tf_op jit(solution)/shard_map/pallas_call | solution.py:30
  173.7 26.1 %all-to-all-done.3.owned = bf16[16,2,16,512]{3,2,1,0:T(8,128)(2,1)S(1)} async-done(((bf16[16,2,16,512]{3,2,1,0:T(8,128)(2,1)}), bf16[16,2,16,512]{3,2,1,0:T(8,128)(2,1)S(1)}, u32[]{:S(2)}, u32[]{:S(2)}) %all-to-all-start.3) | async-done | bytes 524320 | tf_op jit(solution)/shard_map/all_to_all | solution.py:174
  (37 shorter events, 18.8 us)
Async XLA Ops:
  0.6 0.9 copy-start.2
  1.5 0.9 copy-start.3
  2.4 47.2 %copy-start.4 = (s32[256]{0:T(256)S(1)}, s32[256]{0:T(256)}, u32[]{:S(2)}) copy-start(s32[256]{0:T(256)} %table.3) | copy-start | bytes 3076
  2.5 86.1 %copy-start = (bf16[1024,512]{1,0:T(8,128)(2,1)S(1)}, bf16[1024,512]{1,0:T(8,128)(2,1)}, u32[]{:S(2)}) copy-start(bf16[1024,512]{1,0:T(8,128)(2,1)} %acts.3) | copy-start | bytes 3145732
  2.5 86.1 %copy-start.1 = (bf16[1024,512]{1,0:T(8,128)(2,1)S(1)}, bf16[1024,512]{1,0:T(8,128)(2,1)}, u32[]{:S(2)}) copy-start(bf16[1024,512]{1,0:T(8,128)(2,1)} %cot.3) | copy-start | bytes 3145732
  45.9 3.8 %collective-permute-start = (bf16[32,16,512]{2,1,0:T(8,128)(2,1)S(1)}, bf16[32,16,512]{2,1,0:T(8,128)(2,1)S(1)}, u32[]{:S(2)}, u32[]{:S(2)}) collective-permute-start(bf16[32,16,512]{2,1,0:T(8,128)(2,1)S(1)} %bitcast.11), channel_id=1, source_target_pairs={{0,16},{16,0},{1,17},{17,1},{2,18},{18,2},{3,19},{19,3},{4,20},{20... | collective-permute-start | bytes 1572872 | tf_op jit(solution)/shard_map/ppermute | solution.py:192
  51.9 19.8 %collective-permute-start.1 = (bf16[8,16,512]{2,1,0:T(8,128)(2,1)S(1)}, bf16[8,16,512]{2,1,0:T(8,128)(2,1)S(1)}, u32[]{:S(2)}, u32[]{:S(2)}) collective-permute-start(bf16[8,16,512]{2,1,0:T(8,128)(2,1)S(1)} %get-tuple-element.27), channel_id=1, source_target_pairs={{0,128},{16,400},{32,160},{48,432},{64,192},{80,464},{96,224},{112... | collective-permute-start | bytes 393224 | tf_op jit(solution)/shard_map/ppermute | solution.py:180
  57.9 17.9 %collective-permute-start.2 = (bf16[8,16,512]{2,1,0:T(8,128)(2,1)S(1)}, bf16[8,16,512]{2,1,0:T(8,128)(2,1)S(1)}, u32[]{:S(2)}, u32[]{:S(2)}) collective-permute-start(bf16[8,16,512]{2,1,0:T(8,128)(2,1)S(1)} %get-tuple-element.28), channel_id=1, source_target_pairs={{0,32},{16,496},{32,64},{48,16},{64,96},{80,48},{96,128},{112,80},... | collective-permute-start | bytes 393224 | tf_op jit(solution)/shard_map/ppermute | solution.py:180
  60.3 20.3 %collective-permute-start.3 = (bf16[8,16,512]{2,1,0:T(8,128)(2,1)S(1)}, bf16[8,16,512]{2,1,0:T(8,128)(2,1)S(1)}, u32[]{:S(2)}, u32[]{:S(2)}) collective-permute-start(bf16[8,16,512]{2,1,0:T(8,128)(2,1)S(1)} %get-tuple-element.29), channel_id=1, source_target_pairs={{0,480},{16,48},{32,0},{48,80},{64,32},{80,112},{96,64},{112,144},... | collective-permute-start | bytes 393224 | tf_op jit(solution)/shard_map/ppermute | solution.py:180
  63.7 16.9 %collective-permute-start.4 = (bf16[8,16,512]{2,1,0:T(8,128)(2,1)S(1)}, bf16[8,16,512]{2,1,0:T(8,128)(2,1)S(1)}, u32[]{:S(2)}, u32[]{:S(2)}) collective-permute-start(bf16[8,16,512]{2,1,0:T(8,128)(2,1)S(1)} %get-tuple-element.30), channel_id=1, source_target_pairs={{0,64},{16,464},{32,96},{48,496},{64,128},{80,16},{96,160},{112,48... | collective-permute-start | bytes 393224 | tf_op jit(solution)/shard_map/ppermute | solution.py:180
  66.6 14.0 %collective-permute-start.5 = (bf16[8,16,512]{2,1,0:T(8,128)(2,1)S(1)}, bf16[8,16,512]{2,1,0:T(8,128)(2,1)S(1)}, u32[]{:S(2)}, u32[]{:S(2)}) collective-permute-start(bf16[8,16,512]{2,1,0:T(8,128)(2,1)S(1)} %get-tuple-element.31), channel_id=1, source_target_pairs={{0,448},{16,80},{32,480},{48,112},{64,0},{80,144},{96,32},{112,176... | collective-permute-start | bytes 393224 | tf_op jit(solution)/shard_map/ppermute | solution.py:180
  71.7 15.2 %collective-permute-start.6 = (bf16[8,16,512]{2,1,0:T(8,128)(2,1)S(1)}, bf16[8,16,512]{2,1,0:T(8,128)(2,1)S(1)}, u32[]{:S(2)}, u32[]{:S(2)}) collective-permute-start(bf16[8,16,512]{2,1,0:T(8,128)(2,1)S(1)} %get-tuple-element.32), channel_id=1, source_target_pairs={{0,96},{16,432},{32,128},{48,464},{64,160},{80,496},{96,192},{112,... | collective-permute-start | bytes 393224 | tf_op jit(solution)/shard_map/ppermute | solution.py:180
  75.8 12.8 %collective-permute-start.7 = (bf16[8,16,512]{2,1,0:T(8,128)(2,1)S(1)}, bf16[8,16,512]{2,1,0:T(8,128)(2,1)S(1)}, u32[]{:S(2)}, u32[]{:S(2)}) collective-permute-start(bf16[8,16,512]{2,1,0:T(8,128)(2,1)S(1)} %get-tuple-element.33), channel_id=1, source_target_pairs={{0,416},{16,112},{32,448},{48,144},{64,480},{80,176},{96,0},{112,2... | collective-permute-start | bytes 393224 | tf_op jit(solution)/shard_map/ppermute | solution.py:180
  122.8 17.1 %collective-permute-start.8 = (bf16[8,16,512]{2,1,0:T(8,128)(2,1)S(1)}, bf16[8,16,512]{2,1,0:T(8,128)(2,1)S(1)}, u32[]{:S(2)}, u32[]{:S(2)}) collective-permute-start(bf16[8,16,512]{2,1,0:T(8,128)(2,1)S(1)} %get-tuple-element.37), channel_id=1, source_target_pairs={{0,384},{16,144},{32,416},{48,176},{64,448},{80,208},{96,480},{112... | collective-permute-start | bytes 393224 | tf_op jit(solution)/shard_map/ppermute | solution.py:180
  125.4 19.9 %collective-permute-start.9 = (bf16[8,16,512]{2,1,0:T(8,128)(2,1)S(1)}, bf16[8,16,512]{2,1,0:T(8,128)(2,1)S(1)}, u32[]{:S(2)}, u32[]{:S(2)}) collective-permute-start(bf16[8,16,512]{2,1,0:T(8,128)(2,1)S(1)} %get-tuple-element.38), channel_id=1, source_target_pairs={{0,480},{16,48},{32,0},{48,80},{64,32},{80,112},{96,64},{112,144},... | collective-permute-start | bytes 393224 | tf_op jit(solution)/shard_map/ppermute | solution.py:180
  131.1 17.6 %collective-permute-start.10 = (bf16[8,16,512]{2,1,0:T(8,128)(2,1)S(1)}, bf16[8,16,512]{2,1,0:T(8,128)(2,1)S(1)}, u32[]{:S(2)}, u32[]{:S(2)}) collective-permute-start(bf16[8,16,512]{2,1,0:T(8,128)(2,1)S(1)} %get-tuple-element.39), channel_id=1, source_target_pairs={{0,32},{16,496},{32,64},{48,16},{64,96},{80,48},{96,128},{112,80},... | collective-permute-start | bytes 393224 | tf_op jit(solution)/shard_map/ppermute | solution.py:180
  133.1 15.7 %collective-permute-start.11 = (bf16[8,16,512]{2,1,0:T(8,128)(2,1)S(1)}, bf16[8,16,512]{2,1,0:T(8,128)(2,1)S(1)}, u32[]{:S(2)}, u32[]{:S(2)}) collective-permute-start(bf16[8,16,512]{2,1,0:T(8,128)(2,1)S(1)} %get-tuple-element.40), channel_id=1, source_target_pairs={{0,448},{16,80},{32,480},{48,112},{64,0},{80,144},{96,32},{112,176... | collective-permute-start | bytes 393224 | tf_op jit(solution)/shard_map/ppermute | solution.py:180
  137.7 11.9 %collective-permute-start.12 = (bf16[8,16,512]{2,1,0:T(8,128)(2,1)S(1)}, bf16[8,16,512]{2,1,0:T(8,128)(2,1)S(1)}, u32[]{:S(2)}, u32[]{:S(2)}) collective-permute-start(bf16[8,16,512]{2,1,0:T(8,128)(2,1)S(1)} %get-tuple-element.41), channel_id=1, source_target_pairs={{0,64},{16,464},{32,96},{48,496},{64,128},{80,16},{96,160},{112,48... | collective-permute-start | bytes 393224 | tf_op jit(solution)/shard_map/ppermute | solution.py:180
  139.8 10.5 %collective-permute-start.13 = (bf16[8,16,512]{2,1,0:T(8,128)(2,1)S(1)}, bf16[8,16,512]{2,1,0:T(8,128)(2,1)S(1)}, u32[]{:S(2)}, u32[]{:S(2)}) collective-permute-start(bf16[8,16,512]{2,1,0:T(8,128)(2,1)S(1)} %get-tuple-element.42), channel_id=1, source_target_pairs={{0,416},{16,112},{32,448},{48,144},{64,480},{80,176},{96,0},{112,2... | collective-permute-start | bytes 393224 | tf_op jit(solution)/shard_map/ppermute | solution.py:180
  145.3 11.5 %collective-permute-start.14 = (bf16[8,16,512]{2,1,0:T(8,128)(2,1)S(1)}, bf16[8,16,512]{2,1,0:T(8,128)(2,1)S(1)}, u32[]{:S(2)}, u32[]{:S(2)}) collective-permute-start(bf16[8,16,512]{2,1,0:T(8,128)(2,1)S(1)} %get-tuple-element.43), channel_id=1, source_target_pairs={{0,96},{16,432},{32,128},{48,464},{64,160},{80,496},{96,192},{112,... | collective-permute-start | bytes 393224 | tf_op jit(solution)/shard_map/ppermute | solution.py:180
  158.4 3.8 %collective-permute-start.15 = (bf16[32,16,512]{2,1,0:T(8,128)(2,1)S(1)}, bf16[32,16,512]{2,1,0:T(8,128)(2,1)S(1)}, u32[]{:S(2)}, u32[]{:S(2)}) collective-permute-start(bf16[32,16,512]{2,1,0:T(8,128)(2,1)S(1)} %get-tuple-element.45), channel_id=1, source_target_pairs={{0,16},{16,0},{1,17},{17,1},{2,18},{18,2},{3,19},{19,3},{4,20},{20... | collective-permute-start | bytes 1572872 | tf_op jit(solution)/shard_map/ppermute | solution.py:208
  163.2 36.6 %all-to-all-start.3 = ((bf16[16,2,16,512]{3,2,1,0:T(8,128)(2,1)}), bf16[16,2,16,512]{3,2,1,0:T(8,128)(2,1)S(1)}, u32[]{:S(2)}, u32[]{:S(2)}) async-start(bf16[16,2,16,512]{3,2,1,0:T(8,128)(2,1)} %bitcast.6), calls=%async_computation.3 | async-start | bytes 1048576 | tf_op jit(solution)/shard_map/all_to_all | solution.py:174

commit v4 on v3

--- a/solution.py
+++ b/solution.py
@@ -89,6 +89,19 @@
             @pl.when(par != core)
             def _():
                 out[b] = other[row]
+
+
+def sum_parts(got, out):
+    total = got[0]
+    for i in range(1, got.shape[0]):
+        total = total + got[i]
+    total = total.astype(BF16)
+    for i in range(out.shape[0]):
+        out[i] = total
+
+
+def add_other(keep, other, out):
+    out[...] = (keep[...] + other[...].astype(F32)).astype(BF16).reshape(out.shape)
 
 
 def is_first(dims, axis):
@@ -182,8 +195,7 @@
     def total(part):
         rows = part.shape[0] // nxy
         got = lax.all_to_all(part.reshape(nxy, rows, part.shape[1]), "xy", 0, 0, tiled=True)
-        mine = jnp.sum(got, axis=0).astype(BF16)
-        spread = jnp.broadcast_to(mine[None], (nxy,) + mine.shape)
+        spread = call(sum_parts, shape(got.shape, BF16), (got,), [VMEM])
         return lax.all_to_all(spread, "xy", 0, 0, tiled=True).reshape(part.shape)
 
     down = jnp.swapaxes(adapter_down_weights, 1, 2)
@@ -194,6 +206,9 @@
         functools.partial(pick_pieces, nz), slots, (table, where, held, held_other), [SMEM, SMEM, VMEM, VMEM]
     )
     pieces = [shift(w, step) for w, step in zip(wanted, STEPS)]
+    ids = (where[0] * CORES + where[1]) * share + jnp.arange(share, dtype=jnp.int32)
+    counts = jnp.sum((table[:, None] == ids[None, :]).astype(F32), axis=0) * BLOCK
+    pieces, counts = lax.optimization_barrier((pieces, counts))
     sums = total(
         call(
             partial_sums, shape((tokens, 2 * rank), F32), (activations, cotangent, *pieces), [VMEM] * (2 + len(STEPS))
@@ -201,17 +216,15 @@
     )
     parts = call(block_grads, slots, (activations, cotangent, sums), [VMEM] * 3)
     gots = [shift(g, -step) for g, step in zip(parts, STEPS)]
+    out, grad = call(outputs, (shape((tokens, width), BF16),) * 2, (sums, *pieces), [VMEM] * (1 + len(STEPS)))
+    gots, out, grad = lax.optimization_barrier((gots, out, grad))
     keep, send = call(
         functools.partial(sum_pieces, nz), (shape((own,) + piece, F32), shape((own,) + piece, BF16)),
         (table, where, *gots), [SMEM, SMEM] + [VMEM] * len(STEPS), [pltpu.VMEM((CORES * own,) + piece, F32)],
     )
-    merged = (keep + lax.ppermute(send, "core", swap).astype(F32)).astype(BF16)
-    owned = over_z(merged.reshape(nz, share, *piece))
-
-    out, grad = call(outputs, (shape((tokens, width), BF16),) * 2, (sums, *pieces), [VMEM] * (1 + len(STEPS)))
-
-    ids = (where[0] * CORES + where[1]) * share + jnp.arange(share, dtype=jnp.int32)
-    counts = jnp.sum((table[:, None] == ids[None, :]).astype(F32), axis=0) * BLOCK
+    from_other = lax.ppermute(send, "core", swap)
+    merged = call(add_other, shape((nz, share) + piece, BF16), (keep, from_other), [VMEM] * 2)
+    owned = over_z(merged)
     down_grad, up_grad = call(means, (shape((share, rank, width), F32),) * 2, (counts, owned), [SMEM, VMEM])
     return out, grad, jnp.swapaxes(down_grad, 1, 2), up_grad
 

time: 202 us -> 200 us (0.990)
  blocking collectives: 73.5 us -> 110 us
  waiting for transfers between devices: 45.8 us -> 16.8 us
  starting transfers between devices: 65.6 us -> 58.3 us
  other arithmetic: 2.33 us -> 0.27 us
    all_to_all x1 -> x2, blocking collectives: 43.4 us -> 79.8 us  [over_z(): return lax.all_to_all(x, 'z', 0, 0, tiled=True)]
    all_to_all x1 -> x0, waiting for transfers between devices: 26.1 us -> none  [over_z(): return lax.all_to_all(x, 'z', 0, 0, tiled=True)]
    all_to_all x1 -> x0, starting transfers between devices: 7.23 us -> none  [over_z(): return lax.all_to_all(x, 'z', 0, 0, tiled=True)]
    ppermute x14, waiting for transfers between devices: 16 us -> 13.1 us  [shift(): return lax.ppermute(x, ('z', 'core'), pairs)]
    pallas_call x7 -> x9, Pallas kernels: 11.2 us -> 11.2 us  [call(): pl.pallas_call(body, out_shape=outs, in_specs=in_specs, out_specs=jax.tre...]
  transfers between devices with their start and end apart: 17 -> 16, of which waited for: 8 -> 5; matrix products, arithmetic and copies ran while one was open for 0% -> 0% of each run, Pallas kernels for 2% -> 2%
where the time goes in v4:
time: 200 us; the launch traced here: 199 us
  blocking collectives  110 us (55%)
  starting transfers between devices  58.3 us (29%)
  waiting for transfers between devices  16.8 us (8%)
  Pallas kernels  11.2 us (6%)
    all_to_all x2, blocking collectives, over_z(): return lax.all_to_all(x, 'z', 0, 0, tiled=True)  79.8 us
    ppermute x14, starting transfers between devices, shift(): return lax.ppermute(x, ('z', 'core'), pairs)  54.5 us
    all_to_all x1, blocking collectives, total(): lax.all_to_all(part.reshape(nxy, rows, part.shape[1]), 'xy', 0, 0, tiled=...  18.3 us
    ppermute x14, waiting for transfers between devices, shift(): return lax.ppermute(x, ('z', 'core'), pairs)  13.1 us
    all_to_all x1, blocking collectives, total(): return lax.all_to_all(spread, 'xy', 0, 0, tiled=True).reshape(part.shape)  11.8 us
    pallas_call x9, Pallas kernels, call(): pl.pallas_call(body, out_shape=outs, in_specs=in_specs, out_specs=jax.tre...  11.2 us
  transfers between devices with their start and end apart: 16, of which 5 were waited for; matrix products, arithmetic and copies ran while one was open for 0% of the time, Pallas kernels for 2%

profile of v4, /device:TPU:32, one launch (start us, length us, event | category | flops | bytes accessed | tf_op | source)
XLA Modules:
  0.0 199.2 jit_solution(2596132108122708964)
XLA Ops:
  2.5 43.4 %all_to_all.20 = bf16[16,2,16,512]{3,2,1,0:T(8,128)(2,1)S(1)} all-to-all(bf16[16,2,16,512]{3,2,1,0:T(8,128)(2,1)S(1)} %shard_map.84), channel_id=1, replica_groups=mesh['z'=16,'core'=2,'xy'=16] {'z'}, dimensions={0} | all-to-all | bytes 1048576 | tf_op jit(solution)/shard_map/all_to_all | solution.py:187
  49.7 2.2 %shard_map.85 = (bf16[8,16,512]{2,1,0:T(8,128)(2,1)S(1)}, bf16[8,16,512]{2,1,0:T(8,128)(2,1)S(1)}, bf16[8,16,512]{2,1,0:T(8,128)(2,1)S(1)}, bf16[8,16,512]{2,1,0...) custom-call(s32[256]{0:T(256)S(1)} %copy-done.4, ...), custom_call_target="tpu_custom_call" | custom-call | tf_op jit(solution)/shard_map/pallas_call | solution.py:30
  51.8 6.0 %collective-permute-start.1 = (bf16[8,16,512]{2,1,0:T(8,128)(2,1)S(1)}, bf16[8,16,512]{2,1,0:T(8,128)(2,1)S(1)}, u32[]{:S(2)}, u32[]{:S(2)}) collective-permute-start(bf16[8,16,512]{2,1,0:T(8,128)(2,1)S(1)} %get-tuple-element.46), channel_id=1, source_target_pairs={{0,128},{16,400},{32,160},{48,432},{64,192},{80,464},{96,224},{112... | collective-permute-start | bytes 393224 | tf_op jit(solution)/shard_map/ppermute | solution.py:193
  57.8 2.4 %collective-permute-start.2 = (bf16[8,16,512]{2,1,0:T(8,128)(2,1)S(1)}, bf16[8,16,512]{2,1,0:T(8,128)(2,1)S(1)}, u32[]{:S(2)}, u32[]{:S(2)}) collective-permute-start(bf16[8,16,512]{2,1,0:T(8,128)(2,1)S(1)} %get-tuple-element.47), channel_id=1, source_target_pairs={{0,32},{16,496},{32,64},{48,16},{64,96},{80,48},{96,128},{112,80},... | collective-permute-start | bytes 393224 | tf_op jit(solution)/shard_map/ppermute | solution.py:193
  60.4 3.5 %collective-permute-start.3 = (bf16[8,16,512]{2,1,0:T(8,128)(2,1)S(1)}, bf16[8,16,512]{2,1,0:T(8,128)(2,1)S(1)}, u32[]{:S(2)}, u32[]{:S(2)}) collective-permute-start(bf16[8,16,512]{2,1,0:T(8,128)(2,1)S(1)} %get-tuple-element.48), channel_id=1, source_target_pairs={{0,480},{16,48},{32,0},{48,80},{64,32},{80,112},{96,64},{112,144},... | collective-permute-start | bytes 393224 | tf_op jit(solution)/shard_map/ppermute | solution.py:193
  63.9 2.8 %collective-permute-start.4 = (bf16[8,16,512]{2,1,0:T(8,128)(2,1)S(1)}, bf16[8,16,512]{2,1,0:T(8,128)(2,1)S(1)}, u32[]{:S(2)}, u32[]{:S(2)}) collective-permute-start(bf16[8,16,512]{2,1,0:T(8,128)(2,1)S(1)} %get-tuple-element.49), channel_id=1, source_target_pairs={{0,64},{16,464},{32,96},{48,496},{64,128},{80,16},{96,160},{112,48... | collective-permute-start | bytes 393224 | tf_op jit(solution)/shard_map/ppermute | solution.py:193
  66.7 5.1 %collective-permute-start.5 = (bf16[8,16,512]{2,1,0:T(8,128)(2,1)S(1)}, bf16[8,16,512]{2,1,0:T(8,128)(2,1)S(1)}, u32[]{:S(2)}, u32[]{:S(2)}) collective-permute-start(bf16[8,16,512]{2,1,0:T(8,128)(2,1)S(1)} %get-tuple-element.50), channel_id=1, source_target_pairs={{0,448},{16,80},{32,480},{48,112},{64,0},{80,144},{96,32},{112,176... | collective-permute-start | bytes 393224 | tf_op jit(solution)/shard_map/ppermute | solution.py:193
  71.8 4.0 %collective-permute-start.6 = (bf16[8,16,512]{2,1,0:T(8,128)(2,1)S(1)}, bf16[8,16,512]{2,1,0:T(8,128)(2,1)S(1)}, u32[]{:S(2)}, u32[]{:S(2)}) collective-permute-start(bf16[8,16,512]{2,1,0:T(8,128)(2,1)S(1)} %get-tuple-element.51), channel_id=1, source_target_pairs={{0,96},{16,432},{32,128},{48,464},{64,160},{80,496},{96,192},{112,... | collective-permute-start | bytes 393224 | tf_op jit(solution)/shard_map/ppermute | solution.py:193
  75.9 4.8 %collective-permute-start.7 = (bf16[8,16,512]{2,1,0:T(8,128)(2,1)S(1)}, bf16[8,16,512]{2,1,0:T(8,128)(2,1)S(1)}, u32[]{:S(2)}, u32[]{:S(2)}) collective-permute-start(bf16[8,16,512]{2,1,0:T(8,128)(2,1)S(1)} %get-tuple-element.52), channel_id=1, source_target_pairs={{0,416},{16,112},{32,448},{48,144},{64,480},{80,176},{96,0},{112,2... | collective-permute-start | bytes 393224 | tf_op jit(solution)/shard_map/ppermute | solution.py:193
  80.8 7.4 %collective-permute-done.6.refs_6_ = bf16[8,16,512]{2,1,0:T(8,128)(2,1)S(1)} collective-permute-done((bf16[8,16,512]{2,1,0:T(8,128)(2,1)S(1)}, bf16[8,16,512]{2,1,0:T(8,128)(2,1)S(1)}, u32[]{:S(2)}, u32[]{:S(2)}) %collective-permute-start.6) | collective-permute-done | bytes 131104 | tf_op jit(solution)/shard_map/ppermute | solution.py:193
  89.4 18.3 %all_to_all.21.got = f32[16,64,128]{2,1,0:T(8,128)S(1)} all-to-all(f32[16,64,128]{2,1,0:T(8,128)S(1)} %bitcast.9), channel_id=1, replica_groups=mesh['z'=16,'core'=2,'xy'=16] {'xy'}, dimensions={0} | all-to-all | bytes 1048576 | tf_op jit(solution)/shard_map/all_to_all | solution.py:197
  107.8 11.8 %all_to_all.22 = bf16[16,64,128]{2,1,0:T(8,128)(2,1)S(1)} all-to-all(bf16[16,64,128]{2,1,0:T(8,128)(2,1)S(1)} %shard_map.87), channel_id=1, replica_groups=mesh['z'=16,'core'=2,'xy'=16] {'xy'}, dimensions={0} | all-to-all | bytes 524288 | tf_op jit(solution)/shard_map/all_to_all | solution.py:199
  119.5 2.2 %shard_map.88 = (bf16[8,16,512]{2,1,0:T(8,128)(2,1)S(1)}, bf16[8,16,512]{2,1,0:T(8,128)(2,1)S(1)}, bf16[8,16,512]{2,1,0:T(8,128)(2,1)S(1)}, bf16[8,16,512]{2,1,0...) custom-call(bf16[1024,512]{1,0:T(8,128)(2,1)S(1)} %copy-done, ...), custom_call_target="tpu_custom_call" | custom-call | tf_op jit(solution)/shard_map/pallas_call | solution.py:30
  121.7 2.7 %collective-permute-start.8 = (bf16[8,16,512]{2,1,0:T(8,128)(2,1)S(1)}, bf16[8,16,512]{2,1,0:T(8,128)(2,1)S(1)}, u32[]{:S(2)}, u32[]{:S(2)}) collective-permute-start(bf16[8,16,512]{2,1,0:T(8,128)(2,1)S(1)} %get-tuple-element.62), channel_id=1, source_target_pairs={{0,384},{16,144},{32,416},{48,176},{64,448},{80,208},{96,480},{112... | collective-permute-start | bytes 393224 | tf_op jit(solution)/shard_map/ppermute | solution.py:193
  124.4 5.6 %collective-permute-start.9 = (bf16[8,16,512]{2,1,0:T(8,128)(2,1)S(1)}, bf16[8,16,512]{2,1,0:T(8,128)(2,1)S(1)}, u32[]{:S(2)}, u32[]{:S(2)}) collective-permute-start(bf16[8,16,512]{2,1,0:T(8,128)(2,1)S(1)} %get-tuple-element.63), channel_id=1, source_target_pairs={{0,480},{16,48},{32,0},{48,80},{64,32},{80,112},{96,64},{112,144},... | collective-permute-start | bytes 393224 | tf_op jit(solution)/shard_map/ppermute | solution.py:193
  130.1 1.9 collective-permute-start.10
  132.0 4.6 %collective-permute-start.11 = (bf16[8,16,512]{2,1,0:T(8,128)(2,1)S(1)}, bf16[8,16,512]{2,1,0:T(8,128)(2,1)S(1)}, u32[]{:S(2)}, u32[]{:S(2)}) collective-permute-start(bf16[8,16,512]{2,1,0:T(8,128)(2,1)S(1)} %get-tuple-element.65), channel_id=1, source_target_pairs={{0,448},{16,80},{32,480},{48,112},{64,0},{80,144},{96,32},{112,176... | collective-permute-start | bytes 393224 | tf_op jit(solution)/shard_map/ppermute | solution.py:193
  136.6 2.2 %collective-permute-start.12 = (bf16[8,16,512]{2,1,0:T(8,128)(2,1)S(1)}, bf16[8,16,512]{2,1,0:T(8,128)(2,1)S(1)}, u32[]{:S(2)}, u32[]{:S(2)}) collective-permute-start(bf16[8,16,512]{2,1,0:T(8,128)(2,1)S(1)} %get-tuple-element.66), channel_id=1, source_target_pairs={{0,64},{16,464},{32,96},{48,496},{64,128},{80,16},{96,160},{112,48... | collective-permute-start | bytes 393224 | tf_op jit(solution)/shard_map/ppermute | solution.py:193
  138.8 5.6 %collective-permute-start.13 = (bf16[8,16,512]{2,1,0:T(8,128)(2,1)S(1)}, bf16[8,16,512]{2,1,0:T(8,128)(2,1)S(1)}, u32[]{:S(2)}, u32[]{:S(2)}) collective-permute-start(bf16[8,16,512]{2,1,0:T(8,128)(2,1)S(1)} %get-tuple-element.67), channel_id=1, source_target_pairs={{0,416},{16,112},{32,448},{48,144},{64,480},{80,176},{96,0},{112,2... | collective-permute-start | bytes 393224 | tf_op jit(solution)/shard_map/ppermute | solution.py:193
  144.4 3.3 %collective-permute-start.14 = (bf16[8,16,512]{2,1,0:T(8,128)(2,1)S(1)}, bf16[8,16,512]{2,1,0:T(8,128)(2,1)S(1)}, u32[]{:S(2)}, u32[]{:S(2)}) collective-permute-start(bf16[8,16,512]{2,1,0:T(8,128)(2,1)S(1)} %get-tuple-element.68), channel_id=1, source_target_pairs={{0,96},{16,432},{32,128},{48,464},{64,160},{80,496},{96,192},{112,... | collective-permute-start | bytes 393224 | tf_op jit(solution)/shard_map/ppermute | solution.py:193
  147.6 3.0 %shard_map.89 = (bf16[1024,512]{1,0:T(8,128)(2,1)}, bf16[1024,512]{1,0:T(8,128)(2,1)}) custom-call(bf16[1024,128]{1,0:T(8,128)(2,1)S(1)} %bitcast.8, bf16[8,16,512]{2,1,0:T(8,128)(2,1)S(1)} %get-tuple-element.53.refs_0_, bf16[8,16,512]{2,1,0:T(8,128)(2,1)S(1)} %collective-permute-done.1.refs_1_, bf16[8,16,512]{2,1,0:T(8,128)(2,1)S(1)} %collective-permute-done.2.refs_2_, ...), custom_call_target="tpu_custom_call" | custom-call | tf_op jit(solution)/shard_map/pallas_call | solution.py:30
  150.7 5.2 %collective-permute-done.14.refs_7_ = bf16[8,16,512]{2,1,0:T(8,128)(2,1)S(1)} collective-permute-done((bf16[8,16,512]{2,1,0:T(8,128)(2,1)S(1)}, bf16[8,16,512]{2,1,0:T(8,128)(2,1)S(1)}, u32[]{:S(2)}, u32[]{:S(2)}) %collective-permute-start.14) | collective-permute-done | bytes 131104 | tf_op jit(solution)/shard_map/ppermute | solution.py:193
  157.5 1.9 collective-permute-start.15
  161.4 36.4 %all_to_all.23.owned = bf16[16,2,16,512]{3,2,1,0:T(8,128)(2,1)S(1)} all-to-all(bf16[16,2,16,512]{3,2,1,0:T(8,128)(2,1)S(1)} %shard_map.91), channel_id=1, replica_groups=mesh['z'=16,'core'=2,'xy'=16] {'z'}, dimensions={0} | all-to-all | bytes 1048576 | tf_op jit(solution)/shard_map/all_to_all | solution.py:187
  (35 shorter events, 12.1 us)
Async XLA Ops:
  0.6 0.9 copy-start.2
  1.5 0.9 copy-start.3
  2.4 47.2 %copy-start.4 = (s32[256]{0:T(256)S(1)}, s32[256]{0:T(256)}, u32[]{:S(2)}) copy-start(s32[256]{0:T(256)} %table.3) | copy-start | bytes 3076
  2.5 86.2 %copy-start = (bf16[1024,512]{1,0:T(8,128)(2,1)S(1)}, bf16[1024,512]{1,0:T(8,128)(2,1)}, u32[]{:S(2)}) copy-start(bf16[1024,512]{1,0:T(8,128)(2,1)} %acts.3) | copy-start | bytes 3145732
  2.5 86.2 %copy-start.1 = (bf16[1024,512]{1,0:T(8,128)(2,1)S(1)}, bf16[1024,512]{1,0:T(8,128)(2,1)}, u32[]{:S(2)}) copy-start(bf16[1024,512]{1,0:T(8,128)(2,1)} %cot.3) | copy-start | bytes 3145732
  45.9 3.8 %collective-permute-start = (bf16[32,16,512]{2,1,0:T(8,128)(2,1)S(1)}, bf16[32,16,512]{2,1,0:T(8,128)(2,1)S(1)}, u32[]{:S(2)}, u32[]{:S(2)}) collective-permute-start(bf16[32,16,512]{2,1,0:T(8,128)(2,1)S(1)} %bitcast.10), channel_id=1, source_target_pairs={{0,16},{16,0},{1,17},{17,1},{2,18},{18,2},{3,19},{19,3},{4,20},{20... | collective-permute-start | bytes 1572872 | tf_op jit(solution)/shard_map/ppermute | solution.py:204
  51.8 20.0 %collective-permute-start.1 = (bf16[8,16,512]{2,1,0:T(8,128)(2,1)S(1)}, bf16[8,16,512]{2,1,0:T(8,128)(2,1)S(1)}, u32[]{:S(2)}, u32[]{:S(2)}) collective-permute-start(bf16[8,16,512]{2,1,0:T(8,128)(2,1)S(1)} %get-tuple-element.46), channel_id=1, source_target_pairs={{0,128},{16,400},{32,160},{48,432},{64,192},{80,464},{96,224},{112... | collective-permute-start | bytes 393224 | tf_op jit(solution)/shard_map/ppermute | solution.py:193
  57.8 18.1 %collective-permute-start.2 = (bf16[8,16,512]{2,1,0:T(8,128)(2,1)S(1)}, bf16[8,16,512]{2,1,0:T(8,128)(2,1)S(1)}, u32[]{:S(2)}, u32[]{:S(2)}) collective-permute-start(bf16[8,16,512]{2,1,0:T(8,128)(2,1)S(1)} %get-tuple-element.47), channel_id=1, source_target_pairs={{0,32},{16,496},{32,64},{48,16},{64,96},{80,48},{96,128},{112,80},... | collective-permute-start | bytes 393224 | tf_op jit(solution)/shard_map/ppermute | solution.py:193
  60.4 20.3 %collective-permute-start.3 = (bf16[8,16,512]{2,1,0:T(8,128)(2,1)S(1)}, bf16[8,16,512]{2,1,0:T(8,128)(2,1)S(1)}, u32[]{:S(2)}, u32[]{:S(2)}) collective-permute-start(bf16[8,16,512]{2,1,0:T(8,128)(2,1)S(1)} %get-tuple-element.48), channel_id=1, source_target_pairs={{0,480},{16,48},{32,0},{48,80},{64,32},{80,112},{96,64},{112,144},... | collective-permute-start | bytes 393224 | tf_op jit(solution)/shard_map/ppermute | solution.py:193
  63.9 16.9 %collective-permute-start.4 = (bf16[8,16,512]{2,1,0:T(8,128)(2,1)S(1)}, bf16[8,16,512]{2,1,0:T(8,128)(2,1)S(1)}, u32[]{:S(2)}, u32[]{:S(2)}) collective-permute-start(bf16[8,16,512]{2,1,0:T(8,128)(2,1)S(1)} %get-tuple-element.49), channel_id=1, source_target_pairs={{0,64},{16,464},{32,96},{48,496},{64,128},{80,16},{96,160},{112,48... | collective-permute-start | bytes 393224 | tf_op jit(solution)/shard_map/ppermute | solution.py:193
  66.7 14.1 %collective-permute-start.5 = (bf16[8,16,512]{2,1,0:T(8,128)(2,1)S(1)}, bf16[8,16,512]{2,1,0:T(8,128)(2,1)S(1)}, u32[]{:S(2)}, u32[]{:S(2)}) collective-permute-start(bf16[8,16,512]{2,1,0:T(8,128)(2,1)S(1)} %get-tuple-element.50), channel_id=1, source_target_pairs={{0,448},{16,80},{32,480},{48,112},{64,0},{80,144},{96,32},{112,176... | collective-permute-start | bytes 393224 | tf_op jit(solution)/shard_map/ppermute | solution.py:193
  71.8 16.3 %collective-permute-start.6 = (bf16[8,16,512]{2,1,0:T(8,128)(2,1)S(1)}, bf16[8,16,512]{2,1,0:T(8,128)(2,1)S(1)}, u32[]{:S(2)}, u32[]{:S(2)}) collective-permute-start(bf16[8,16,512]{2,1,0:T(8,128)(2,1)S(1)} %get-tuple-element.51), channel_id=1, source_target_pairs={{0,96},{16,432},{32,128},{48,464},{64,160},{80,496},{96,192},{112,... | collective-permute-start | bytes 393224 | tf_op jit(solution)/shard_map/ppermute | solution.py:193
  75.9 12.8 %collective-permute-start.7 = (bf16[8,16,512]{2,1,0:T(8,128)(2,1)S(1)}, bf16[8,16,512]{2,1,0:T(8,128)(2,1)S(1)}, u32[]{:S(2)}, u32[]{:S(2)}) collective-permute-start(bf16[8,16,512]{2,1,0:T(8,128)(2,1)S(1)} %get-tuple-element.52), channel_id=1, source_target_pairs={{0,416},{16,112},{32,448},{48,144},{64,480},{80,176},{96,0},{112,2... | collective-permute-start | bytes 393224 | tf_op jit(solution)/shard_map/ppermute | solution.py:193
  121.7 17.0 %collective-permute-start.8 = (bf16[8,16,512]{2,1,0:T(8,128)(2,1)S(1)}, bf16[8,16,512]{2,1,0:T(8,128)(2,1)S(1)}, u32[]{:S(2)}, u32[]{:S(2)}) collective-permute-start(bf16[8,16,512]{2,1,0:T(8,128)(2,1)S(1)} %get-tuple-element.62), channel_id=1, source_target_pairs={{0,384},{16,144},{32,416},{48,176},{64,448},{80,208},{96,480},{112... | collective-permute-start | bytes 393224 | tf_op jit(solution)/shard_map/ppermute | solution.py:193
  124.4 19.9 %collective-permute-start.9 = (bf16[8,16,512]{2,1,0:T(8,128)(2,1)S(1)}, bf16[8,16,512]{2,1,0:T(8,128)(2,1)S(1)}, u32[]{:S(2)}, u32[]{:S(2)}) collective-permute-start(bf16[8,16,512]{2,1,0:T(8,128)(2,1)S(1)} %get-tuple-element.63), channel_id=1, source_target_pairs={{0,480},{16,48},{32,0},{48,80},{64,32},{80,112},{96,64},{112,144},... | collective-permute-start | bytes 393224 | tf_op jit(solution)/shard_map/ppermute | solution.py:193
  130.1 20.6 %collective-permute-start.10 = (bf16[8,16,512]{2,1,0:T(8,128)(2,1)S(1)}, bf16[8,16,512]{2,1,0:T(8,128)(2,1)S(1)}, u32[]{:S(2)}, u32[]{:S(2)}) collective-permute-start(bf16[8,16,512]{2,1,0:T(8,128)(2,1)S(1)} %get-tuple-element.64), channel_id=1, source_target_pairs={{0,32},{16,496},{32,64},{48,16},{64,96},{80,48},{96,128},{112,80},... | collective-permute-start | bytes 393224 | tf_op jit(solution)/shard_map/ppermute | solution.py:193
  132.0 18.7 %collective-permute-start.11 = (bf16[8,16,512]{2,1,0:T(8,128)(2,1)S(1)}, bf16[8,16,512]{2,1,0:T(8,128)(2,1)S(1)}, u32[]{:S(2)}, u32[]{:S(2)}) collective-permute-start(bf16[8,16,512]{2,1,0:T(8,128)(2,1)S(1)} %get-tuple-element.65), channel_id=1, source_target_pairs={{0,448},{16,80},{32,480},{48,112},{64,0},{80,144},{96,32},{112,176... | collective-permute-start | bytes 393224 | tf_op jit(solution)/shard_map/ppermute | solution.py:193
  136.6 14.1 %collective-permute-start.12 = (bf16[8,16,512]{2,1,0:T(8,128)(2,1)S(1)}, bf16[8,16,512]{2,1,0:T(8,128)(2,1)S(1)}, u32[]{:S(2)}, u32[]{:S(2)}) collective-permute-start(bf16[8,16,512]{2,1,0:T(8,128)(2,1)S(1)} %get-tuple-element.66), channel_id=1, source_target_pairs={{0,64},{16,464},{32,96},{48,496},{64,128},{80,16},{96,160},{112,48... | collective-permute-start | bytes 393224 | tf_op jit(solution)/shard_map/ppermute | solution.py:193
  138.8 11.9 %collective-permute-start.13 = (bf16[8,16,512]{2,1,0:T(8,128)(2,1)S(1)}, bf16[8,16,512]{2,1,0:T(8,128)(2,1)S(1)}, u32[]{:S(2)}, u32[]{:S(2)}) collective-permute-start(bf16[8,16,512]{2,1,0:T(8,128)(2,1)S(1)} %get-tuple-element.67), channel_id=1, source_target_pairs={{0,416},{16,112},{32,448},{48,144},{64,480},{80,176},{96,0},{112,2... | collective-permute-start | bytes 393224 | tf_op jit(solution)/shard_map/ppermute | solution.py:193
  144.4 11.5 %collective-permute-start.14 = (bf16[8,16,512]{2,1,0:T(8,128)(2,1)S(1)}, bf16[8,16,512]{2,1,0:T(8,128)(2,1)S(1)}, u32[]{:S(2)}, u32[]{:S(2)}) collective-permute-start(bf16[8,16,512]{2,1,0:T(8,128)(2,1)S(1)} %get-tuple-element.68), channel_id=1, source_target_pairs={{0,96},{16,432},{32,128},{48,464},{64,160},{80,496},{96,192},{112,... | collective-permute-start | bytes 393224 | tf_op jit(solution)/shard_map/ppermute | solution.py:193
  157.5 3.8 %collective-permute-start.15 = (bf16[32,16,512]{2,1,0:T(8,128)(2,1)S(1)}, bf16[32,16,512]{2,1,0:T(8,128)(2,1)S(1)}, u32[]{:S(2)}, u32[]{:S(2)}) collective-permute-start(bf16[32,16,512]{2,1,0:T(8,128)(2,1)S(1)} %get-tuple-element.83), channel_id=1, source_target_pairs={{0,16},{16,0},{1,17},{17,1},{2,18},{18,2},{3,19},{19,3},{4,20},{20... | collective-permute-start | bytes 1572872 | tf_op jit(solution)/shard_map/ppermute | solution.py:225

commit v5 on v4

--- a/solution.py
+++ b/solution.py
@@ -12,7 +12,8 @@
 CORES = 2
 COPIES = 2
 GROUP = 8
-STEPS = (0, 4, 1, -1, 2, -2, 3, -3)
+STEPS = (0, 4, -3, 3, -2, 2, -1, 1)
+HALVES = (slice(0, 4), slice(4, 8))
 F32, BF16 = jnp.float32, jnp.bfloat16
 
 VMEM = pl.BlockSpec(memory_space=pltpu.VMEM)
@@ -112,18 +113,22 @@
     return ref[b * BLOCK:(b + 1) * BLOCK, :]
 
 
-def matrix(pieces, b):
-    return jnp.concatenate([p[b] for p in pieces], axis=0)
+def matrix(pieces, b, blocks):
+    w = jnp.concatenate([p[b] for p in pieces], axis=0)
+    zero = jnp.zeros_like(w)
+    return jnp.concatenate([w, zero] if b < blocks // 2 else [zero, w], axis=0)
 
 
 def partial_sums(acts, cot, *refs):
     pieces, out = refs[:-1], refs[-1]
-    lanes = out.shape[1]
-    first = is_first((BLOCK, lanes), 1)
-    for b in range(pieces[0].shape[0]):
-        w = matrix(pieces, b)
-        proj, back = dot(rows_of(acts, b), w, NT), dot(rows_of(cot, b), w, NT)
-        out[b * BLOCK:(b + 1) * BLOCK, :] = jnp.where(first, proj, SCALE * back)
+    blocks = pieces[0].shape[0]
+    first = is_first((BLOCK, out.shape[1]), 1)
+    for j in range(blocks // 2):
+        proj, back = 0, 0
+        for b in (j, j + blocks // 2):
+            w = matrix(pieces, b, blocks)
+            proj, back = proj + dot(rows_of(acts, b), w, NT), back + dot(rows_of(cot, b), w, NT)
+        out[j * BLOCK:(j + 1) * BLOCK, :] = jnp.where(first, proj, SCALE * back)
 
 
 def swapped(sums, b):
@@ -135,25 +140,34 @@
 
 
 def block_grads(acts, cot, sums, *outs):
+    blocks = outs[0].shape[0]
     lanes = sums.shape[1]
     first = is_first((lanes, acts.shape[1]), 0)
-    for b in range(outs[0].shape[0]):
-        q = swapped(sums, b)
-        down, up = dot(q, rows_of(acts, b), TN), dot(q, rows_of(cot, b), TN)
-        g = jnp.where(first, down, SCALE * up).astype(BF16)
-        for i, out in enumerate(outs):
-            out[b] = g[i * 2 * GROUP:(i + 1) * 2 * GROUP]
-
-
-def outputs(sums, *refs):
+    for j in range(blocks // 2):
+        q = swapped(sums, j)
+        for at, b in ((0, j), (lanes // 2, j + blocks // 2)):
+            down, up = dot(q, rows_of(acts, b), TN), dot(q, rows_of(cot, b), TN)
+            g = jnp.where(first, down, SCALE * up).astype(BF16)
+            for i, out in enumerate(outs):
+                out[b] = g[at + i * 2 * GROUP:at + (i + 1) * 2 * GROUP]
+
+
+def outputs(sums_a, sums_b, *refs):
     pieces, out, grad = refs[:-2], refs[-2], refs[-1]
-    first = is_first((BLOCK, sums.shape[1]), 1)
-    for b in range(pieces[0].shape[0]):
-        q, w = swapped(sums, b), matrix(pieces, b)
-        zero = jnp.zeros_like(q)
-        at = slice(b * BLOCK, (b + 1) * BLOCK)
-        out[at, :] = (SCALE * dot(jnp.where(first, zero, q), w, NN)).astype(BF16)
-        grad[at, :] = dot(jnp.where(first, q, zero), w, NN).astype(BF16)
+    blocks = pieces[0].shape[0]
+    first = is_first((BLOCK, sums_a.shape[1]), 1)
+    zero = jnp.zeros((BLOCK, sums_a.shape[1]), BF16)
+    for j in range(blocks // 2):
+        qs = [swapped(sums, j) for sums in (sums_a, sums_b)]
+        for b in (j, j + blocks // 2):
+            up, down = 0, 0
+            for q, half in zip(qs, HALVES):
+                w = matrix(pieces[half], b, blocks)
+                up = up + dot(jnp.where(first, zero, q), w, NN)
+                down = down + dot(jnp.where(first, q, zero), w, NN)
+            at = slice(b * BLOCK, (b + 1) * BLOCK)
+            out[at, :] = (SCALE * up).astype(BF16)
+            grad[at, :] = down.astype(BF16)
 
 
 def sum_pieces(nz, table, where, *refs):
@@ -208,15 +222,17 @@
     pieces = [shift(w, step) for w, step in zip(wanted, STEPS)]
     ids = (where[0] * CORES + where[1]) * share + jnp.arange(share, dtype=jnp.int32)
     counts = jnp.sum((table[:, None] == ids[None, :]).astype(F32), axis=0) * BLOCK
-    pieces, counts = lax.optimization_barrier((pieces, counts))
-    sums = total(
-        call(
-            partial_sums, shape((tokens, 2 * rank), F32), (activations, cotangent, *pieces), [VMEM] * (2 + len(STEPS))
+    pieces[-1], counts = lax.optimization_barrier((pieces[-1], counts))
+    sums, gots = [], []
+    for half in HALVES:
+        some, steps = pieces[half], STEPS[half]
+        part = call(
+            partial_sums, shape((tokens // 2, 2 * rank), F32), (activations, cotangent, *some), [VMEM] * (2 + len(some))
         )
-    )
-    parts = call(block_grads, slots, (activations, cotangent, sums), [VMEM] * 3)
-    gots = [shift(g, -step) for g, step in zip(parts, STEPS)]
-    out, grad = call(outputs, (shape((tokens, width), BF16),) * 2, (sums, *pieces), [VMEM] * (1 + len(STEPS)))
+        sums.append(total(part))
+        parts = call(block_grads, slots[half], (activations, cotangent, sums[-1]), [VMEM] * 3)
+        gots += [shift(g, -step) for g, step in zip(parts, steps)]
+    out, grad = call(outputs, (shape((tokens, width), BF16),) * 2, (*sums, *pieces), [VMEM] * (2 + len(STEPS)))
     gots, out, grad = lax.optimization_barrier((gots, out, grad))
     keep, send = call(
         functools.partial(sum_pieces, nz), (shape((own,) + piece, F32), shape((own,) + piece, BF16)),

time: 200 us -> 214 us (1.070)
  blocking collectives: 110 us -> 83.1 us
  starting transfers between devices: 58.3 us -> 84.3 us
  waiting for transfers between devices: 16.8 us -> 22.5 us
  Pallas kernels: 11.2 us -> 16.6 us
  local copies, waits for them, and re-layouts: 1.82 us -> 4.95 us
    all_to_all x2 -> x0, blocking collectives: 30.1 us -> none  [the longest x1 18.3 us: total(): lax.all_to_all(part.reshape(nxy, rows, part.shape[1]), 'xy', 0, 0, tiled=...]
    all_to_all x0 -> x4, starting transfers between devices: none -> 25.1 us  [the longest x2 14.4 us: total(): return lax.all_to_all(spread, 'xy', 0, 0, tiled=True).reshape(part.shape)]
    all_to_all x0 -> x4, waiting for transfers between devices: none -> 10.9 us  [the longest x2 10.9 us: total(): return lax.all_to_all(spread, 'xy', 0, 0, tiled=True).reshape(part.shape)]
    pallas_call x9 -> x12, Pallas kernels: 11.2 us -> 16.6 us  [call(): pl.pallas_call(body, out_shape=outs, in_specs=in_specs, out_specs=jax.tre...]
    ppermute x14, waiting for transfers between devices: 13.1 us -> 7.85 us  [shift(): return lax.ppermute(x, ('z', 'core'), pairs)]
    all_to_all x2, blocking collectives: 79.8 us -> 83.1 us  [over_z(): return lax.all_to_all(x, 'z', 0, 0, tiled=True)]
    unnamed x10 -> x24, local copies, waits for them, and re-layouts: 1.82 us -> 4.95 us
  transfers between devices with their start and end apart: 16 -> 20, of which waited for: 5 -> 7; matrix products, arithmetic and copies ran while one was open for 0% -> 0% of each run, Pallas kernels for 2% -> 4%
where the time goes in v5:
time: 214 us; the launch traced here: 213 us
  starting transfers between devices  84.3 us (39%)
  blocking collectives  83.1 us (39%)
  waiting for transfers between devices  22.5 us (11%)
  Pallas kernels  16.6 us (8%)
  local copies, waits for them, and re-layouts  4.95 us (2%)
    all_to_all x2, blocking collectives, over_z(): return lax.all_to_all(x, 'z', 0, 0, tiled=True)  83.1 us
    ppermute x14, starting transfers between devices, shift(): return lax.ppermute(x, ('z', 'core'), pairs)  55.4 us
    pallas_call x12, Pallas kernels, call(): pl.pallas_call(body, out_shape=outs, in_specs=in_specs, out_specs=jax.tre...  16.6 us
    all_to_all x2, starting transfers between devices, total(): return lax.all_to_all(spread, 'xy', 0, 0, tiled=True).reshape(part.shape)  14.4 us
    all_to_all x2, waiting for transfers between devices, total(): return lax.all_to_all(spread, 'xy', 0, 0, tiled=True).reshape(part.shape)  10.9 us
    all_to_all x2, starting transfers between devices, total(): lax.all_to_all(part.reshape(nxy, rows, part.shape[1]), 'xy', 0, 0, tiled=...  10.6 us
    ppermute x14, waiting for transfers between devices, shift(): return lax.ppermute(x, ('z', 'core'), pairs)  7.85 us
    unnamed x24, local copies, waits for them, and re-layouts  4.95 us
  transfers between devices with their start and end apart: 20, of which 7 were waited for; matrix products, arithmetic and copies ran while one was open for 0% of the time, Pallas kernels for 4%

profile of v5, /device:TPU:32, one launch (start us, length us, event | category | flops | bytes accessed | tf_op | source)
XLA Modules:
  0.0 212.7 jit_solution(12968172793661219486)
XLA Ops:
  2.5 43.4 %all_to_all.30 = bf16[16,2,16,512]{3,2,1,0:T(8,128)(2,1)S(1)} all-to-all(bf16[16,2,16,512]{3,2,1,0:T(8,128)(2,1)S(1)} %shard_map.84), channel_id=1, replica_groups=mesh['z'=16,'core'=2,'xy'=16] {'z'}, dimensions={0} | all-to-all | bytes 1048576 | tf_op jit(solution)/shard_map/all_to_all | solution.py:201
  51.5 2.9 %shard_map.85 = (bf16[8,16,512]{2,1,0:T(8,128)(2,1)S(1)}, bf16[8,16,512]{2,1,0:T(8,128)(2,1)S(1)}, bf16[8,16,512]{2,1,0:T(8,128)(2,1)S(1)}, bf16[8,16,512]{2,1,0...) custom-call(s32[256]{0:T(256)S(1)} %copy-done.9, ...), custom_call_target="tpu_custom_call" | custom-call | tf_op jit(solution)/shard_map/pallas_call | solution.py:31
  54.4 5.9 %collective-permute-start.1 = (bf16[8,16,512]{2,1,0:T(8,128)(2,1)S(1)}, bf16[8,16,512]{2,1,0:T(8,128)(2,1)S(1)}, u32[]{:S(2)}, u32[]{:S(2)}) collective-permute-start(bf16[8,16,512]{2,1,0:T(8,128)(2,1)S(1)} %get-tuple-element.39), channel_id=1, source_target_pairs={{0,128},{16,400},{32,160},{48,432},{64,192},{80,464},{96,224},{112... | collective-permute-start | bytes 393224 | tf_op jit(solution)/shard_map/ppermute | solution.py:207
  60.4 2.9 %collective-permute-start.2 = (bf16[8,16,512]{2,1,0:T(8,128)(2,1)S(1)}, bf16[8,16,512]{2,1,0:T(8,128)(2,1)S(1)}, u32[]{:S(2)}, u32[]{:S(2)}) collective-permute-start(bf16[8,16,512]{2,1,0:T(8,128)(2,1)S(1)} %get-tuple-element.40), channel_id=1, source_target_pairs={{0,416},{16,112},{32,448},{48,144},{64,480},{80,176},{96,0},{112,2... | collective-permute-start | bytes 393224 | tf_op jit(solution)/shard_map/ppermute | solution.py:207
  63.4 5.9 %collective-permute-start.3 = (bf16[8,16,512]{2,1,0:T(8,128)(2,1)S(1)}, bf16[8,16,512]{2,1,0:T(8,128)(2,1)S(1)}, u32[]{:S(2)}, u32[]{:S(2)}) collective-permute-start(bf16[8,16,512]{2,1,0:T(8,128)(2,1)S(1)} %get-tuple-element.41), channel_id=1, source_target_pairs={{0,96},{16,432},{32,128},{48,464},{64,160},{80,496},{96,192},{112,... | collective-permute-start | bytes 393224 | tf_op jit(solution)/shard_map/ppermute | solution.py:207
  70.4 3.7 %collective-permute-done.2.refs_2_ = bf16[8,16,512]{2,1,0:T(8,128)(2,1)S(1)} collective-permute-done((bf16[8,16,512]{2,1,0:T(8,128)(2,1)S(1)}, bf16[8,16,512]{2,1,0:T(8,128)(2,1)S(1)}, u32[]{:S(2)}, u32[]{:S(2)}) %collective-permute-start.2) | collective-permute-done | bytes 131104 | tf_op jit(solution)/shard_map/ppermute | solution.py:207
  74.1 3.0 %collective-permute-done.3.refs_3_ = bf16[8,16,512]{2,1,0:T(8,128)(2,1)S(1)} collective-permute-done((bf16[8,16,512]{2,1,0:T(8,128)(2,1)S(1)}, bf16[8,16,512]{2,1,0:T(8,128)(2,1)S(1)}, u32[]{:S(2)}, u32[]{:S(2)}) %collective-permute-start.3) | collective-permute-done | bytes 131104 | tf_op jit(solution)/shard_map/ppermute | solution.py:207
  78.5 7.0 %all-to-all-start.1 = ((f32[16,32,128]{2,1,0:T(8,128)}), f32[16,32,128]{2,1,0:T(8,128)S(1)}, u32[]{:S(2)}, u32[]{:S(2)}) async-start(f32[16,32,128]{2,1,0:T(8,128)} %bitcast.4), calls=%async_computation.1 | async-start | bytes 524288 | tf_op jit(solution)/shard_map/all_to_all | solution.py:211
  85.8 4.7 %collective-permute-start.7 = (bf16[8,16,512]{2,1,0:T(8,128)(2,1)}, bf16[8,16,512]{2,1,0:T(8,128)(2,1)S(1)}, u32[]{:S(2)}, u32[]{:S(2)}) collective-permute-start(bf16[8,16,512]{2,1,0:T(8,128)(2,1)} %get-tuple-element.46), channel_id=1, source_target_pairs={{0,448},{16,80},{32,480},{48,112},{64,0},{80,144},{96,32},{112,176... | collective-permute-start | bytes 393224 | tf_op jit(solution)/shard_map/ppermute | solution.py:207
  92.5 2.3 %collective-permute-start.9 = (bf16[8,16,512]{2,1,0:T(8,128)(2,1)S(1)}, bf16[8,16,512]{2,1,0:T(8,128)(2,1)S(1)}, u32[]{:S(2)}, u32[]{:S(2)}) collective-permute-start(bf16[8,16,512]{2,1,0:T(8,128)(2,1)S(1)} %get-tuple-element.48), channel_id=1, source_target_pairs={{0,480},{16,48},{32,0},{48,80},{64,32},{80,112},{96,64},{112,144},... | collective-permute-start | bytes 393224 | tf_op jit(solution)/shard_map/ppermute | solution.py:207
  94.8 4.6 %collective-permute-start.10 = (bf16[8,16,512]{2,1,0:T(8,128)(2,1)}, bf16[8,16,512]{2,1,0:T(8,128)(2,1)S(1)}, u32[]{:S(2)}, u32[]{:S(2)}) collective-permute-start(bf16[8,16,512]{2,1,0:T(8,128)(2,1)} %copy-done.10), channel_id=1, source_target_pairs={{0,32},{16,496},{32,64},{48,16},{64,96},{80,48},{96,128},{112,80},... | collective-permute-start | bytes 393224 | tf_op jit(solution)/shard_map/ppermute | solution.py:207
  100.1 7.2 %all-to-all-start.2 = ((bf16[16,32,128]{2,1,0:T(8,128)(2,1)}), bf16[16,32,128]{2,1,0:T(8,128)(2,1)S(1)}, u32[]{:S(2)}, u32[]{:S(2)}) async-start(bf16[16,32,128]{2,1,0:T(8,128)(2,1)} %shard_map.87), calls=%async_computation.2 | async-start | bytes 262144 | tf_op jit(solution)/shard_map/all_to_all | solution.py:213
  108.8 6.4 %all-to-all-done.2 = bf16[16,32,128]{2,1,0:T(8,128)(2,1)S(1)} async-done(((bf16[16,32,128]{2,1,0:T(8,128)(2,1)}), bf16[16,32,128]{2,1,0:T(8,128)(2,1)S(1)}, u32[]{:S(2)}, u32[]{:S(2)}) %all-to-all-start.2) | async-done | bytes 131104 | tf_op jit(solution)/shard_map/all_to_all | solution.py:213
  115.2 3.6 %all-to-all-start.3 = ((f32[16,32,128]{2,1,0:T(8,128)}), f32[16,32,128]{2,1,0:T(8,128)S(1)}, u32[]{:S(2)}, u32[]{:S(2)}) async-start(f32[16,32,128]{2,1,0:T(8,128)} %bitcast.6), calls=%async_computation.3 | async-start | bytes 524288 | tf_op jit(solution)/shard_map/all_to_all | solution.py:211
  121.5 4.2 %collective-permute-start.4 = (bf16[8,16,512]{2,1,0:T(8,128)(2,1)}, bf16[8,16,512]{2,1,0:T(8,128)(2,1)}, u32[]{:S(2)}, u32[]{:S(2)}) collective-permute-start(bf16[8,16,512]{2,1,0:T(8,128)(2,1)} %get-tuple-element.43), channel_id=1, source_target_pairs={{0,384},{16,144},{32,416},{48,176},{64,448},{80,208},{96,480},{112... | collective-permute-start | bytes 393224 | tf_op jit(solution)/shard_map/ppermute | solution.py:207
  125.8 5.6 %collective-permute-start.5 = (bf16[8,16,512]{2,1,0:T(8,128)(2,1)}, bf16[8,16,512]{2,1,0:T(8,128)(2,1)}, u32[]{:S(2)}, u32[]{:S(2)}) collective-permute-start(bf16[8,16,512]{2,1,0:T(8,128)(2,1)} %get-tuple-element.44), channel_id=1, source_target_pairs={{0,96},{16,432},{32,128},{48,464},{64,160},{80,496},{96,192},{112,... | collective-permute-start | bytes 393224 | tf_op jit(solution)/shard_map/ppermute | solution.py:207
  132.1 7.2 %all-to-all-start.4 = ((bf16[16,32,128]{2,1,0:T(8,128)(2,1)}), bf16[16,32,128]{2,1,0:T(8,128)(2,1)S(1)}, u32[]{:S(2)}, u32[]{:S(2)}) async-start(bf16[16,32,128]{2,1,0:T(8,128)(2,1)} %copy-done.2), calls=%async_computation.4 | async-start | bytes 262144 | tf_op jit(solution)/shard_map/all_to_all | solution.py:213
  139.3 3.3 %collective-permute-start.6 = (bf16[8,16,512]{2,1,0:T(8,128)(2,1)}, bf16[8,16,512]{2,1,0:T(8,128)(2,1)S(1)}, u32[]{:S(2)}, u32[]{:S(2)}) collective-permute-start(bf16[8,16,512]{2,1,0:T(8,128)(2,1)} %copy-done.11), channel_id=1, source_target_pairs={{0,416},{16,112},{32,448},{48,144},{64,480},{80,176},{96,0},{112,2... | collective-permute-start | bytes 393224 | tf_op jit(solution)/shard_map/ppermute | solution.py:207
  142.6 4.6 %all-to-all-done.4 = bf16[16,32,128]{2,1,0:T(8,128)(2,1)S(1)} async-done(((bf16[16,32,128]{2,1,0:T(8,128)(2,1)}), bf16[16,32,128]{2,1,0:T(8,128)(2,1)S(1)}, u32[]{:S(2)}, u32[]{:S(2)}) %all-to-all-start.4) | async-done | bytes 131104 | tf_op jit(solution)/shard_map/all_to_all | solution.py:213
  148.6 3.9 %collective-permute-start.11 = (bf16[8,16,512]{2,1,0:T(8,128)(2,1)S(1)}, bf16[8,16,512]{2,1,0:T(8,128)(2,1)S(1)}, u32[]{:S(2)}, u32[]{:S(2)}) collective-permute-start(bf16[8,16,512]{2,1,0:T(8,128)(2,1)S(1)} %get-tuple-element.51), channel_id=1, source_target_pairs={{0,64},{16,464},{32,96},{48,496},{64,128},{80,16},{96,160},{112,48... | collective-permute-start | bytes 393224 | tf_op jit(solution)/shard_map/ppermute | solution.py:207
  152.5 4.1 %collective-permute-start.12 = (bf16[8,16,512]{2,1,0:T(8,128)(2,1)S(1)}, bf16[8,16,512]{2,1,0:T(8,128)(2,1)S(1)}, u32[]{:S(2)}, u32[]{:S(2)}) collective-permute-start(bf16[8,16,512]{2,1,0:T(8,128)(2,1)S(1)} %get-tuple-element.52), channel_id=1, source_target_pairs={{0,448},{16,80},{32,480},{48,112},{64,0},{80,144},{96,32},{112,176... | collective-permute-start | bytes 393224 | tf_op jit(solution)/shard_map/ppermute | solution.py:207
  158.5 4.1 %collective-permute-start.14 = (bf16[8,16,512]{2,1,0:T(8,128)(2,1)S(1)}, bf16[8,16,512]{2,1,0:T(8,128)(2,1)S(1)}, u32[]{:S(2)}, u32[]{:S(2)}) collective-permute-start(bf16[8,16,512]{2,1,0:T(8,128)(2,1)S(1)} %get-tuple-element.54), channel_id=1, source_target_pairs={{0,480},{16,48},{32,0},{48,80},{64,32},{80,112},{96,64},{112,144},... | collective-permute-start | bytes 393224 | tf_op jit(solution)/shard_map/ppermute | solution.py:207
  162.6 3.0 %shard_map.92 = (bf16[1024,512]{1,0:T(8,128)(2,1)}, bf16[1024,512]{1,0:T(8,128)(2,1)}) custom-call(bf16[512,128]{1,0:T(8,128)(2,1)S(1)} %bitcast.12, bf16[512,128]{1,0:T(8,128)(2,1)S(1)} %bitcast.14, bf16[8,16,512]{2,1,0:T(8,128)(2,1)S(1)} %get-tuple-element.38.refs_0_, bf16[8,16,512]{2,1,0:T(8,128)(2,1)S(1)} %collective-permute-done.1.refs_1_, ...), custom_call_target="tpu_custom_call" | custom-call | tf_op jit(solution)/shard_map/pallas_call | solution.py:31
  171.6 39.7 %all_to_all.31.owned = bf16[16,2,16,512]{3,2,1,0:T(8,128)(2,1)S(1)} all-to-all(bf16[16,2,16,512]{3,2,1,0:T(8,128)(2,1)S(1)} %shard_map.94), channel_id=1, replica_groups=mesh['z'=16,'core'=2,'xy'=16] {'z'}, dimensions={0} | all-to-all | bytes 1048576 | tf_op jit(solution)/shard_map/all_to_all | solution.py:201
  (58 shorter events, 28.4 us)
Async XLA Ops:
  2.4 48.0 %copy-start.9 = (s32[256]{0:T(256)S(1)}, s32[256]{0:T(256)}, u32[]{:S(2)}) copy-start(s32[256]{0:T(256)} %table.3) | copy-start | bytes 3076
  2.5 74.6 %copy-start = (bf16[1024,512]{1,0:T(8,128)(2,1)S(1)}, bf16[1024,512]{1,0:T(8,128)(2,1)}, u32[]{:S(2)}) copy-start(bf16[1024,512]{1,0:T(8,128)(2,1)} %acts.7) | copy-start | bytes 3145732
  2.5 74.6 %copy-start.1 = (bf16[1024,512]{1,0:T(8,128)(2,1)S(1)}, bf16[1024,512]{1,0:T(8,128)(2,1)}, u32[]{:S(2)}) copy-start(bf16[1024,512]{1,0:T(8,128)(2,1)} %cot.7) | copy-start | bytes 3145732
  45.9 3.8 %collective-permute-start = (bf16[32,16,512]{2,1,0:T(8,128)(2,1)S(1)}, bf16[32,16,512]{2,1,0:T(8,128)(2,1)S(1)}, u32[]{:S(2)}, u32[]{:S(2)}) collective-permute-start(bf16[32,16,512]{2,1,0:T(8,128)(2,1)S(1)} %bitcast.9), channel_id=1, source_target_pairs={{0,16},{16,0},{1,17},{17,1},{2,18},{18,2},{3,19},{19,3},{4,20},{20... | collective-permute-start | bytes 1572872 | tf_op jit(solution)/shard_map/ppermute | solution.py:218
  54.4 24.1 %copy-start.10 = (bf16[8,16,512]{2,1,0:T(8,128)(2,1)}, bf16[8,16,512]{2,1,0:T(8,128)(2,1)S(1)}, u32[]{:S(2)}) copy-start(bf16[8,16,512]{2,1,0:T(8,128)(2,1)S(1)} %get-tuple-element.49) | copy-start | bytes 393220
  54.4 15.9 %collective-permute-start.1 = (bf16[8,16,512]{2,1,0:T(8,128)(2,1)S(1)}, bf16[8,16,512]{2,1,0:T(8,128)(2,1)S(1)}, u32[]{:S(2)}, u32[]{:S(2)}) collective-permute-start(bf16[8,16,512]{2,1,0:T(8,128)(2,1)S(1)} %get-tuple-element.39), channel_id=1, source_target_pairs={{0,128},{16,400},{32,160},{48,432},{64,192},{80,464},{96,224},{112... | collective-permute-start | bytes 393224 | tf_op jit(solution)/shard_map/ppermute | solution.py:207
  60.4 13.7 %collective-permute-start.2 = (bf16[8,16,512]{2,1,0:T(8,128)(2,1)S(1)}, bf16[8,16,512]{2,1,0:T(8,128)(2,1)S(1)}, u32[]{:S(2)}, u32[]{:S(2)}) collective-permute-start(bf16[8,16,512]{2,1,0:T(8,128)(2,1)S(1)} %get-tuple-element.40), channel_id=1, source_target_pairs={{0,416},{16,112},{32,448},{48,144},{64,480},{80,176},{96,0},{112,2... | collective-permute-start | bytes 393224 | tf_op jit(solution)/shard_map/ppermute | solution.py:207
  63.4 13.7 %collective-permute-start.3 = (bf16[8,16,512]{2,1,0:T(8,128)(2,1)S(1)}, bf16[8,16,512]{2,1,0:T(8,128)(2,1)S(1)}, u32[]{:S(2)}, u32[]{:S(2)}) collective-permute-start(bf16[8,16,512]{2,1,0:T(8,128)(2,1)S(1)} %get-tuple-element.41), channel_id=1, source_target_pairs={{0,96},{16,432},{32,128},{48,464},{64,160},{80,496},{96,192},{112,... | collective-permute-start | bytes 393224 | tf_op jit(solution)/shard_map/ppermute | solution.py:207
  78.5 20.9 %all-to-all-start.1 = ((f32[16,32,128]{2,1,0:T(8,128)}), f32[16,32,128]{2,1,0:T(8,128)S(1)}, u32[]{:S(2)}, u32[]{:S(2)}) async-start(f32[16,32,128]{2,1,0:T(8,128)} %bitcast.4), calls=%async_computation.1 | async-start | bytes 524288 | tf_op jit(solution)/shard_map/all_to_all | solution.py:211
  85.8 21.6 %collective-permute-start.7 = (bf16[8,16,512]{2,1,0:T(8,128)(2,1)}, bf16[8,16,512]{2,1,0:T(8,128)(2,1)S(1)}, u32[]{:S(2)}, u32[]{:S(2)}) collective-permute-start(bf16[8,16,512]{2,1,0:T(8,128)(2,1)} %get-tuple-element.46), channel_id=1, source_target_pairs={{0,448},{16,80},{32,480},{48,112},{64,0},{80,144},{96,32},{112,176... | collective-permute-start | bytes 393224 | tf_op jit(solution)/shard_map/ppermute | solution.py:207
  90.5 16.9 %collective-permute-start.8 = (bf16[8,16,512]{2,1,0:T(8,128)(2,1)}, bf16[8,16,512]{2,1,0:T(8,128)(2,1)S(1)}, u32[]{:S(2)}, u32[]{:S(2)}) collective-permute-start(bf16[8,16,512]{2,1,0:T(8,128)(2,1)} %get-tuple-element.47), channel_id=1, source_target_pairs={{0,64},{16,464},{32,96},{48,496},{64,128},{80,16},{96,160},{112,48... | collective-permute-start | bytes 393224 | tf_op jit(solution)/shard_map/ppermute | solution.py:207
  92.5 14.9 %collective-permute-start.9 = (bf16[8,16,512]{2,1,0:T(8,128)(2,1)S(1)}, bf16[8,16,512]{2,1,0:T(8,128)(2,1)S(1)}, u32[]{:S(2)}, u32[]{:S(2)}) collective-permute-start(bf16[8,16,512]{2,1,0:T(8,128)(2,1)S(1)} %get-tuple-element.48), channel_id=1, source_target_pairs={{0,480},{16,48},{32,0},{48,80},{64,32},{80,112},{96,64},{112,144},... | collective-permute-start | bytes 393224 | tf_op jit(solution)/shard_map/ppermute | solution.py:207
  94.8 12.5 %collective-permute-start.10 = (bf16[8,16,512]{2,1,0:T(8,128)(2,1)}, bf16[8,16,512]{2,1,0:T(8,128)(2,1)S(1)}, u32[]{:S(2)}, u32[]{:S(2)}) collective-permute-start(bf16[8,16,512]{2,1,0:T(8,128)(2,1)} %copy-done.10), channel_id=1, source_target_pairs={{0,32},{16,496},{32,64},{48,16},{64,96},{80,48},{96,128},{112,80},... | collective-permute-start | bytes 393224 | tf_op jit(solution)/shard_map/ppermute | solution.py:207
  100.1 15.1 %all-to-all-start.2 = ((bf16[16,32,128]{2,1,0:T(8,128)(2,1)}), bf16[16,32,128]{2,1,0:T(8,128)(2,1)S(1)}, u32[]{:S(2)}, u32[]{:S(2)}) async-start(bf16[16,32,128]{2,1,0:T(8,128)(2,1)} %shard_map.87), calls=%async_computation.2 | async-start | bytes 262144 | tf_op jit(solution)/shard_map/all_to_all | solution.py:213
  115.2 16.2 %all-to-all-start.3 = ((f32[16,32,128]{2,1,0:T(8,128)}), f32[16,32,128]{2,1,0:T(8,128)S(1)}, u32[]{:S(2)}, u32[]{:S(2)}) async-start(f32[16,32,128]{2,1,0:T(8,128)} %bitcast.6), calls=%async_computation.3 | async-start | bytes 524288 | tf_op jit(solution)/shard_map/all_to_all | solution.py:211
  121.5 35.0 %collective-permute-start.4 = (bf16[8,16,512]{2,1,0:T(8,128)(2,1)}, bf16[8,16,512]{2,1,0:T(8,128)(2,1)}, u32[]{:S(2)}, u32[]{:S(2)}) collective-permute-start(bf16[8,16,512]{2,1,0:T(8,128)(2,1)} %get-tuple-element.43), channel_id=1, source_target_pairs={{0,384},{16,144},{32,416},{48,176},{64,448},{80,208},{96,480},{112... | collective-permute-start | bytes 393224 | tf_op jit(solution)/shard_map/ppermute | solution.py:207
  125.8 32.7 %collective-permute-start.5 = (bf16[8,16,512]{2,1,0:T(8,128)(2,1)}, bf16[8,16,512]{2,1,0:T(8,128)(2,1)}, u32[]{:S(2)}, u32[]{:S(2)}) collective-permute-start(bf16[8,16,512]{2,1,0:T(8,128)(2,1)} %get-tuple-element.44), channel_id=1, source_target_pairs={{0,96},{16,432},{32,128},{48,464},{64,160},{80,496},{96,192},{112,... | collective-permute-start | bytes 393224 | tf_op jit(solution)/shard_map/ppermute | solution.py:207
  132.1 15.1 %all-to-all-start.4 = ((bf16[16,32,128]{2,1,0:T(8,128)(2,1)}), bf16[16,32,128]{2,1,0:T(8,128)(2,1)S(1)}, u32[]{:S(2)}, u32[]{:S(2)}) async-start(bf16[16,32,128]{2,1,0:T(8,128)(2,1)} %copy-done.2), calls=%async_computation.4 | async-start | bytes 262144 | tf_op jit(solution)/shard_map/all_to_all | solution.py:213
  139.3 26.3 %collective-permute-start.6 = (bf16[8,16,512]{2,1,0:T(8,128)(2,1)}, bf16[8,16,512]{2,1,0:T(8,128)(2,1)S(1)}, u32[]{:S(2)}, u32[]{:S(2)}) collective-permute-start(bf16[8,16,512]{2,1,0:T(8,128)(2,1)} %copy-done.11), channel_id=1, source_target_pairs={{0,416},{16,112},{32,448},{48,144},{64,480},{80,176},{96,0},{112,2... | collective-permute-start | bytes 393224 | tf_op jit(solution)/shard_map/ppermute | solution.py:207
  148.6 17.0 %collective-permute-start.11 = (bf16[8,16,512]{2,1,0:T(8,128)(2,1)S(1)}, bf16[8,16,512]{2,1,0:T(8,128)(2,1)S(1)}, u32[]{:S(2)}, u32[]{:S(2)}) collective-permute-start(bf16[8,16,512]{2,1,0:T(8,128)(2,1)S(1)} %get-tuple-element.51), channel_id=1, source_target_pairs={{0,64},{16,464},{32,96},{48,496},{64,128},{80,16},{96,160},{112,48... | collective-permute-start | bytes 393224 | tf_op jit(solution)/shard_map/ppermute | solution.py:207
  152.5 13.1 %collective-permute-start.12 = (bf16[8,16,512]{2,1,0:T(8,128)(2,1)S(1)}, bf16[8,16,512]{2,1,0:T(8,128)(2,1)S(1)}, u32[]{:S(2)}, u32[]{:S(2)}) collective-permute-start(bf16[8,16,512]{2,1,0:T(8,128)(2,1)S(1)} %get-tuple-element.52), channel_id=1, source_target_pairs={{0,448},{16,80},{32,480},{48,112},{64,0},{80,144},{96,32},{112,176... | collective-permute-start | bytes 393224 | tf_op jit(solution)/shard_map/ppermute | solution.py:207
  156.6 9.1 %collective-permute-start.13 = (bf16[8,16,512]{2,1,0:T(8,128)(2,1)S(1)}, bf16[8,16,512]{2,1,0:T(8,128)(2,1)S(1)}, u32[]{:S(2)}, u32[]{:S(2)}) collective-permute-start(bf16[8,16,512]{2,1,0:T(8,128)(2,1)S(1)} %get-tuple-element.53), channel_id=1, source_target_pairs={{0,32},{16,496},{32,64},{48,16},{64,96},{80,48},{96,128},{112,80},... | collective-permute-start | bytes 393224 | tf_op jit(solution)/shard_map/ppermute | solution.py:207
  158.5 7.1 %collective-permute-start.14 = (bf16[8,16,512]{2,1,0:T(8,128)(2,1)S(1)}, bf16[8,16,512]{2,1,0:T(8,128)(2,1)S(1)}, u32[]{:S(2)}, u32[]{:S(2)}) collective-permute-start(bf16[8,16,512]{2,1,0:T(8,128)(2,1)S(1)} %get-tuple-element.54), channel_id=1, source_target_pairs={{0,480},{16,48},{32,0},{48,80},{64,32},{80,112},{96,64},{112,144},... | collective-permute-start | bytes 393224 | tf_op jit(solution)/shard_map/ppermute | solution.py:207
  167.7 3.8 %collective-permute-start.15 = (bf16[32,16,512]{2,1,0:T(8,128)(2,1)S(1)}, bf16[32,16,512]{2,1,0:T(8,128)(2,1)S(1)}, u32[]{:S(2)}, u32[]{:S(2)}) collective-permute-start(bf16[32,16,512]{2,1,0:T(8,128)(2,1)S(1)} %get-tuple-element.69), channel_id=1, source_target_pairs={{0,16},{16,0},{1,17},{17,1},{2,18},{18,2},{3,19},{19,3},{4,20},{20... | collective-permute-start | bytes 1572872 | tf_op jit(solution)/shard_map/ppermute | solution.py:241
  (8 other events, 16.3 us)

commit v6 on v4

--- a/solution.py
+++ b/solution.py
@@ -12,11 +12,12 @@
 CORES = 2
 COPIES = 2
 GROUP = 8
-STEPS = (0, 4, 1, -1, 2, -2, 3, -3)
+STEPS = (0, 4, -3, 3, -2, 2, -1, 1)
 F32, BF16 = jnp.float32, jnp.bfloat16
 
 VMEM = pl.BlockSpec(memory_space=pltpu.VMEM)
 SMEM = pl.BlockSpec(memory_space=pltpu.SMEM)
+HBM = pl.BlockSpec(memory_space=pltpu.HBM)
 NT = (((1,), (1,)), ((), ()))
 NN = (((1,), (0,)), ((), ()))
 TN = (((0,), (0,)), ((), ()))
@@ -47,7 +48,12 @@
     return owner % 2, (owner // 2) * 2 + adapter % 2
 
 
-def cut(down, up, out):
+def cut(down_hbm, up_hbm, out, down, up, sems):
+    copies = [pltpu.make_async_copy(down_hbm, down, sems.at[0]), pltpu.make_async_copy(up_hbm, up, sems.at[1])]
+    for copy in copies:
+        copy.start()
+    for copy in copies:
+        copy.wait()
     parts = out.shape[0] // COPIES
     for k in range(down.shape[0]):
         d, u = down[k].astype(F32), up[k].astype(F32)
@@ -126,20 +132,19 @@
         out[b * BLOCK:(b + 1) * BLOCK, :] = jnp.where(first, proj, SCALE * back)
 
 
-def swapped(sums, b):
-    lanes = sums.shape[1]
+def swap_matrix(lanes):
     row = lax.broadcasted_iota(jnp.int32, (lanes, lanes), 0)
     col = lax.broadcasted_iota(jnp.int32, (lanes, lanes), 1)
-    place = row == jnp.where(is_first((lanes, lanes), 1), col + GROUP, col - GROUP)
-    return dot(rows_of(sums, b), place.astype(BF16), NN).astype(BF16)
+    return (row == jnp.where(is_first((lanes, lanes), 1), col + GROUP, col - GROUP)).astype(BF16)
 
 
 def block_grads(acts, cot, sums, *outs):
     lanes = sums.shape[1]
     first = is_first((lanes, acts.shape[1]), 0)
+    place = swap_matrix(lanes)
     for b in range(outs[0].shape[0]):
-        q = swapped(sums, b)
-        down, up = dot(q, rows_of(acts, b), TN), dot(q, rows_of(cot, b), TN)
+        q = dot(place, rows_of(sums, b), NT).astype(BF16)
+        down, up = dot(q, rows_of(acts, b), NN), dot(q, rows_of(cot, b), NN)
         g = jnp.where(first, down, SCALE * up).astype(BF16)
         for i, out in enumerate(outs):
             out[b] = g[i * 2 * GROUP:(i + 1) * 2 * GROUP]
@@ -148,8 +153,9 @@
 def outputs(sums, *refs):
     pieces, out, grad = refs[:-2], refs[-2], refs[-1]
     first = is_first((BLOCK, sums.shape[1]), 1)
+    place = swap_matrix(sums.shape[1])
     for b in range(pieces[0].shape[0]):
-        q, w = swapped(sums, b), matrix(pieces, b)
+        q, w = dot(rows_of(sums, b), place, NN).astype(BF16), matrix(pieces, b)
         zero = jnp.zeros_like(q)
         at = slice(b * BLOCK, (b + 1) * BLOCK)
         out[at, :] = (SCALE * dot(jnp.where(first, zero, q), w, NN)).astype(BF16)
@@ -199,7 +205,8 @@
         return lax.all_to_all(spread, "xy", 0, 0, tiled=True).reshape(part.shape)
 
     down = jnp.swapaxes(adapter_down_weights, 1, 2)
-    spread = call(cut, shape((nz, share) + piece, BF16), (down, adapter_up_weights), [VMEM] * 2)
+    both = [pltpu.VMEM(down.shape, BF16)] * 2 + [pltpu.SemaphoreType.DMA((2,))]
+    spread = call(cut, shape((nz, share) + piece, BF16), (down, adapter_up_weights), [HBM] * 2, both)
     held = over_z(spread).reshape(own, *piece)
     held_other = lax.ppermute(held, "core", swap)
     wanted = call(

time: 200 us -> 194 us (0.970)
  waiting for transfers between devices: 16.8 us -> 8.38 us
  starting transfers between devices: 58.3 us -> 61.6 us
    ppermute x14, waiting for transfers between devices: 13.1 us -> 4.72 us  [shift(): return lax.ppermute(x, ('z', 'core'), pairs)]
    ppermute x14, starting transfers between devices: 54.5 us -> 57.8 us  [shift(): return lax.ppermute(x, ('z', 'core'), pairs)]
  transfers between devices with their start and end apart: 16 -> 16, of which waited for: 5 -> 4; matrix products, arithmetic and copies ran while one was open for 0% -> 0% of each run, Pallas kernels for 2% -> 2%
where the time goes in v6:
time: 194 us
  blocking collectives  109 us (56%)
  starting transfers between devices  61.6 us (32%)
  Pallas kernels  11.2 us (6%)
  waiting for transfers between devices  8.38 us (4%)
    all_to_all x2, blocking collectives, over_z(): return lax.all_to_all(x, 'z', 0, 0, tiled=True)  80.6 us
    ppermute x14, starting transfers between devices, shift(): return lax.ppermute(x, ('z', 'core'), pairs)  57.8 us
    all_to_all x1, blocking collectives, total(): lax.all_to_all(part.reshape(nxy, rows, part.shape[1]), 'xy', 0, 0, tiled=...  16.9 us
    all_to_all x1, blocking collectives, total(): return lax.all_to_all(spread, 'xy', 0, 0, tiled=True).reshape(part.shape)  11.7 us
    pallas_call x9, Pallas kernels, call(): pl.pallas_call(body, out_shape=outs, in_specs=in_specs, out_specs=jax.tre...  11.2 us
    ppermute x14, waiting for transfers between devices, shift(): return lax.ppermute(x, ('z', 'core'), pairs)  4.72 us
  transfers between devices with their start and end apart: 16, of which 4 were waited for; matrix products, arithmetic and copies ran while one was open for 0% of the time, Pallas kernels for 2%

profile of v6, /device:TPU:32, one launch (start us, length us, event | category | flops | bytes accessed | tf_op | source)
XLA Modules:
  0.0 193.5 jit_solution(14591400355033460578)
XLA Ops:
  2.8 43.4 %all_to_all.20 = bf16[16,2,16,512]{3,2,1,0:T(8,128)(2,1)S(1)} all-to-all(bf16[16,2,16,512]{3,2,1,0:T(8,128)(2,1)S(1)} %shard_map.84), channel_id=1, replica_groups=mesh['z'=16,'core'=2,'xy'=16] {'z'}, dimensions={0} | all-to-all | bytes 1048576 | tf_op jit(solution)/shard_map/all_to_all | solution.py:193
  46.2 1.9 collective-permute-start
  50.0 2.2 %shard_map.85 = (bf16[8,16,512]{2,1,0:T(8,128)(2,1)S(1)}, bf16[8,16,512]{2,1,0:T(8,128)(2,1)S(1)}, bf16[8,16,512]{2,1,0:T(8,128)(2,1)S(1)}, bf16[8,16,512]{2,1,0...) custom-call(s32[256]{0:T(256)S(1)} %copy-done.4, ...), custom_call_target="tpu_custom_call" | custom-call | tf_op jit(solution)/shard_map/pallas_call | solution.py:31
  52.2 6.0 %collective-permute-start.1 = (bf16[8,16,512]{2,1,0:T(8,128)(2,1)S(1)}, bf16[8,16,512]{2,1,0:T(8,128)(2,1)S(1)}, u32[]{:S(2)}, u32[]{:S(2)}) collective-permute-start(bf16[8,16,512]{2,1,0:T(8,128)(2,1)S(1)} %get-tuple-element.46), channel_id=1, source_target_pairs={{0,128},{16,400},{32,160},{48,432},{64,192},{80,464},{96,224},{112... | collective-permute-start | bytes 393224 | tf_op jit(solution)/shard_map/ppermute | solution.py:199
  58.2 2.9 %collective-permute-start.2 = (bf16[8,16,512]{2,1,0:T(8,128)(2,1)S(1)}, bf16[8,16,512]{2,1,0:T(8,128)(2,1)S(1)}, u32[]{:S(2)}, u32[]{:S(2)}) collective-permute-start(bf16[8,16,512]{2,1,0:T(8,128)(2,1)S(1)} %get-tuple-element.47), channel_id=1, source_target_pairs={{0,416},{16,112},{32,448},{48,144},{64,480},{80,176},{96,0},{112,2... | collective-permute-start | bytes 393224 | tf_op jit(solution)/shard_map/ppermute | solution.py:199
  61.3 5.9 %collective-permute-start.3 = (bf16[8,16,512]{2,1,0:T(8,128)(2,1)S(1)}, bf16[8,16,512]{2,1,0:T(8,128)(2,1)S(1)}, u32[]{:S(2)}, u32[]{:S(2)}) collective-permute-start(bf16[8,16,512]{2,1,0:T(8,128)(2,1)S(1)} %get-tuple-element.48), channel_id=1, source_target_pairs={{0,96},{16,432},{32,128},{48,464},{64,160},{80,496},{96,192},{112,... | collective-permute-start | bytes 393224 | tf_op jit(solution)/shard_map/ppermute | solution.py:199
  67.2 3.9 %collective-permute-start.4 = (bf16[8,16,512]{2,1,0:T(8,128)(2,1)S(1)}, bf16[8,16,512]{2,1,0:T(8,128)(2,1)S(1)}, u32[]{:S(2)}, u32[]{:S(2)}) collective-permute-start(bf16[8,16,512]{2,1,0:T(8,128)(2,1)S(1)} %get-tuple-element.49), channel_id=1, source_target_pairs={{0,448},{16,80},{32,480},{48,112},{64,0},{80,144},{96,32},{112,176... | collective-permute-start | bytes 393224 | tf_op jit(solution)/shard_map/ppermute | solution.py:199
  71.2 2.8 %collective-permute-start.5 = (bf16[8,16,512]{2,1,0:T(8,128)(2,1)S(1)}, bf16[8,16,512]{2,1,0:T(8,128)(2,1)S(1)}, u32[]{:S(2)}, u32[]{:S(2)}) collective-permute-start(bf16[8,16,512]{2,1,0:T(8,128)(2,1)S(1)} %get-tuple-element.50), channel_id=1, source_target_pairs={{0,64},{16,464},{32,96},{48,496},{64,128},{80,16},{96,160},{112,48... | collective-permute-start | bytes 393224 | tf_op jit(solution)/shard_map/ppermute | solution.py:199
  74.0 1.9 collective-permute-start.6
  76.0 3.9 %collective-permute-start.7 = (bf16[8,16,512]{2,1,0:T(8,128)(2,1)S(1)}, bf16[8,16,512]{2,1,0:T(8,128)(2,1)S(1)}, u32[]{:S(2)}, u32[]{:S(2)}) collective-permute-start(bf16[8,16,512]{2,1,0:T(8,128)(2,1)S(1)} %get-tuple-element.52), channel_id=1, source_target_pairs={{0,32},{16,496},{32,64},{48,16},{64,96},{80,48},{96,128},{112,80},... | collective-permute-start | bytes 393224 | tf_op jit(solution)/shard_map/ppermute | solution.py:199
  79.9 2.4 %collective-permute-done.5.refs_5_ = bf16[8,16,512]{2,1,0:T(8,128)(2,1)S(1)} collective-permute-done((bf16[8,16,512]{2,1,0:T(8,128)(2,1)S(1)}, bf16[8,16,512]{2,1,0:T(8,128)(2,1)S(1)}, u32[]{:S(2)}, u32[]{:S(2)}) %collective-permute-start.5) | collective-permute-done | bytes 131104 | tf_op jit(solution)/shard_map/ppermute | solution.py:199
  82.3 2.3 %collective-permute-done.7.refs_7_ = bf16[8,16,512]{2,1,0:T(8,128)(2,1)S(1)} collective-permute-done((bf16[8,16,512]{2,1,0:T(8,128)(2,1)S(1)}, bf16[8,16,512]{2,1,0:T(8,128)(2,1)S(1)}, u32[]{:S(2)}, u32[]{:S(2)}) %collective-permute-start.7) | collective-permute-done | bytes 131104 | tf_op jit(solution)/shard_map/ppermute | solution.py:199
  85.3 16.9 %all_to_all.21.got = f32[16,64,128]{2,1,0:T(8,128)S(1)} all-to-all(f32[16,64,128]{2,1,0:T(8,128)S(1)} %bitcast.9), channel_id=1, replica_groups=mesh['z'=16,'core'=2,'xy'=16] {'xy'}, dimensions={0} | all-to-all | bytes 1048576 | tf_op jit(solution)/shard_map/all_to_all | solution.py:203
  102.3 11.7 %all_to_all.22 = bf16[16,64,128]{2,1,0:T(8,128)(2,1)S(1)} all-to-all(bf16[16,64,128]{2,1,0:T(8,128)(2,1)S(1)} %shard_map.87), channel_id=1, replica_groups=mesh['z'=16,'core'=2,'xy'=16] {'xy'}, dimensions={0} | all-to-all | bytes 524288 | tf_op jit(solution)/shard_map/all_to_all | solution.py:205
  115.8 6.5 %collective-permute-start.8 = (bf16[8,16,512]{2,1,0:T(8,128)(2,1)S(1)}, bf16[8,16,512]{2,1,0:T(8,128)(2,1)S(1)}, u32[]{:S(2)}, u32[]{:S(2)}) collective-permute-start(bf16[8,16,512]{2,1,0:T(8,128)(2,1)S(1)} %get-tuple-element.62), channel_id=1, source_target_pairs={{0,384},{16,144},{32,416},{48,176},{64,448},{80,208},{96,480},{112... | collective-permute-start | bytes 393224 | tf_op jit(solution)/shard_map/ppermute | solution.py:199
  122.3 5.0 %collective-permute-start.9 = (bf16[8,16,512]{2,1,0:T(8,128)(2,1)S(1)}, bf16[8,16,512]{2,1,0:T(8,128)(2,1)S(1)}, u32[]{:S(2)}, u32[]{:S(2)}) collective-permute-start(bf16[8,16,512]{2,1,0:T(8,128)(2,1)S(1)} %get-tuple-element.63), channel_id=1, source_target_pairs={{0,96},{16,432},{32,128},{48,464},{64,160},{80,496},{96,192},{112,... | collective-permute-start | bytes 393224 | tf_op jit(solution)/shard_map/ppermute | solution.py:199
  127.4 3.8 %collective-permute-start.10 = (bf16[8,16,512]{2,1,0:T(8,128)(2,1)S(1)}, bf16[8,16,512]{2,1,0:T(8,128)(2,1)S(1)}, u32[]{:S(2)}, u32[]{:S(2)}) collective-permute-start(bf16[8,16,512]{2,1,0:T(8,128)(2,1)S(1)} %get-tuple-element.64), channel_id=1, source_target_pairs={{0,416},{16,112},{32,448},{48,144},{64,480},{80,176},{96,0},{112,2... | collective-permute-start | bytes 393224 | tf_op jit(solution)/shard_map/ppermute | solution.py:199
  131.2 2.5 %collective-permute-start.11 = (bf16[8,16,512]{2,1,0:T(8,128)(2,1)S(1)}, bf16[8,16,512]{2,1,0:T(8,128)(2,1)S(1)}, u32[]{:S(2)}, u32[]{:S(2)}) collective-permute-start(bf16[8,16,512]{2,1,0:T(8,128)(2,1)S(1)} %get-tuple-element.65), channel_id=1, source_target_pairs={{0,64},{16,464},{32,96},{48,496},{64,128},{80,16},{96,160},{112,48... | collective-permute-start | bytes 393224 | tf_op jit(solution)/shard_map/ppermute | solution.py:199
  133.7 5.5 %collective-permute-start.12 = (bf16[8,16,512]{2,1,0:T(8,128)(2,1)S(1)}, bf16[8,16,512]{2,1,0:T(8,128)(2,1)S(1)}, u32[]{:S(2)}, u32[]{:S(2)}) collective-permute-start(bf16[8,16,512]{2,1,0:T(8,128)(2,1)S(1)} %get-tuple-element.66), channel_id=1, source_target_pairs={{0,448},{16,80},{32,480},{48,112},{64,0},{80,144},{96,32},{112,176... | collective-permute-start | bytes 393224 | tf_op jit(solution)/shard_map/ppermute | solution.py:199
  139.2 2.5 %collective-permute-start.13 = (bf16[8,16,512]{2,1,0:T(8,128)(2,1)S(1)}, bf16[8,16,512]{2,1,0:T(8,128)(2,1)S(1)}, u32[]{:S(2)}, u32[]{:S(2)}) collective-permute-start(bf16[8,16,512]{2,1,0:T(8,128)(2,1)S(1)} %get-tuple-element.67), channel_id=1, source_target_pairs={{0,32},{16,496},{32,64},{48,16},{64,96},{80,48},{96,128},{112,80},... | collective-permute-start | bytes 393224 | tf_op jit(solution)/shard_map/ppermute | solution.py:199
  141.7 4.6 %collective-permute-start.14 = (bf16[8,16,512]{2,1,0:T(8,128)(2,1)S(1)}, bf16[8,16,512]{2,1,0:T(8,128)(2,1)S(1)}, u32[]{:S(2)}, u32[]{:S(2)}) collective-permute-start(bf16[8,16,512]{2,1,0:T(8,128)(2,1)S(1)} %get-tuple-element.68), channel_id=1, source_target_pairs={{0,480},{16,48},{32,0},{48,80},{64,32},{80,112},{96,64},{112,144},... | collective-permute-start | bytes 393224 | tf_op jit(solution)/shard_map/ppermute | solution.py:199
  146.3 3.0 %shard_map.89 = (bf16[1024,512]{1,0:T(8,128)(2,1)}, bf16[1024,512]{1,0:T(8,128)(2,1)}) custom-call(bf16[1024,128]{1,0:T(8,128)(2,1)S(1)} %bitcast.8, bf16[8,16,512]{2,1,0:T(8,128)(2,1)S(1)} %get-tuple-element.53.refs_0_, bf16[8,16,512]{2,1,0:T(8,128)(2,1)S(1)} %collective-permute-done.1.refs_1_, bf16[8,16,512]{2,1,0:T(8,128)(2,1)S(1)} %collective-permute-done.2.refs_2_, ...), custom_call_target="tpu_custom_call" | custom-call | tf_op jit(solution)/shard_map/pallas_call | solution.py:31
  150.9 1.9 collective-permute-start.15
  154.9 37.3 %all_to_all.23.owned = bf16[16,2,16,512]{3,2,1,0:T(8,128)(2,1)S(1)} all-to-all(bf16[16,2,16,512]{3,2,1,0:T(8,128)(2,1)S(1)} %shard_map.91), channel_id=1, replica_groups=mesh['z'=16,'core'=2,'xy'=16] {'z'}, dimensions={0} | all-to-all | bytes 1048576 | tf_op jit(solution)/shard_map/all_to_all | solution.py:193
  (35 shorter events, 11.8 us)
Async XLA Ops:
  0.6 0.9 copy-start.2
  1.5 0.9 copy-start.3
  2.4 47.6 %copy-start.4 = (s32[256]{0:T(256)S(1)}, s32[256]{0:T(256)}, u32[]{:S(2)}) copy-start(s32[256]{0:T(256)} %table.3) | copy-start | bytes 3076
  2.8 81.8 %copy-start = (bf16[1024,512]{1,0:T(8,128)(2,1)S(1)}, bf16[1024,512]{1,0:T(8,128)(2,1)}, u32[]{:S(2)}) copy-start(bf16[1024,512]{1,0:T(8,128)(2,1)} %acts.3) | copy-start | bytes 3145732
  2.8 81.8 %copy-start.1 = (bf16[1024,512]{1,0:T(8,128)(2,1)S(1)}, bf16[1024,512]{1,0:T(8,128)(2,1)}, u32[]{:S(2)}) copy-start(bf16[1024,512]{1,0:T(8,128)(2,1)} %cot.3) | copy-start | bytes 3145732
  46.2 3.8 %collective-permute-start = (bf16[32,16,512]{2,1,0:T(8,128)(2,1)S(1)}, bf16[32,16,512]{2,1,0:T(8,128)(2,1)S(1)}, u32[]{:S(2)}, u32[]{:S(2)}) collective-permute-start(bf16[32,16,512]{2,1,0:T(8,128)(2,1)S(1)} %bitcast.10), channel_id=1, source_target_pairs={{0,16},{16,0},{1,17},{17,1},{2,18},{18,2},{3,19},{19,3},{4,20},{20... | collective-permute-start | bytes 1572872 | tf_op jit(solution)/shard_map/ppermute | solution.py:211
  52.2 21.8 %collective-permute-start.1 = (bf16[8,16,512]{2,1,0:T(8,128)(2,1)S(1)}, bf16[8,16,512]{2,1,0:T(8,128)(2,1)S(1)}, u32[]{:S(2)}, u32[]{:S(2)}) collective-permute-start(bf16[8,16,512]{2,1,0:T(8,128)(2,1)S(1)} %get-tuple-element.46), channel_id=1, source_target_pairs={{0,128},{16,400},{32,160},{48,432},{64,192},{80,464},{96,224},{112... | collective-permute-start | bytes 393224 | tf_op jit(solution)/shard_map/ppermute | solution.py:199
  58.2 17.8 %collective-permute-start.2 = (bf16[8,16,512]{2,1,0:T(8,128)(2,1)S(1)}, bf16[8,16,512]{2,1,0:T(8,128)(2,1)S(1)}, u32[]{:S(2)}, u32[]{:S(2)}) collective-permute-start(bf16[8,16,512]{2,1,0:T(8,128)(2,1)S(1)} %get-tuple-element.47), channel_id=1, source_target_pairs={{0,416},{16,112},{32,448},{48,144},{64,480},{80,176},{96,0},{112,2... | collective-permute-start | bytes 393224 | tf_op jit(solution)/shard_map/ppermute | solution.py:199
  61.3 18.6 %collective-permute-start.3 = (bf16[8,16,512]{2,1,0:T(8,128)(2,1)S(1)}, bf16[8,16,512]{2,1,0:T(8,128)(2,1)S(1)}, u32[]{:S(2)}, u32[]{:S(2)}) collective-permute-start(bf16[8,16,512]{2,1,0:T(8,128)(2,1)S(1)} %get-tuple-element.48), channel_id=1, source_target_pairs={{0,96},{16,432},{32,128},{48,464},{64,160},{80,496},{96,192},{112,... | collective-permute-start | bytes 393224 | tf_op jit(solution)/shard_map/ppermute | solution.py:199
  67.2 12.7 %collective-permute-start.4 = (bf16[8,16,512]{2,1,0:T(8,128)(2,1)S(1)}, bf16[8,16,512]{2,1,0:T(8,128)(2,1)S(1)}, u32[]{:S(2)}, u32[]{:S(2)}) collective-permute-start(bf16[8,16,512]{2,1,0:T(8,128)(2,1)S(1)} %get-tuple-element.49), channel_id=1, source_target_pairs={{0,448},{16,80},{32,480},{48,112},{64,0},{80,144},{96,32},{112,176... | collective-permute-start | bytes 393224 | tf_op jit(solution)/shard_map/ppermute | solution.py:199
  71.2 11.1 %collective-permute-start.5 = (bf16[8,16,512]{2,1,0:T(8,128)(2,1)S(1)}, bf16[8,16,512]{2,1,0:T(8,128)(2,1)S(1)}, u32[]{:S(2)}, u32[]{:S(2)}) collective-permute-start(bf16[8,16,512]{2,1,0:T(8,128)(2,1)S(1)} %get-tuple-element.50), channel_id=1, source_target_pairs={{0,64},{16,464},{32,96},{48,496},{64,128},{80,16},{96,160},{112,48... | collective-permute-start | bytes 393224 | tf_op jit(solution)/shard_map/ppermute | solution.py:199
  74.0 8.3 %collective-permute-start.6 = (bf16[8,16,512]{2,1,0:T(8,128)(2,1)S(1)}, bf16[8,16,512]{2,1,0:T(8,128)(2,1)S(1)}, u32[]{:S(2)}, u32[]{:S(2)}) collective-permute-start(bf16[8,16,512]{2,1,0:T(8,128)(2,1)S(1)} %get-tuple-element.51), channel_id=1, source_target_pairs={{0,480},{16,48},{32,0},{48,80},{64,32},{80,112},{96,64},{112,144},... | collective-permute-start | bytes 393224 | tf_op jit(solution)/shard_map/ppermute | solution.py:199
  76.0 8.6 %collective-permute-start.7 = (bf16[8,16,512]{2,1,0:T(8,128)(2,1)S(1)}, bf16[8,16,512]{2,1,0:T(8,128)(2,1)S(1)}, u32[]{:S(2)}, u32[]{:S(2)}) collective-permute-start(bf16[8,16,512]{2,1,0:T(8,128)(2,1)S(1)} %get-tuple-element.52), channel_id=1, source_target_pairs={{0,32},{16,496},{32,64},{48,16},{64,96},{80,48},{96,128},{112,80},... | collective-permute-start | bytes 393224 | tf_op jit(solution)/shard_map/ppermute | solution.py:199
  115.8 23.4 %collective-permute-start.8 = (bf16[8,16,512]{2,1,0:T(8,128)(2,1)S(1)}, bf16[8,16,512]{2,1,0:T(8,128)(2,1)S(1)}, u32[]{:S(2)}, u32[]{:S(2)}) collective-permute-start(bf16[8,16,512]{2,1,0:T(8,128)(2,1)S(1)} %get-tuple-element.62), channel_id=1, source_target_pairs={{0,384},{16,144},{32,416},{48,176},{64,448},{80,208},{96,480},{112... | collective-permute-start | bytes 393224 | tf_op jit(solution)/shard_map/ppermute | solution.py:199
  122.3 19.3 %collective-permute-start.9 = (bf16[8,16,512]{2,1,0:T(8,128)(2,1)S(1)}, bf16[8,16,512]{2,1,0:T(8,128)(2,1)S(1)}, u32[]{:S(2)}, u32[]{:S(2)}) collective-permute-start(bf16[8,16,512]{2,1,0:T(8,128)(2,1)S(1)} %get-tuple-element.63), channel_id=1, source_target_pairs={{0,96},{16,432},{32,128},{48,464},{64,160},{80,496},{96,192},{112,... | collective-permute-start | bytes 393224 | tf_op jit(solution)/shard_map/ppermute | solution.py:199
  127.4 22.0 %collective-permute-start.10 = (bf16[8,16,512]{2,1,0:T(8,128)(2,1)S(1)}, bf16[8,16,512]{2,1,0:T(8,128)(2,1)S(1)}, u32[]{:S(2)}, u32[]{:S(2)}) collective-permute-start(bf16[8,16,512]{2,1,0:T(8,128)(2,1)S(1)} %get-tuple-element.64), channel_id=1, source_target_pairs={{0,416},{16,112},{32,448},{48,144},{64,480},{80,176},{96,0},{112,2... | collective-permute-start | bytes 393224 | tf_op jit(solution)/shard_map/ppermute | solution.py:199
  131.2 18.1 %collective-permute-start.11 = (bf16[8,16,512]{2,1,0:T(8,128)(2,1)S(1)}, bf16[8,16,512]{2,1,0:T(8,128)(2,1)S(1)}, u32[]{:S(2)}, u32[]{:S(2)}) collective-permute-start(bf16[8,16,512]{2,1,0:T(8,128)(2,1)S(1)} %get-tuple-element.65), channel_id=1, source_target_pairs={{0,64},{16,464},{32,96},{48,496},{64,128},{80,16},{96,160},{112,48... | collective-permute-start | bytes 393224 | tf_op jit(solution)/shard_map/ppermute | solution.py:199
  133.7 15.6 %collective-permute-start.12 = (bf16[8,16,512]{2,1,0:T(8,128)(2,1)S(1)}, bf16[8,16,512]{2,1,0:T(8,128)(2,1)S(1)}, u32[]{:S(2)}, u32[]{:S(2)}) collective-permute-start(bf16[8,16,512]{2,1,0:T(8,128)(2,1)S(1)} %get-tuple-element.66), channel_id=1, source_target_pairs={{0,448},{16,80},{32,480},{48,112},{64,0},{80,144},{96,32},{112,176... | collective-permute-start | bytes 393224 | tf_op jit(solution)/shard_map/ppermute | solution.py:199
  139.2 10.1 %collective-permute-start.13 = (bf16[8,16,512]{2,1,0:T(8,128)(2,1)S(1)}, bf16[8,16,512]{2,1,0:T(8,128)(2,1)S(1)}, u32[]{:S(2)}, u32[]{:S(2)}) collective-permute-start(bf16[8,16,512]{2,1,0:T(8,128)(2,1)S(1)} %get-tuple-element.67), channel_id=1, source_target_pairs={{0,32},{16,496},{32,64},{48,16},{64,96},{80,48},{96,128},{112,80},... | collective-permute-start | bytes 393224 | tf_op jit(solution)/shard_map/ppermute | solution.py:199
  141.7 7.7 %collective-permute-start.14 = (bf16[8,16,512]{2,1,0:T(8,128)(2,1)S(1)}, bf16[8,16,512]{2,1,0:T(8,128)(2,1)S(1)}, u32[]{:S(2)}, u32[]{:S(2)}) collective-permute-start(bf16[8,16,512]{2,1,0:T(8,128)(2,1)S(1)} %get-tuple-element.68), channel_id=1, source_target_pairs={{0,480},{16,48},{32,0},{48,80},{64,32},{80,112},{96,64},{112,144},... | collective-permute-start | bytes 393224 | tf_op jit(solution)/shard_map/ppermute | solution.py:199
  150.9 3.8 %collective-permute-start.15 = (bf16[32,16,512]{2,1,0:T(8,128)(2,1)S(1)}, bf16[32,16,512]{2,1,0:T(8,128)(2,1)S(1)}, u32[]{:S(2)}, u32[]{:S(2)}) collective-permute-start(bf16[32,16,512]{2,1,0:T(8,128)(2,1)S(1)} %get-tuple-element.83), channel_id=1, source_target_pairs={{0,16},{16,0},{1,17},{17,1},{2,18},{18,2},{3,19},{19,3},{4,20},{20... | collective-permute-start | bytes 1572872 | tf_op jit(solution)/shard_map/ppermute | solution.py:232

commit v7 on v6

--- a/solution.py
+++ b/solution.py
@@ -27,14 +27,14 @@
     return lax.dot_general(a, b, dims, preferred_element_type=F32)
 
 
-def call(body, outs, ins, in_specs, scratch=()):
+def call(body, outs, ins, in_specs, scratch=(), room=40):
     return pl.pallas_call(
         body,
         out_shape=outs,
         in_specs=in_specs,
         out_specs=jax.tree.map(lambda _: VMEM, outs),
         scratch_shapes=list(scratch),
-        compiler_params=pltpu.CompilerParams(vmem_limit_bytes=40 * 2**20),
+        compiler_params=pltpu.CompilerParams(vmem_limit_bytes=room * 2**20),
     )(*ins)
 
 
@@ -162,20 +162,21 @@
         grad[at, :] = dot(jnp.where(first, q, zero), w, NN).astype(BF16)
 
 
-def sum_pieces(nz, table, where, *refs):
-    gots, (keep, send, acc) = refs[:-3], refs[-3:]
-    core = where[1]
-    half = keep.shape[0]
+def sum_pieces(nz, kept, table, where, *refs):
+    gots, (out, acc) = refs[:-2], refs[-2:]
+    core = where[1] if kept else 1 - where[1]
     blocks = gots[0].shape[0]
     acc[...] = jnp.zeros_like(acc)
     for step, got in zip(STEPS, gots):
         z = partner(where, nz, step)
         for b in range(blocks):
-            par, row = named(table, z, core, b, blocks)
-            at = par * half + row
-            acc[at] = acc[at] + got[b].astype(F32)
-    keep[...] = acc[pl.ds(core * half, half)]
-    send[...] = acc[pl.ds((1 - core) * half, half)].astype(BF16)
+            par, row = named(table, z, where[1], b, blocks)
+
+            @pl.when(par == core)
+            def _():
+                acc[row] = acc[row] + got[b].astype(F32)
+
+    out[...] = acc[...].astype(out.dtype)
 
 
 def local(activations, cotangent, adapter_down_weights, adapter_up_weights, table):
@@ -206,7 +207,7 @@
 
     down = jnp.swapaxes(adapter_down_weights, 1, 2)
     both = [pltpu.VMEM(down.shape, BF16)] * 2 + [pltpu.SemaphoreType.DMA((2,))]
-    spread = call(cut, shape((nz, share) + piece, BF16), (down, adapter_up_weights), [HBM] * 2, both)
+    spread = call(cut, shape((nz, share) + piece, BF16), (down, adapter_up_weights), [HBM] * 2, both, 60)
     held = over_z(spread).reshape(own, *piece)
     held_other = lax.ppermute(held, "core", swap)
     wanted = call(
@@ -223,15 +224,16 @@
     )
     parts = call(block_grads, slots, (activations, cotangent, sums), [VMEM] * 3)
     gots = [shift(g, -step) for g, step in zip(parts, STEPS)]
+    def summed(kept, kind):
+        return call(
+            functools.partial(sum_pieces, nz, kept), shape((own,) + piece, kind), (table, where, *gots),
+            [SMEM, SMEM] + [VMEM] * len(STEPS), [pltpu.VMEM((own,) + piece, F32)],
+        )
+
+    from_other = lax.ppermute(summed(False, BF16), "core", swap)
+    merged = call(add_other, shape((nz, share) + piece, BF16), (summed(True, F32), from_other), [VMEM] * 2)
+    owned = over_z(merged)
     out, grad = call(outputs, (shape((tokens, width), BF16),) * 2, (sums, *pieces), [VMEM] * (1 + len(STEPS)))
-    gots, out, grad = lax.optimization_barrier((gots, out, grad))
-    keep, send = call(
-        functools.partial(sum_pieces, nz), (shape((own,) + piece, F32), shape((own,) + piece, BF16)),
-        (table, where, *gots), [SMEM, SMEM] + [VMEM] * len(STEPS), [pltpu.VMEM((CORES * own,) + piece, F32)],
-    )
-    from_other = lax.ppermute(send, "core", swap)
-    merged = call(add_other, shape((nz, share) + piece, BF16), (keep, from_other), [VMEM] * 2)
-    owned = over_z(merged)
     down_grad, up_grad = call(means, (shape((share, rank, width), F32),) * 2, (counts, owned), [SMEM, VMEM])
     return out, grad, jnp.swapaxes(down_grad, 1, 2), up_grad
 

time: 194 us -> 197 us (1.015)
  blocking collectives: 109 us -> 72.2 us
  waiting for transfers between devices: 8.38 us -> 35.8 us
  starting transfers between devices: 61.6 us -> 70.3 us
  Pallas kernels: 11.2 us -> 16.5 us
    all_to_all x2 -> x1, blocking collectives: 80.6 us -> 43.6 us  [over_z(): return lax.all_to_all(x, 'z', 0, 0, tiled=True)]
    all_to_all x0 -> x1, waiting for transfers between devices: none -> 26.8 us  [over_z(): return lax.all_to_all(x, 'z', 0, 0, tiled=True)]
    all_to_all x0 -> x1, starting transfers between devices: none -> 8.66 us  [over_z(): return lax.all_to_all(x, 'z', 0, 0, tiled=True)]
    pallas_call x9 -> x10, Pallas kernels: 11.2 us -> 16.5 us  [call(): pl.pallas_call(body, out_shape=outs, in_specs=in_specs, out_specs=jax.tre...]
    ppermute x14, waiting for transfers between devices: 4.72 us -> 7.19 us  [shift(): return lax.ppermute(x, ('z', 'core'), pairs)]
  transfers between devices with their start and end apart: 16 -> 17, of which waited for: 4 -> 6; matrix products, arithmetic and copies ran while one was open for 0% -> 0% of each run, Pallas kernels for 2% -> 3%
where the time goes in v7:
time: 197 us; the launch traced here: 196 us
  blocking collectives  72.2 us (37%)
  starting transfers between devices  70.3 us (36%)
  waiting for transfers between devices  35.8 us (18%)
  Pallas kernels  16.5 us (8%)
    ppermute x14, starting transfers between devices, shift(): return lax.ppermute(x, ('z', 'core'), pairs)  57.8 us
    all_to_all x1, blocking collectives, over_z(): return lax.all_to_all(x, 'z', 0, 0, tiled=True)  43.6 us
    all_to_all x1, waiting for transfers between devices, over_z(): return lax.all_to_all(x, 'z', 0, 0, tiled=True)  26.8 us
    all_to_all x1, blocking collectives, total(): lax.all_to_all(part.reshape(nxy, rows, part.shape[1]), 'xy', 0, 0, tiled=...  16.9 us
    pallas_call x10, Pallas kernels, call(): pl.pallas_call(body, out_shape=outs, in_specs=in_specs, out_specs=jax.tre...  16.5 us
    all_to_all x1, blocking collectives, total(): return lax.all_to_all(spread, 'xy', 0, 0, tiled=True).reshape(part.shape)  11.7 us
    all_to_all x1, starting transfers between devices, over_z(): return lax.all_to_all(x, 'z', 0, 0, tiled=True)  8.66 us
    ppermute x14, waiting for transfers between devices, shift(): return lax.ppermute(x, ('z', 'core'), pairs)  7.19 us
  transfers between devices with their start and end apart: 17, of which 6 were waited for; matrix products, arithmetic and copies ran while one was open for 0% of the time, Pallas kernels for 3%

profile of v7, /device:TPU:32, one launch (start us, length us, event | category | flops | bytes accessed | tf_op | source)
XLA Modules:
  0.0 196.0 jit_solution(16169603447650145757)
XLA Ops:
  2.5 43.6 %all_to_all.20 = bf16[16,2,16,512]{3,2,1,0:T(8,128)(2,1)S(1)} all-to-all(bf16[16,2,16,512]{3,2,1,0:T(8,128)(2,1)} %shard_map.84), channel_id=1, replica_groups=mesh['z'=16,'core'=2,'xy'=16] {'z'}, dimensions={0} | all-to-all | bytes 1048576 | tf_op jit(solution)/shard_map/all_to_all | solution.py:194
  49.9 2.2 %shard_map.85 = (bf16[8,16,512]{2,1,0:T(8,128)(2,1)S(1)}, bf16[8,16,512]{2,1,0:T(8,128)(2,1)S(1)}, bf16[8,16,512]{2,1,0:T(8,128)(2,1)S(1)}, bf16[8,16,512]{2,1,0...) custom-call(s32[256]{0:T(256)S(1)} %copy-done.2, ...), custom_call_target="tpu_custom_call" | custom-call | tf_op jit(solution)/shard_map/pallas_call | solution.py:31
  52.1 6.0 %collective-permute-start.1 = (bf16[8,16,512]{2,1,0:T(8,128)(2,1)S(1)}, bf16[8,16,512]{2,1,0:T(8,128)(2,1)S(1)}, u32[]{:S(2)}, u32[]{:S(2)}) collective-permute-start(bf16[8,16,512]{2,1,0:T(8,128)(2,1)S(1)} %get-tuple-element.34), channel_id=1, source_target_pairs={{0,128},{16,400},{32,160},{48,432},{64,192},{80,464},{96,224},{112... | collective-permute-start | bytes 393224 | tf_op jit(solution)/shard_map/ppermute | solution.py:200
  58.0 2.9 %collective-permute-start.2 = (bf16[8,16,512]{2,1,0:T(8,128)(2,1)S(1)}, bf16[8,16,512]{2,1,0:T(8,128)(2,1)S(1)}, u32[]{:S(2)}, u32[]{:S(2)}) collective-permute-start(bf16[8,16,512]{2,1,0:T(8,128)(2,1)S(1)} %get-tuple-element.35), channel_id=1, source_target_pairs={{0,416},{16,112},{32,448},{48,144},{64,480},{80,176},{96,0},{112,2... | collective-permute-start | bytes 393224 | tf_op jit(solution)/shard_map/ppermute | solution.py:200
  61.2 5.9 %collective-permute-start.3 = (bf16[8,16,512]{2,1,0:T(8,128)(2,1)S(1)}, bf16[8,16,512]{2,1,0:T(8,128)(2,1)S(1)}, u32[]{:S(2)}, u32[]{:S(2)}) collective-permute-start(bf16[8,16,512]{2,1,0:T(8,128)(2,1)S(1)} %get-tuple-element.36), channel_id=1, source_target_pairs={{0,96},{16,432},{32,128},{48,464},{64,160},{80,496},{96,192},{112,... | collective-permute-start | bytes 393224 | tf_op jit(solution)/shard_map/ppermute | solution.py:200
  67.1 4.0 %collective-permute-start.4 = (bf16[8,16,512]{2,1,0:T(8,128)(2,1)S(1)}, bf16[8,16,512]{2,1,0:T(8,128)(2,1)S(1)}, u32[]{:S(2)}, u32[]{:S(2)}) collective-permute-start(bf16[8,16,512]{2,1,0:T(8,128)(2,1)S(1)} %get-tuple-element.37), channel_id=1, source_target_pairs={{0,448},{16,80},{32,480},{48,112},{64,0},{80,144},{96,32},{112,176... | collective-permute-start | bytes 393224 | tf_op jit(solution)/shard_map/ppermute | solution.py:200
  71.0 2.8 %collective-permute-start.5 = (bf16[8,16,512]{2,1,0:T(8,128)(2,1)S(1)}, bf16[8,16,512]{2,1,0:T(8,128)(2,1)S(1)}, u32[]{:S(2)}, u32[]{:S(2)}) collective-permute-start(bf16[8,16,512]{2,1,0:T(8,128)(2,1)S(1)} %get-tuple-element.38), channel_id=1, source_target_pairs={{0,64},{16,464},{32,96},{48,496},{64,128},{80,16},{96,160},{112,48... | collective-permute-start | bytes 393224 | tf_op jit(solution)/shard_map/ppermute | solution.py:200
  75.8 3.9 %collective-permute-start.7 = (bf16[8,16,512]{2,1,0:T(8,128)(2,1)S(1)}, bf16[8,16,512]{2,1,0:T(8,128)(2,1)S(1)}, u32[]{:S(2)}, u32[]{:S(2)}) collective-permute-start(bf16[8,16,512]{2,1,0:T(8,128)(2,1)S(1)} %get-tuple-element.40), channel_id=1, source_target_pairs={{0,32},{16,496},{32,64},{48,16},{64,96},{80,48},{96,128},{112,80},... | collective-permute-start | bytes 393224 | tf_op jit(solution)/shard_map/ppermute | solution.py:200
  79.8 2.4 %collective-permute-done.5.refs_5_ = bf16[8,16,512]{2,1,0:T(8,128)(2,1)S(1)} collective-permute-done((bf16[8,16,512]{2,1,0:T(8,128)(2,1)S(1)}, bf16[8,16,512]{2,1,0:T(8,128)(2,1)S(1)}, u32[]{:S(2)}, u32[]{:S(2)}) %collective-permute-start.5) | collective-permute-done | bytes 131104 | tf_op jit(solution)/shard_map/ppermute | solution.py:200
  82.1 2.3 %collective-permute-done.7.refs_7_ = bf16[8,16,512]{2,1,0:T(8,128)(2,1)S(1)} collective-permute-done((bf16[8,16,512]{2,1,0:T(8,128)(2,1)S(1)}, bf16[8,16,512]{2,1,0:T(8,128)(2,1)S(1)}, u32[]{:S(2)}, u32[]{:S(2)}) %collective-permute-start.7) | collective-permute-done | bytes 131104 | tf_op jit(solution)/shard_map/ppermute | solution.py:200
  85.2 16.9 %all_to_all.21.got = f32[16,64,128]{2,1,0:T(8,128)S(1)} all-to-all(f32[16,64,128]{2,1,0:T(8,128)S(1)} %bitcast.9), channel_id=1, replica_groups=mesh['z'=16,'core'=2,'xy'=16] {'xy'}, dimensions={0} | all-to-all | bytes 1048576 | tf_op jit(solution)/shard_map/all_to_all | solution.py:204
  102.1 11.7 %all_to_all.22 = bf16[16,64,128]{2,1,0:T(8,128)(2,1)S(1)} all-to-all(bf16[16,64,128]{2,1,0:T(8,128)(2,1)S(1)} %shard_map.87), channel_id=1, replica_groups=mesh['z'=16,'core'=2,'xy'=16] {'xy'}, dimensions={0} | all-to-all | bytes 524288 | tf_op jit(solution)/shard_map/all_to_all | solution.py:206
  115.7 6.5 %collective-permute-start.8 = (bf16[8,16,512]{2,1,0:T(8,128)(2,1)S(1)}, bf16[8,16,512]{2,1,0:T(8,128)(2,1)S(1)}, u32[]{:S(2)}, u32[]{:S(2)}) collective-permute-start(bf16[8,16,512]{2,1,0:T(8,128)(2,1)S(1)} %get-tuple-element.53), channel_id=1, source_target_pairs={{0,384},{16,144},{32,416},{48,176},{64,448},{80,208},{96,480},{112... | collective-permute-start | bytes 393224 | tf_op jit(solution)/shard_map/ppermute | solution.py:200
  122.2 5.0 %collective-permute-start.9 = (bf16[8,16,512]{2,1,0:T(8,128)(2,1)S(1)}, bf16[8,16,512]{2,1,0:T(8,128)(2,1)S(1)}, u32[]{:S(2)}, u32[]{:S(2)}) collective-permute-start(bf16[8,16,512]{2,1,0:T(8,128)(2,1)S(1)} %get-tuple-element.54), channel_id=1, source_target_pairs={{0,96},{16,432},{32,128},{48,464},{64,160},{80,496},{96,192},{112,... | collective-permute-start | bytes 393224 | tf_op jit(solution)/shard_map/ppermute | solution.py:200
  127.2 3.9 %collective-permute-start.10 = (bf16[8,16,512]{2,1,0:T(8,128)(2,1)S(1)}, bf16[8,16,512]{2,1,0:T(8,128)(2,1)S(1)}, u32[]{:S(2)}, u32[]{:S(2)}) collective-permute-start(bf16[8,16,512]{2,1,0:T(8,128)(2,1)S(1)} %get-tuple-element.55), channel_id=1, source_target_pairs={{0,416},{16,112},{32,448},{48,144},{64,480},{80,176},{96,0},{112,2... | collective-permute-start | bytes 393224 | tf_op jit(solution)/shard_map/ppermute | solution.py:200
  131.1 2.5 %collective-permute-start.11 = (bf16[8,16,512]{2,1,0:T(8,128)(2,1)S(1)}, bf16[8,16,512]{2,1,0:T(8,128)(2,1)S(1)}, u32[]{:S(2)}, u32[]{:S(2)}) collective-permute-start(bf16[8,16,512]{2,1,0:T(8,128)(2,1)S(1)} %get-tuple-element.56), channel_id=1, source_target_pairs={{0,64},{16,464},{32,96},{48,496},{64,128},{80,16},{96,160},{112,48... | collective-permute-start | bytes 393224 | tf_op jit(solution)/shard_map/ppermute | solution.py:200
  133.6 5.5 %collective-permute-start.12 = (bf16[8,16,512]{2,1,0:T(8,128)(2,1)S(1)}, bf16[8,16,512]{2,1,0:T(8,128)(2,1)S(1)}, u32[]{:S(2)}, u32[]{:S(2)}) collective-permute-start(bf16[8,16,512]{2,1,0:T(8,128)(2,1)S(1)} %get-tuple-element.57), channel_id=1, source_target_pairs={{0,448},{16,80},{32,480},{48,112},{64,0},{80,144},{96,32},{112,176... | collective-permute-start | bytes 393224 | tf_op jit(solution)/shard_map/ppermute | solution.py:200
  139.0 2.5 %collective-permute-start.13 = (bf16[8,16,512]{2,1,0:T(8,128)(2,1)S(1)}, bf16[8,16,512]{2,1,0:T(8,128)(2,1)S(1)}, u32[]{:S(2)}, u32[]{:S(2)}) collective-permute-start(bf16[8,16,512]{2,1,0:T(8,128)(2,1)S(1)} %get-tuple-element.58), channel_id=1, source_target_pairs={{0,32},{16,496},{32,64},{48,16},{64,96},{80,48},{96,128},{112,80},... | collective-permute-start | bytes 393224 | tf_op jit(solution)/shard_map/ppermute | solution.py:200
  141.6 4.6 %collective-permute-start.14 = (bf16[8,16,512]{2,1,0:T(8,128)(2,1)S(1)}, bf16[8,16,512]{2,1,0:T(8,128)(2,1)S(1)}, u32[]{:S(2)}, u32[]{:S(2)}) collective-permute-start(bf16[8,16,512]{2,1,0:T(8,128)(2,1)S(1)} %get-tuple-element.59), channel_id=1, source_target_pairs={{0,480},{16,48},{32,0},{48,80},{64,32},{80,112},{96,64},{112,144},... | collective-permute-start | bytes 393224 | tf_op jit(solution)/shard_map/ppermute | solution.py:200
  148.6 2.3 %shard_map.91 = bf16[32,16,512]{2,1,0:T(8,128)(2,1)S(1)} custom-call(s32[256]{0:T(256)S(1)} %copy-done.2, s32[2]{0:T(128)S(1)} %pad_add_fusion.where, bf16[8,16,512]{2,1,0:T(8,128)(2,1)S(1)} %get-tuple-element.52.refs_0_, bf16[8,16,512]{2,1,0:T(8,128)(2,1)S(1)} %collective-permute-done.8.refs_1_, bf16[8,16,512]{2,1,0:T(8,128)(2,1)S(1)} %collective-permute-done.9.refs_2_, ...), custom_call_target="tpu_custom_call" | custom-call | tf_op jit(solution)/shard_map/pallas_call | solution.py:31
  152.9 2.3 %shard_map.90.keep = f32[32,16,512]{2,1,0:T(8,128)S(1)} custom-call(s32[256]{0:T(256)S(1)} %copy-done.2, s32[2]{0:T(128)S(1)} %pad_add_fusion.where, bf16[8,16,512]{2,1,0:T(8,128)(2,1)S(1)} %get-tuple-element.52.refs_0_, bf16[8,16,512]{2,1,0:T(8,128)(2,1)S(1)} %collective-permute-done.8.refs_1_, bf16[8,16,512]{2,1,0:T(8,128)(2,1)S(1)} %collective-permute-done.9.refs_2_, ...), custom_call_target="tpu_custom_call" | custom-call | tf_op jit(solution)/shard_map/pallas_call | solution.py:31
  156.1 8.7 %all-to-all-start.3 = ((bf16[16,2,16,512]{3,2,1,0:T(8,128)(2,1)}), bf16[16,2,16,512]{3,2,1,0:T(8,128)(2,1)S(1)}, u32[]{:S(2)}, u32[]{:S(2)}) async-start(bf16[16,2,16,512]{3,2,1,0:T(8,128)(2,1)} %shard_map.92), calls=%async_computation.3 | async-start | bytes 1048576 | tf_op jit(solution)/shard_map/all_to_all | solution.py:194
  164.7 3.0 %shard_map.88 = (bf16[1024,512]{1,0:T(8,128)(2,1)}, bf16[1024,512]{1,0:T(8,128)(2,1)}) custom-call(bf16[1024,128]{1,0:T(8,128)(2,1)S(1)} %bitcast.8, bf16[8,16,512]{2,1,0:T(8,128)(2,1)S(1)} %get-tuple-element.41.refs_0_, bf16[8,16,512]{2,1,0:T(8,128)(2,1)S(1)} %collective-permute-done.1.refs_1_, bf16[8,16,512]{2,1,0:T(8,128)(2,1)S(1)} %collective-permute-done.2.refs_2_, ...), custom_call_target="tpu_custom_call" | custom-call | tf_op jit(solution)/shard_map/pallas_call | solution.py:31
  167.8 26.8 %all-to-all-done.3.owned = bf16[16,2,16,512]{3,2,1,0:T(8,128)(2,1)S(1)} async-done(((bf16[16,2,16,512]{3,2,1,0:T(8,128)(2,1)}), bf16[16,2,16,512]{3,2,1,0:T(8,128)(2,1)S(1)}, u32[]{:S(2)}, u32[]{:S(2)}) %all-to-all-start.3) | async-done | bytes 524320 | tf_op jit(solution)/shard_map/all_to_all | solution.py:194
  (33 shorter events, 17.0 us)
Async XLA Ops:
  0.6 49.2 %copy-start.2 = (s32[256]{0:T(256)S(1)}, s32[256]{0:T(256)}, u32[]{:S(2)}) copy-start(s32[256]{0:T(256)} %table.5) | copy-start | bytes 3076
  2.5 82.0 %copy-start = (bf16[1024,512]{1,0:T(8,128)(2,1)S(1)}, bf16[1024,512]{1,0:T(8,128)(2,1)}, u32[]{:S(2)}) copy-start(bf16[1024,512]{1,0:T(8,128)(2,1)} %acts.3) | copy-start | bytes 3145732
  2.5 82.0 %copy-start.1 = (bf16[1024,512]{1,0:T(8,128)(2,1)S(1)}, bf16[1024,512]{1,0:T(8,128)(2,1)}, u32[]{:S(2)}) copy-start(bf16[1024,512]{1,0:T(8,128)(2,1)} %cot.3) | copy-start | bytes 3145732
  46.1 3.8 %collective-permute-start = (bf16[32,16,512]{2,1,0:T(8,128)(2,1)S(1)}, bf16[32,16,512]{2,1,0:T(8,128)(2,1)S(1)}, u32[]{:S(2)}, u32[]{:S(2)}) collective-permute-start(bf16[32,16,512]{2,1,0:T(8,128)(2,1)S(1)} %bitcast.10), channel_id=1, source_target_pairs={{0,16},{16,0},{1,17},{17,1},{2,18},{18,2},{3,19},{19,3},{4,20},{20... | collective-permute-start | bytes 1572872 | tf_op jit(solution)/shard_map/ppermute | solution.py:212
  52.1 21.8 %collective-permute-start.1 = (bf16[8,16,512]{2,1,0:T(8,128)(2,1)S(1)}, bf16[8,16,512]{2,1,0:T(8,128)(2,1)S(1)}, u32[]{:S(2)}, u32[]{:S(2)}) collective-permute-start(bf16[8,16,512]{2,1,0:T(8,128)(2,1)S(1)} %get-tuple-element.34), channel_id=1, source_target_pairs={{0,128},{16,400},{32,160},{48,432},{64,192},{80,464},{96,224},{112... | collective-permute-start | bytes 393224 | tf_op jit(solution)/shard_map/ppermute | solution.py:200
  58.0 17.8 %collective-permute-start.2 = (bf16[8,16,512]{2,1,0:T(8,128)(2,1)S(1)}, bf16[8,16,512]{2,1,0:T(8,128)(2,1)S(1)}, u32[]{:S(2)}, u32[]{:S(2)}) collective-permute-start(bf16[8,16,512]{2,1,0:T(8,128)(2,1)S(1)} %get-tuple-element.35), channel_id=1, source_target_pairs={{0,416},{16,112},{32,448},{48,144},{64,480},{80,176},{96,0},{112,2... | collective-permute-start | bytes 393224 | tf_op jit(solution)/shard_map/ppermute | solution.py:200
  61.2 18.6 %collective-permute-start.3 = (bf16[8,16,512]{2,1,0:T(8,128)(2,1)S(1)}, bf16[8,16,512]{2,1,0:T(8,128)(2,1)S(1)}, u32[]{:S(2)}, u32[]{:S(2)}) collective-permute-start(bf16[8,16,512]{2,1,0:T(8,128)(2,1)S(1)} %get-tuple-element.36), channel_id=1, source_target_pairs={{0,96},{16,432},{32,128},{48,464},{64,160},{80,496},{96,192},{112,... | collective-permute-start | bytes 393224 | tf_op jit(solution)/shard_map/ppermute | solution.py:200
  67.1 12.7 %collective-permute-start.4 = (bf16[8,16,512]{2,1,0:T(8,128)(2,1)S(1)}, bf16[8,16,512]{2,1,0:T(8,128)(2,1)S(1)}, u32[]{:S(2)}, u32[]{:S(2)}) collective-permute-start(bf16[8,16,512]{2,1,0:T(8,128)(2,1)S(1)} %get-tuple-element.37), channel_id=1, source_target_pairs={{0,448},{16,80},{32,480},{48,112},{64,0},{80,144},{96,32},{112,176... | collective-permute-start | bytes 393224 | tf_op jit(solution)/shard_map/ppermute | solution.py:200
  71.0 11.1 %collective-permute-start.5 = (bf16[8,16,512]{2,1,0:T(8,128)(2,1)S(1)}, bf16[8,16,512]{2,1,0:T(8,128)(2,1)S(1)}, u32[]{:S(2)}, u32[]{:S(2)}) collective-permute-start(bf16[8,16,512]{2,1,0:T(8,128)(2,1)S(1)} %get-tuple-element.38), channel_id=1, source_target_pairs={{0,64},{16,464},{32,96},{48,496},{64,128},{80,16},{96,160},{112,48... | collective-permute-start | bytes 393224 | tf_op jit(solution)/shard_map/ppermute | solution.py:200
  73.8 8.3 %collective-permute-start.6 = (bf16[8,16,512]{2,1,0:T(8,128)(2,1)S(1)}, bf16[8,16,512]{2,1,0:T(8,128)(2,1)S(1)}, u32[]{:S(2)}, u32[]{:S(2)}) collective-permute-start(bf16[8,16,512]{2,1,0:T(8,128)(2,1)S(1)} %get-tuple-element.39), channel_id=1, source_target_pairs={{0,480},{16,48},{32,0},{48,80},{64,32},{80,112},{96,64},{112,144},... | collective-permute-start | bytes 393224 | tf_op jit(solution)/shard_map/ppermute | solution.py:200
  75.8 8.7 %collective-permute-start.7 = (bf16[8,16,512]{2,1,0:T(8,128)(2,1)S(1)}, bf16[8,16,512]{2,1,0:T(8,128)(2,1)S(1)}, u32[]{:S(2)}, u32[]{:S(2)}) collective-permute-start(bf16[8,16,512]{2,1,0:T(8,128)(2,1)S(1)} %get-tuple-element.40), channel_id=1, source_target_pairs={{0,32},{16,496},{32,64},{48,16},{64,96},{80,48},{96,128},{112,80},... | collective-permute-start | bytes 393224 | tf_op jit(solution)/shard_map/ppermute | solution.py:200
  115.7 23.4 %collective-permute-start.8 = (bf16[8,16,512]{2,1,0:T(8,128)(2,1)S(1)}, bf16[8,16,512]{2,1,0:T(8,128)(2,1)S(1)}, u32[]{:S(2)}, u32[]{:S(2)}) collective-permute-start(bf16[8,16,512]{2,1,0:T(8,128)(2,1)S(1)} %get-tuple-element.53), channel_id=1, source_target_pairs={{0,384},{16,144},{32,416},{48,176},{64,448},{80,208},{96,480},{112... | collective-permute-start | bytes 393224 | tf_op jit(solution)/shard_map/ppermute | solution.py:200
  122.2 19.4 %collective-permute-start.9 = (bf16[8,16,512]{2,1,0:T(8,128)(2,1)S(1)}, bf16[8,16,512]{2,1,0:T(8,128)(2,1)S(1)}, u32[]{:S(2)}, u32[]{:S(2)}) collective-permute-start(bf16[8,16,512]{2,1,0:T(8,128)(2,1)S(1)} %get-tuple-element.54), channel_id=1, source_target_pairs={{0,96},{16,432},{32,128},{48,464},{64,160},{80,496},{96,192},{112,... | collective-permute-start | bytes 393224 | tf_op jit(solution)/shard_map/ppermute | solution.py:200
  127.2 19.0 %collective-permute-start.10 = (bf16[8,16,512]{2,1,0:T(8,128)(2,1)S(1)}, bf16[8,16,512]{2,1,0:T(8,128)(2,1)S(1)}, u32[]{:S(2)}, u32[]{:S(2)}) collective-permute-start(bf16[8,16,512]{2,1,0:T(8,128)(2,1)S(1)} %get-tuple-element.55), channel_id=1, source_target_pairs={{0,416},{16,112},{32,448},{48,144},{64,480},{80,176},{96,0},{112,2... | collective-permute-start | bytes 393224 | tf_op jit(solution)/shard_map/ppermute | solution.py:200
  131.1 15.1 %collective-permute-start.11 = (bf16[8,16,512]{2,1,0:T(8,128)(2,1)S(1)}, bf16[8,16,512]{2,1,0:T(8,128)(2,1)S(1)}, u32[]{:S(2)}, u32[]{:S(2)}) collective-permute-start(bf16[8,16,512]{2,1,0:T(8,128)(2,1)S(1)} %get-tuple-element.56), channel_id=1, source_target_pairs={{0,64},{16,464},{32,96},{48,496},{64,128},{80,16},{96,160},{112,48... | collective-permute-start | bytes 393224 | tf_op jit(solution)/shard_map/ppermute | solution.py:200
  133.6 12.6 %collective-permute-start.12 = (bf16[8,16,512]{2,1,0:T(8,128)(2,1)S(1)}, bf16[8,16,512]{2,1,0:T(8,128)(2,1)S(1)}, u32[]{:S(2)}, u32[]{:S(2)}) collective-permute-start(bf16[8,16,512]{2,1,0:T(8,128)(2,1)S(1)} %get-tuple-element.57), channel_id=1, source_target_pairs={{0,448},{16,80},{32,480},{48,112},{64,0},{80,144},{96,32},{112,176... | collective-permute-start | bytes 393224 | tf_op jit(solution)/shard_map/ppermute | solution.py:200
  139.0 8.1 %collective-permute-start.13 = (bf16[8,16,512]{2,1,0:T(8,128)(2,1)S(1)}, bf16[8,16,512]{2,1,0:T(8,128)(2,1)S(1)}, u32[]{:S(2)}, u32[]{:S(2)}) collective-permute-start(bf16[8,16,512]{2,1,0:T(8,128)(2,1)S(1)} %get-tuple-element.58), channel_id=1, source_target_pairs={{0,32},{16,496},{32,64},{48,16},{64,96},{80,48},{96,128},{112,80},... | collective-permute-start | bytes 393224 | tf_op jit(solution)/shard_map/ppermute | solution.py:200
  141.6 7.1 %collective-permute-start.14 = (bf16[8,16,512]{2,1,0:T(8,128)(2,1)S(1)}, bf16[8,16,512]{2,1,0:T(8,128)(2,1)S(1)}, u32[]{:S(2)}, u32[]{:S(2)}) collective-permute-start(bf16[8,16,512]{2,1,0:T(8,128)(2,1)S(1)} %get-tuple-element.59), channel_id=1, source_target_pairs={{0,480},{16,48},{32,0},{48,80},{64,32},{80,112},{96,64},{112,144},... | collective-permute-start | bytes 393224 | tf_op jit(solution)/shard_map/ppermute | solution.py:200
  150.9 4.2 %collective-permute-start.15 = (bf16[32,16,512]{2,1,0:T(8,128)(2,1)S(1)}, bf16[32,16,512]{2,1,0:T(8,128)(2,1)S(1)}, u32[]{:S(2)}, u32[]{:S(2)}) collective-permute-start(bf16[32,16,512]{2,1,0:T(8,128)(2,1)S(1)} %shard_map.91), channel_id=1, source_target_pairs={{0,16},{16,0},{1,17},{17,1},{2,18},{18,2},{3,19},{19,3},{4,20},{20... | collective-permute-start | bytes 1572872 | tf_op jit(solution)/shard_map/ppermute | solution.py:233
  156.1 38.5 %all-to-all-start.3 = ((bf16[16,2,16,512]{3,2,1,0:T(8,128)(2,1)}), bf16[16,2,16,512]{3,2,1,0:T(8,128)(2,1)S(1)}, u32[]{:S(2)}, u32[]{:S(2)}) async-start(bf16[16,2,16,512]{3,2,1,0:T(8,128)(2,1)} %shard_map.92), calls=%async_computation.3 | async-start | bytes 1048576 | tf_op jit(solution)/shard_map/all_to_all | solution.py:194

commit v8 on v6

--- a/solution.py
+++ b/solution.py
@@ -12,7 +12,8 @@
 CORES = 2
 COPIES = 2
 GROUP = 8
-STEPS = (0, 4, -3, 3, -2, 2, -1, 1)
+STEPS = (4, -3, 3, -2, 2, -1, 1, 0)
+FIRST, REST = slice(0, 2), slice(2, 8)
 F32, BF16 = jnp.float32, jnp.bfloat16
 
 VMEM = pl.BlockSpec(memory_space=pltpu.VMEM)
@@ -80,10 +81,10 @@
     return lax.rem(where[0] + (1 - 2 * where[1]) * step + nz, nz)
 
 
-def pick_pieces(nz, table, where, mine, other, *outs):
+def pick_pieces(nz, steps, table, where, mine, other, *outs):
     core = where[1]
     blocks = outs[0].shape[0]
-    for step, out in zip(STEPS, outs):
+    for step, out in zip(steps, outs):
         z = partner(where, nz, step)
         for b in range(blocks):
             par, row = named(table, z, core, b, blocks)
@@ -138,10 +139,10 @@
     return (row == jnp.where(is_first((lanes, lanes), 1), col + GROUP, col - GROUP)).astype(BF16)
 
 
-def block_grads(acts, cot, sums, *outs):
-    lanes = sums.shape[1]
-    first = is_first((lanes, acts.shape[1]), 0)
-    place = swap_matrix(lanes)
+def block_grads(start, acts, cot, sums, *outs):
+    rows = len(outs) * 2 * GROUP
+    first = is_first((rows, acts.shape[1]), 0)
+    place = swap_matrix(sums.shape[1])[start * 2 * GROUP:start * 2 * GROUP + rows]
     for b in range(outs[0].shape[0]):
         q = dot(place, rows_of(sums, b), NT).astype(BF16)
         down, up = dot(q, rows_of(acts, b), NN), dot(q, rows_of(cot, b), NN)
@@ -209,9 +210,14 @@
     spread = call(cut, shape((nz, share) + piece, BF16), (down, adapter_up_weights), [HBM] * 2, both)
     held = over_z(spread).reshape(own, *piece)
     held_other = lax.ppermute(held, "core", swap)
-    wanted = call(
-        functools.partial(pick_pieces, nz), slots, (table, where, held, held_other), [SMEM, SMEM, VMEM, VMEM]
-    )
+    wanted = [
+        w
+        for some in (FIRST, REST)
+        for w in call(
+            functools.partial(pick_pieces, nz, STEPS[some]), slots[some], (table, where, held, held_other),
+            [SMEM, SMEM, VMEM, VMEM],
+        )
+    ]
     pieces = [shift(w, step) for w, step in zip(wanted, STEPS)]
     ids = (where[0] * CORES + where[1]) * share + jnp.arange(share, dtype=jnp.int32)
     counts = jnp.sum((table[:, None] == ids[None, :]).astype(F32), axis=0) * BLOCK
@@ -221,7 +227,13 @@
             partial_sums, shape((tokens, 2 * rank), F32), (activations, cotangent, *pieces), [VMEM] * (2 + len(STEPS))
         )
     )
-    parts = call(block_grads, slots, (activations, cotangent, sums), [VMEM] * 3)
+    parts = [
+        g
+        for some in (FIRST, REST)
+        for g in call(
+            functools.partial(block_grads, some.start), slots[some], (activations, cotangent, sums), [VMEM] * 3
+        )
+    ]
     gots = [shift(g, -step) for g, step in zip(parts, STEPS)]
     out, grad = call(outputs, (shape((tokens, width), BF16),) * 2, (sums, *pieces), [VMEM] * (1 + len(STEPS)))
     gots, out, grad = lax.optimization_barrier((gots, out, grad))

time: 194 us -> 196 us (1.010)
    pallas_call x9 -> x11, Pallas kernels: 11.2 us -> 13.1 us  [call(): pl.pallas_call(body, out_shape=outs, in_specs=in_specs, out_specs=jax.tre...]
  transfers between devices with their start and end apart: 16 -> 16, of which waited for: 4 -> 4; matrix products, arithmetic and copies ran while one was open for 0% -> 0% of each run, Pallas kernels for 2% -> 3%
where the time goes in v8:
time: 196 us; the launch traced here: 195 us
  blocking collectives  109 us (56%)
  starting transfers between devices  61.6 us (31%)
  Pallas kernels  13.1 us (7%)
  waiting for transfers between devices  8.37 us (4%)
    all_to_all x2, blocking collectives, over_z(): return lax.all_to_all(x, 'z', 0, 0, tiled=True)  80.5 us
    ppermute x14, starting transfers between devices, shift(): return lax.ppermute(x, ('z', 'core'), pairs)  57.8 us
    all_to_all x1, blocking collectives, total(): lax.all_to_all(part.reshape(nxy, rows, part.shape[1]), 'xy', 0, 0, tiled=...  16.9 us
    pallas_call x11, Pallas kernels, call(): pl.pallas_call(body, out_shape=outs, in_specs=in_specs, out_specs=jax.tre...  13.1 us
    all_to_all x1, blocking collectives, total(): return lax.all_to_all(spread, 'xy', 0, 0, tiled=True).reshape(part.shape)  11.7 us
    ppermute x14, waiting for transfers between devices, shift(): return lax.ppermute(x, ('z', 'core'), pairs)  4.71 us
  transfers between devices with their start and end apart: 16, of which 4 were waited for; matrix products, arithmetic and copies ran while one was open for 0% of the time, Pallas kernels for 3%

profile of v8, /device:TPU:32, one launch (start us, length us, event | category | flops | bytes accessed | tf_op | source)
XLA Modules:
  0.0 195.2 jit_solution(2898644680185025658)
XLA Ops:
  2.8 43.2 %all_to_all.20 = bf16[16,2,16,512]{3,2,1,0:T(8,128)(2,1)S(1)} all-to-all(bf16[16,2,16,512]{3,2,1,0:T(8,128)(2,1)S(1)} %shard_map.84), channel_id=1, replica_groups=mesh['z'=16,'core'=2,'xy'=16] {'z'}, dimensions={0} | all-to-all | bytes 1048576 | tf_op jit(solution)/shard_map/all_to_all | solution.py:194
  46.0 1.9 collective-permute-start
  50.8 6.0 %collective-permute-start.1 = (bf16[8,16,512]{2,1,0:T(8,128)(2,1)S(1)}, bf16[8,16,512]{2,1,0:T(8,128)(2,1)S(1)}, u32[]{:S(2)}, u32[]{:S(2)}) collective-permute-start(bf16[8,16,512]{2,1,0:T(8,128)(2,1)S(1)} %get-tuple-element.45), channel_id=1, source_target_pairs={{0,128},{16,400},{32,160},{48,432},{64,192},{80,464},{96,224},{112... | collective-permute-start | bytes 393224 | tf_op jit(solution)/shard_map/ppermute | solution.py:200
  56.8 2.9 %collective-permute-start.2 = (bf16[8,16,512]{2,1,0:T(8,128)(2,1)S(1)}, bf16[8,16,512]{2,1,0:T(8,128)(2,1)S(1)}, u32[]{:S(2)}, u32[]{:S(2)}) collective-permute-start(bf16[8,16,512]{2,1,0:T(8,128)(2,1)S(1)} %get-tuple-element.46), channel_id=1, source_target_pairs={{0,416},{16,112},{32,448},{48,144},{64,480},{80,176},{96,0},{112,2... | collective-permute-start | bytes 393224 | tf_op jit(solution)/shard_map/ppermute | solution.py:200
  61.7 5.9 %collective-permute-start.3 = (bf16[8,16,512]{2,1,0:T(8,128)(2,1)S(1)}, bf16[8,16,512]{2,1,0:T(8,128)(2,1)S(1)}, u32[]{:S(2)}, u32[]{:S(2)}) collective-permute-start(bf16[8,16,512]{2,1,0:T(8,128)(2,1)S(1)} %get-tuple-element.47), channel_id=1, source_target_pairs={{0,96},{16,432},{32,128},{48,464},{64,160},{80,496},{96,192},{112,... | collective-permute-start | bytes 393224 | tf_op jit(solution)/shard_map/ppermute | solution.py:200
  67.6 3.9 %collective-permute-start.4 = (bf16[8,16,512]{2,1,0:T(8,128)(2,1)S(1)}, bf16[8,16,512]{2,1,0:T(8,128)(2,1)S(1)}, u32[]{:S(2)}, u32[]{:S(2)}) collective-permute-start(bf16[8,16,512]{2,1,0:T(8,128)(2,1)S(1)} %get-tuple-element.48), channel_id=1, source_target_pairs={{0,448},{16,80},{32,480},{48,112},{64,0},{80,144},{96,32},{112,176... | collective-permute-start | bytes 393224 | tf_op jit(solution)/shard_map/ppermute | solution.py:200
  71.6 2.8 %collective-permute-start.5 = (bf16[8,16,512]{2,1,0:T(8,128)(2,1)S(1)}, bf16[8,16,512]{2,1,0:T(8,128)(2,1)S(1)}, u32[]{:S(2)}, u32[]{:S(2)}) collective-permute-start(bf16[8,16,512]{2,1,0:T(8,128)(2,1)S(1)} %get-tuple-element.49), channel_id=1, source_target_pairs={{0,64},{16,464},{32,96},{48,496},{64,128},{80,16},{96,160},{112,48... | collective-permute-start | bytes 393224 | tf_op jit(solution)/shard_map/ppermute | solution.py:200
  74.4 1.9 collective-permute-start.6
  76.3 3.9 %collective-permute-start.7 = (bf16[8,16,512]{2,1,0:T(8,128)(2,1)S(1)}, bf16[8,16,512]{2,1,0:T(8,128)(2,1)S(1)}, u32[]{:S(2)}, u32[]{:S(2)}) collective-permute-start(bf16[8,16,512]{2,1,0:T(8,128)(2,1)S(1)} %get-tuple-element.51), channel_id=1, source_target_pairs={{0,32},{16,496},{32,64},{48,16},{64,96},{80,48},{96,128},{112,80},... | collective-permute-start | bytes 393224 | tf_op jit(solution)/shard_map/ppermute | solution.py:200
  80.3 2.4 %collective-permute-done.5.refs_4_ = bf16[8,16,512]{2,1,0:T(8,128)(2,1)S(1)} collective-permute-done((bf16[8,16,512]{2,1,0:T(8,128)(2,1)S(1)}, bf16[8,16,512]{2,1,0:T(8,128)(2,1)S(1)}, u32[]{:S(2)}, u32[]{:S(2)}) %collective-permute-start.5) | collective-permute-done | bytes 131104 | tf_op jit(solution)/shard_map/ppermute | solution.py:200
  82.7 2.3 %collective-permute-done.7.refs_6_ = bf16[8,16,512]{2,1,0:T(8,128)(2,1)S(1)} collective-permute-done((bf16[8,16,512]{2,1,0:T(8,128)(2,1)S(1)}, bf16[8,16,512]{2,1,0:T(8,128)(2,1)S(1)}, u32[]{:S(2)}, u32[]{:S(2)}) %collective-permute-start.7) | collective-permute-done | bytes 131104 | tf_op jit(solution)/shard_map/ppermute | solution.py:200
  85.7 16.9 %all_to_all.21.got = f32[16,64,128]{2,1,0:T(8,128)S(1)} all-to-all(f32[16,64,128]{2,1,0:T(8,128)S(1)} %bitcast.13), channel_id=1, replica_groups=mesh['z'=16,'core'=2,'xy'=16] {'xy'}, dimensions={0} | all-to-all | bytes 1048576 | tf_op jit(solution)/shard_map/all_to_all | solution.py:204
  102.7 11.7 %all_to_all.22 = bf16[16,64,128]{2,1,0:T(8,128)(2,1)S(1)} all-to-all(bf16[16,64,128]{2,1,0:T(8,128)(2,1)S(1)} %shard_map.88), channel_id=1, replica_groups=mesh['z'=16,'core'=2,'xy'=16] {'xy'}, dimensions={0} | all-to-all | bytes 524288 | tf_op jit(solution)/shard_map/all_to_all | solution.py:206
  115.8 6.5 %collective-permute-start.8 = (bf16[8,16,512]{2,1,0:T(8,128)(2,1)S(1)}, bf16[8,16,512]{2,1,0:T(8,128)(2,1)S(1)}, u32[]{:S(2)}, u32[]{:S(2)}) collective-permute-start(bf16[8,16,512]{2,1,0:T(8,128)(2,1)S(1)} %get-tuple-element.61), channel_id=1, source_target_pairs={{0,384},{16,144},{32,416},{48,176},{64,448},{80,208},{96,480},{112... | collective-permute-start | bytes 393224 | tf_op jit(solution)/shard_map/ppermute | solution.py:200
  122.4 5.0 %collective-permute-start.9 = (bf16[8,16,512]{2,1,0:T(8,128)(2,1)S(1)}, bf16[8,16,512]{2,1,0:T(8,128)(2,1)S(1)}, u32[]{:S(2)}, u32[]{:S(2)}) collective-permute-start(bf16[8,16,512]{2,1,0:T(8,128)(2,1)S(1)} %get-tuple-element.62), channel_id=1, source_target_pairs={{0,96},{16,432},{32,128},{48,464},{64,160},{80,496},{96,192},{112,... | collective-permute-start | bytes 393224 | tf_op jit(solution)/shard_map/ppermute | solution.py:200
  129.0 3.9 %collective-permute-start.10 = (bf16[8,16,512]{2,1,0:T(8,128)(2,1)S(1)}, bf16[8,16,512]{2,1,0:T(8,128)(2,1)S(1)}, u32[]{:S(2)}, u32[]{:S(2)}) collective-permute-start(bf16[8,16,512]{2,1,0:T(8,128)(2,1)S(1)} %get-tuple-element.63), channel_id=1, source_target_pairs={{0,416},{16,112},{32,448},{48,144},{64,480},{80,176},{96,0},{112,2... | collective-permute-start | bytes 393224 | tf_op jit(solution)/shard_map/ppermute | solution.py:200
  132.9 2.5 %collective-permute-start.11 = (bf16[8,16,512]{2,1,0:T(8,128)(2,1)S(1)}, bf16[8,16,512]{2,1,0:T(8,128)(2,1)S(1)}, u32[]{:S(2)}, u32[]{:S(2)}) collective-permute-start(bf16[8,16,512]{2,1,0:T(8,128)(2,1)S(1)} %get-tuple-element.64), channel_id=1, source_target_pairs={{0,64},{16,464},{32,96},{48,496},{64,128},{80,16},{96,160},{112,48... | collective-permute-start | bytes 393224 | tf_op jit(solution)/shard_map/ppermute | solution.py:200
  135.4 5.5 %collective-permute-start.12 = (bf16[8,16,512]{2,1,0:T(8,128)(2,1)S(1)}, bf16[8,16,512]{2,1,0:T(8,128)(2,1)S(1)}, u32[]{:S(2)}, u32[]{:S(2)}) collective-permute-start(bf16[8,16,512]{2,1,0:T(8,128)(2,1)S(1)} %get-tuple-element.65), channel_id=1, source_target_pairs={{0,448},{16,80},{32,480},{48,112},{64,0},{80,144},{96,32},{112,176... | collective-permute-start | bytes 393224 | tf_op jit(solution)/shard_map/ppermute | solution.py:200
  140.9 2.5 %collective-permute-start.13 = (bf16[8,16,512]{2,1,0:T(8,128)(2,1)S(1)}, bf16[8,16,512]{2,1,0:T(8,128)(2,1)S(1)}, u32[]{:S(2)}, u32[]{:S(2)}) collective-permute-start(bf16[8,16,512]{2,1,0:T(8,128)(2,1)S(1)} %get-tuple-element.66), channel_id=1, source_target_pairs={{0,32},{16,496},{32,64},{48,16},{64,96},{80,48},{96,128},{112,80},... | collective-permute-start | bytes 393224 | tf_op jit(solution)/shard_map/ppermute | solution.py:200
  143.4 4.6 %collective-permute-start.14 = (bf16[8,16,512]{2,1,0:T(8,128)(2,1)S(1)}, bf16[8,16,512]{2,1,0:T(8,128)(2,1)S(1)}, u32[]{:S(2)}, u32[]{:S(2)}) collective-permute-start(bf16[8,16,512]{2,1,0:T(8,128)(2,1)S(1)} %get-tuple-element.67), channel_id=1, source_target_pairs={{0,480},{16,48},{32,0},{48,80},{64,32},{80,112},{96,64},{112,144},... | collective-permute-start | bytes 393224 | tf_op jit(solution)/shard_map/ppermute | solution.py:200
  148.0 3.0 %shard_map.91 = (bf16[1024,512]{1,0:T(8,128)(2,1)}, bf16[1024,512]{1,0:T(8,128)(2,1)}) custom-call(bf16[1024,128]{1,0:T(8,128)(2,1)S(1)} %bitcast.12, bf16[8,16,512]{2,1,0:T(8,128)(2,1)S(1)} %collective-permute-done.1.refs_0_, bf16[8,16,512]{2,1,0:T(8,128)(2,1)S(1)} %collective-permute-done.2.refs_1_, ...), custom_call_target="tpu_custom_call" | custom-call | tf_op jit(solution)/shard_map/pallas_call | solution.py:32
  152.6 1.9 collective-permute-start.15
  154.6 1.9 collective-permute-done.15.other
  156.6 37.2 %all_to_all.23.owned = bf16[16,2,16,512]{3,2,1,0:T(8,128)(2,1)S(1)} all-to-all(bf16[16,2,16,512]{3,2,1,0:T(8,128)(2,1)S(1)} %shard_map.93), channel_id=1, replica_groups=mesh['z'=16,'core'=2,'xy'=16] {'z'}, dimensions={0} | all-to-all | bytes 1048576 | tf_op jit(solution)/shard_map/all_to_all | solution.py:194
  (37 shorter events, 13.9 us)
Async XLA Ops:
  0.6 0.9 copy-start.2
  1.5 0.9 copy-start.3
  46.0 3.8 %collective-permute-start = (bf16[32,16,512]{2,1,0:T(8,128)(2,1)S(1)}, bf16[32,16,512]{2,1,0:T(8,128)(2,1)S(1)}, u32[]{:S(2)}, u32[]{:S(2)}) collective-permute-start(bf16[32,16,512]{2,1,0:T(8,128)(2,1)S(1)} %bitcast.7), channel_id=1, source_target_pairs={{0,16},{16,0},{1,17},{17,1},{2,18},{18,2},{3,19},{19,3},{4,20},{20... | collective-permute-start | bytes 1572872 | tf_op jit(solution)/shard_map/ppermute | solution.py:212
  48.0 1.9 copy-start.4
  48.1 36.9 %copy-start = (bf16[1024,512]{1,0:T(8,128)(2,1)S(1)}, bf16[1024,512]{1,0:T(8,128)(2,1)}, u32[]{:S(2)}) copy-start(bf16[1024,512]{1,0:T(8,128)(2,1)} %acts.5) | copy-start | bytes 3145732
  48.1 36.9 %copy-start.1 = (bf16[1024,512]{1,0:T(8,128)(2,1)S(1)}, bf16[1024,512]{1,0:T(8,128)(2,1)}, u32[]{:S(2)}) copy-start(bf16[1024,512]{1,0:T(8,128)(2,1)} %cot.5) | copy-start | bytes 3145732
  50.8 23.6 %collective-permute-start.1 = (bf16[8,16,512]{2,1,0:T(8,128)(2,1)S(1)}, bf16[8,16,512]{2,1,0:T(8,128)(2,1)S(1)}, u32[]{:S(2)}, u32[]{:S(2)}) collective-permute-start(bf16[8,16,512]{2,1,0:T(8,128)(2,1)S(1)} %get-tuple-element.45), channel_id=1, source_target_pairs={{0,128},{16,400},{32,160},{48,432},{64,192},{80,464},{96,224},{112... | collective-permute-start | bytes 393224 | tf_op jit(solution)/shard_map/ppermute | solution.py:200
  56.8 19.5 %collective-permute-start.2 = (bf16[8,16,512]{2,1,0:T(8,128)(2,1)S(1)}, bf16[8,16,512]{2,1,0:T(8,128)(2,1)S(1)}, u32[]{:S(2)}, u32[]{:S(2)}) collective-permute-start(bf16[8,16,512]{2,1,0:T(8,128)(2,1)S(1)} %get-tuple-element.46), channel_id=1, source_target_pairs={{0,416},{16,112},{32,448},{48,144},{64,480},{80,176},{96,0},{112,2... | collective-permute-start | bytes 393224 | tf_op jit(solution)/shard_map/ppermute | solution.py:200
  61.7 18.6 %collective-permute-start.3 = (bf16[8,16,512]{2,1,0:T(8,128)(2,1)S(1)}, bf16[8,16,512]{2,1,0:T(8,128)(2,1)S(1)}, u32[]{:S(2)}, u32[]{:S(2)}) collective-permute-start(bf16[8,16,512]{2,1,0:T(8,128)(2,1)S(1)} %get-tuple-element.47), channel_id=1, source_target_pairs={{0,96},{16,432},{32,128},{48,464},{64,160},{80,496},{96,192},{112,... | collective-permute-start | bytes 393224 | tf_op jit(solution)/shard_map/ppermute | solution.py:200
  67.6 12.7 %collective-permute-start.4 = (bf16[8,16,512]{2,1,0:T(8,128)(2,1)S(1)}, bf16[8,16,512]{2,1,0:T(8,128)(2,1)S(1)}, u32[]{:S(2)}, u32[]{:S(2)}) collective-permute-start(bf16[8,16,512]{2,1,0:T(8,128)(2,1)S(1)} %get-tuple-element.48), channel_id=1, source_target_pairs={{0,448},{16,80},{32,480},{48,112},{64,0},{80,144},{96,32},{112,176... | collective-permute-start | bytes 393224 | tf_op jit(solution)/shard_map/ppermute | solution.py:200
  71.6 11.1 %collective-permute-start.5 = (bf16[8,16,512]{2,1,0:T(8,128)(2,1)S(1)}, bf16[8,16,512]{2,1,0:T(8,128)(2,1)S(1)}, u32[]{:S(2)}, u32[]{:S(2)}) collective-permute-start(bf16[8,16,512]{2,1,0:T(8,128)(2,1)S(1)} %get-tuple-element.49), channel_id=1, source_target_pairs={{0,64},{16,464},{32,96},{48,496},{64,128},{80,16},{96,160},{112,48... | collective-permute-start | bytes 393224 | tf_op jit(solution)/shard_map/ppermute | solution.py:200
  74.4 8.3 %collective-permute-start.6 = (bf16[8,16,512]{2,1,0:T(8,128)(2,1)S(1)}, bf16[8,16,512]{2,1,0:T(8,128)(2,1)S(1)}, u32[]{:S(2)}, u32[]{:S(2)}) collective-permute-start(bf16[8,16,512]{2,1,0:T(8,128)(2,1)S(1)} %get-tuple-element.50), channel_id=1, source_target_pairs={{0,480},{16,48},{32,0},{48,80},{64,32},{80,112},{96,64},{112,144},... | collective-permute-start | bytes 393224 | tf_op jit(solution)/shard_map/ppermute | solution.py:200
  76.3 8.6 %collective-permute-start.7 = (bf16[8,16,512]{2,1,0:T(8,128)(2,1)S(1)}, bf16[8,16,512]{2,1,0:T(8,128)(2,1)S(1)}, u32[]{:S(2)}, u32[]{:S(2)}) collective-permute-start(bf16[8,16,512]{2,1,0:T(8,128)(2,1)S(1)} %get-tuple-element.51), channel_id=1, source_target_pairs={{0,32},{16,496},{32,64},{48,16},{64,96},{80,48},{96,128},{112,80},... | collective-permute-start | bytes 393224 | tf_op jit(solution)/shard_map/ppermute | solution.py:200
  115.8 25.0 %collective-permute-start.8 = (bf16[8,16,512]{2,1,0:T(8,128)(2,1)S(1)}, bf16[8,16,512]{2,1,0:T(8,128)(2,1)S(1)}, u32[]{:S(2)}, u32[]{:S(2)}) collective-permute-start(bf16[8,16,512]{2,1,0:T(8,128)(2,1)S(1)} %get-tuple-element.61), channel_id=1, source_target_pairs={{0,384},{16,144},{32,416},{48,176},{64,448},{80,208},{96,480},{112... | collective-permute-start | bytes 393224 | tf_op jit(solution)/shard_map/ppermute | solution.py:200
  122.4 21.0 %collective-permute-start.9 = (bf16[8,16,512]{2,1,0:T(8,128)(2,1)S(1)}, bf16[8,16,512]{2,1,0:T(8,128)(2,1)S(1)}, u32[]{:S(2)}, u32[]{:S(2)}) collective-permute-start(bf16[8,16,512]{2,1,0:T(8,128)(2,1)S(1)} %get-tuple-element.62), channel_id=1, source_target_pairs={{0,96},{16,432},{32,128},{48,464},{64,160},{80,496},{96,192},{112,... | collective-permute-start | bytes 393224 | tf_op jit(solution)/shard_map/ppermute | solution.py:200
  129.0 22.0 %collective-permute-start.10 = (bf16[8,16,512]{2,1,0:T(8,128)(2,1)S(1)}, bf16[8,16,512]{2,1,0:T(8,128)(2,1)S(1)}, u32[]{:S(2)}, u32[]{:S(2)}) collective-permute-start(bf16[8,16,512]{2,1,0:T(8,128)(2,1)S(1)} %get-tuple-element.63), channel_id=1, source_target_pairs={{0,416},{16,112},{32,448},{48,144},{64,480},{80,176},{96,0},{112,2... | collective-permute-start | bytes 393224 | tf_op jit(solution)/shard_map/ppermute | solution.py:200
  132.9 18.1 %collective-permute-start.11 = (bf16[8,16,512]{2,1,0:T(8,128)(2,1)S(1)}, bf16[8,16,512]{2,1,0:T(8,128)(2,1)S(1)}, u32[]{:S(2)}, u32[]{:S(2)}) collective-permute-start(bf16[8,16,512]{2,1,0:T(8,128)(2,1)S(1)} %get-tuple-element.64), channel_id=1, source_target_pairs={{0,64},{16,464},{32,96},{48,496},{64,128},{80,16},{96,160},{112,48... | collective-permute-start | bytes 393224 | tf_op jit(solution)/shard_map/ppermute | solution.py:200
  135.4 15.6 %collective-permute-start.12 = (bf16[8,16,512]{2,1,0:T(8,128)(2,1)S(1)}, bf16[8,16,512]{2,1,0:T(8,128)(2,1)S(1)}, u32[]{:S(2)}, u32[]{:S(2)}) collective-permute-start(bf16[8,16,512]{2,1,0:T(8,128)(2,1)S(1)} %get-tuple-element.65), channel_id=1, source_target_pairs={{0,448},{16,80},{32,480},{48,112},{64,0},{80,144},{96,32},{112,176... | collective-permute-start | bytes 393224 | tf_op jit(solution)/shard_map/ppermute | solution.py:200
  140.9 10.1 %collective-permute-start.13 = (bf16[8,16,512]{2,1,0:T(8,128)(2,1)S(1)}, bf16[8,16,512]{2,1,0:T(8,128)(2,1)S(1)}, u32[]{:S(2)}, u32[]{:S(2)}) collective-permute-start(bf16[8,16,512]{2,1,0:T(8,128)(2,1)S(1)} %get-tuple-element.66), channel_id=1, source_target_pairs={{0,32},{16,496},{32,64},{48,16},{64,96},{80,48},{96,128},{112,80},... | collective-permute-start | bytes 393224 | tf_op jit(solution)/shard_map/ppermute | solution.py:200
  143.4 7.7 %collective-permute-start.14 = (bf16[8,16,512]{2,1,0:T(8,128)(2,1)S(1)}, bf16[8,16,512]{2,1,0:T(8,128)(2,1)S(1)}, u32[]{:S(2)}, u32[]{:S(2)}) collective-permute-start(bf16[8,16,512]{2,1,0:T(8,128)(2,1)S(1)} %get-tuple-element.67), channel_id=1, source_target_pairs={{0,480},{16,48},{32,0},{48,80},{64,32},{80,112},{96,64},{112,144},... | collective-permute-start | bytes 393224 | tf_op jit(solution)/shard_map/ppermute | solution.py:200
  152.6 3.8 %collective-permute-start.15 = (bf16[32,16,512]{2,1,0:T(8,128)(2,1)S(1)}, bf16[32,16,512]{2,1,0:T(8,128)(2,1)S(1)}, u32[]{:S(2)}, u32[]{:S(2)}) collective-permute-start(bf16[32,16,512]{2,1,0:T(8,128)(2,1)S(1)} %get-tuple-element.83), channel_id=1, source_target_pairs={{0,16},{16,0},{1,17},{17,1},{2,18},{18,2},{3,19},{19,3},{4,20},{20... | collective-permute-start | bytes 1572872 | tf_op jit(solution)/shard_map/ppermute | solution.py:244

commit v9 on v6

--- a/solution.py
+++ b/solution.py
@@ -98,9 +98,9 @@
 
 
 def sum_parts(got, out):
-    total = got[0]
+    total = got[0].astype(F32)
     for i in range(1, got.shape[0]):
-        total = total + got[i]
+        total = total + got[i].astype(F32)
     total = total.astype(BF16)
     for i in range(out.shape[0]):
         out[i] = total
@@ -129,7 +129,7 @@
     for b in range(pieces[0].shape[0]):
         w = matrix(pieces, b)
         proj, back = dot(rows_of(acts, b), w, NT), dot(rows_of(cot, b), w, NT)
-        out[b * BLOCK:(b + 1) * BLOCK, :] = jnp.where(first, proj, SCALE * back)
+        out[b * BLOCK:(b + 1) * BLOCK, :] = jnp.where(first, proj, SCALE * back).astype(BF16)
 
 
 def swap_matrix(lanes):
@@ -218,7 +218,7 @@
     pieces, counts = lax.optimization_barrier((pieces, counts))
     sums = total(
         call(
-            partial_sums, shape((tokens, 2 * rank), F32), (activations, cotangent, *pieces), [VMEM] * (2 + len(STEPS))
+            partial_sums, shape((tokens, 2 * rank), BF16), (activations, cotangent, *pieces), [VMEM] * (2 + len(STEPS))
         )
     )
     parts = call(block_grads, slots, (activations, cotangent, sums), [VMEM] * 3)

time: 194 us -> 193 us (level)
  no operation moved by 1% of the time
where the time goes in v9:
time: 193 us; the launch traced here: 192 us
  blocking collectives  108 us (56%)
  starting transfers between devices  61.6 us (32%)
  Pallas kernels  11.3 us (6%)
  waiting for transfers between devices  8.39 us (4%)
    all_to_all x2, blocking collectives, over_z(): return lax.all_to_all(x, 'z', 0, 0, tiled=True)  80.6 us
    ppermute x14, starting transfers between devices, shift(): return lax.ppermute(x, ('z', 'core'), pairs)  57.8 us
    all_to_all x1, blocking collectives, total(): lax.all_to_all(part.reshape(nxy, rows, part.shape[1]), 'xy', 0, 0, tiled=...  15.3 us
    all_to_all x1, blocking collectives, total(): return lax.all_to_all(spread, 'xy', 0, 0, tiled=True).reshape(part.shape)  11.9 us
    pallas_call x9, Pallas kernels, call(): pl.pallas_call(body, out_shape=outs, in_specs=in_specs, out_specs=jax.tre...  11.3 us
    ppermute x14, waiting for transfers between devices, shift(): return lax.ppermute(x, ('z', 'core'), pairs)  4.72 us
  transfers between devices with their start and end apart: 16, of which 4 were waited for; matrix products, arithmetic and copies ran while one was open for 0% of the time, Pallas kernels for 2%

profile of v9, /device:TPU:32, one launch (start us, length us, event | category | flops | bytes accessed | tf_op | source)
XLA Modules:
  0.0 192.1 jit_solution(9588478058912899167)
XLA Ops:
  2.8 43.4 %all_to_all.20 = bf16[16,2,16,512]{3,2,1,0:T(8,128)(2,1)S(1)} all-to-all(bf16[16,2,16,512]{3,2,1,0:T(8,128)(2,1)S(1)} %shard_map.84), channel_id=1, replica_groups=mesh['z'=16,'core'=2,'xy'=16] {'z'}, dimensions={0} | all-to-all | bytes 1048576 | tf_op jit(solution)/shard_map/all_to_all | solution.py:193
  46.2 1.9 collective-permute-start
  50.0 2.2 %shard_map.85 = (bf16[8,16,512]{2,1,0:T(8,128)(2,1)S(1)}, bf16[8,16,512]{2,1,0:T(8,128)(2,1)S(1)}, bf16[8,16,512]{2,1,0:T(8,128)(2,1)S(1)}, bf16[8,16,512]{2,1,0...) custom-call(s32[256]{0:T(256)S(1)} %copy-done.4, ...), custom_call_target="tpu_custom_call" | custom-call | tf_op jit(solution)/shard_map/pallas_call | solution.py:31
  52.2 6.0 %collective-permute-start.1 = (bf16[8,16,512]{2,1,0:T(8,128)(2,1)S(1)}, bf16[8,16,512]{2,1,0:T(8,128)(2,1)S(1)}, u32[]{:S(2)}, u32[]{:S(2)}) collective-permute-start(bf16[8,16,512]{2,1,0:T(8,128)(2,1)S(1)} %get-tuple-element.46), channel_id=1, source_target_pairs={{0,128},{16,400},{32,160},{48,432},{64,192},{80,464},{96,224},{112... | collective-permute-start | bytes 393224 | tf_op jit(solution)/shard_map/ppermute | solution.py:199
  58.2 2.9 %collective-permute-start.2 = (bf16[8,16,512]{2,1,0:T(8,128)(2,1)S(1)}, bf16[8,16,512]{2,1,0:T(8,128)(2,1)S(1)}, u32[]{:S(2)}, u32[]{:S(2)}) collective-permute-start(bf16[8,16,512]{2,1,0:T(8,128)(2,1)S(1)} %get-tuple-element.47), channel_id=1, source_target_pairs={{0,416},{16,112},{32,448},{48,144},{64,480},{80,176},{96,0},{112,2... | collective-permute-start | bytes 393224 | tf_op jit(solution)/shard_map/ppermute | solution.py:199
  61.3 5.9 %collective-permute-start.3 = (bf16[8,16,512]{2,1,0:T(8,128)(2,1)S(1)}, bf16[8,16,512]{2,1,0:T(8,128)(2,1)S(1)}, u32[]{:S(2)}, u32[]{:S(2)}) collective-permute-start(bf16[8,16,512]{2,1,0:T(8,128)(2,1)S(1)} %get-tuple-element.48), channel_id=1, source_target_pairs={{0,96},{16,432},{32,128},{48,464},{64,160},{80,496},{96,192},{112,... | collective-permute-start | bytes 393224 | tf_op jit(solution)/shard_map/ppermute | solution.py:199
  67.2 4.0 %collective-permute-start.4 = (bf16[8,16,512]{2,1,0:T(8,128)(2,1)S(1)}, bf16[8,16,512]{2,1,0:T(8,128)(2,1)S(1)}, u32[]{:S(2)}, u32[]{:S(2)}) collective-permute-start(bf16[8,16,512]{2,1,0:T(8,128)(2,1)S(1)} %get-tuple-element.49), channel_id=1, source_target_pairs={{0,448},{16,80},{32,480},{48,112},{64,0},{80,144},{96,32},{112,176... | collective-permute-start | bytes 393224 | tf_op jit(solution)/shard_map/ppermute | solution.py:199
  71.2 2.8 %collective-permute-start.5 = (bf16[8,16,512]{2,1,0:T(8,128)(2,1)S(1)}, bf16[8,16,512]{2,1,0:T(8,128)(2,1)S(1)}, u32[]{:S(2)}, u32[]{:S(2)}) collective-permute-start(bf16[8,16,512]{2,1,0:T(8,128)(2,1)S(1)} %get-tuple-element.50), channel_id=1, source_target_pairs={{0,64},{16,464},{32,96},{48,496},{64,128},{80,16},{96,160},{112,48... | collective-permute-start | bytes 393224 | tf_op jit(solution)/shard_map/ppermute | solution.py:199
  74.0 1.9 collective-permute-start.6
  76.0 3.9 %collective-permute-start.7 = (bf16[8,16,512]{2,1,0:T(8,128)(2,1)S(1)}, bf16[8,16,512]{2,1,0:T(8,128)(2,1)S(1)}, u32[]{:S(2)}, u32[]{:S(2)}) collective-permute-start(bf16[8,16,512]{2,1,0:T(8,128)(2,1)S(1)} %get-tuple-element.52), channel_id=1, source_target_pairs={{0,32},{16,496},{32,64},{48,16},{64,96},{80,48},{96,128},{112,80},... | collective-permute-start | bytes 393224 | tf_op jit(solution)/shard_map/ppermute | solution.py:199
  79.9 2.4 %collective-permute-done.5.refs_5_ = bf16[8,16,512]{2,1,0:T(8,128)(2,1)S(1)} collective-permute-done((bf16[8,16,512]{2,1,0:T(8,128)(2,1)S(1)}, bf16[8,16,512]{2,1,0:T(8,128)(2,1)S(1)}, u32[]{:S(2)}, u32[]{:S(2)}) %collective-permute-start.5) | collective-permute-done | bytes 131104 | tf_op jit(solution)/shard_map/ppermute | solution.py:199
  82.3 2.3 %collective-permute-done.7.refs_7_ = bf16[8,16,512]{2,1,0:T(8,128)(2,1)S(1)} collective-permute-done((bf16[8,16,512]{2,1,0:T(8,128)(2,1)S(1)}, bf16[8,16,512]{2,1,0:T(8,128)(2,1)S(1)}, u32[]{:S(2)}, u32[]{:S(2)}) %collective-permute-start.7) | collective-permute-done | bytes 131104 | tf_op jit(solution)/shard_map/ppermute | solution.py:199
  85.3 15.3 %all_to_all.21.got = bf16[16,64,128]{2,1,0:T(8,128)(2,1)S(1)} all-to-all(bf16[16,64,128]{2,1,0:T(8,128)(2,1)S(1)} %bitcast.11), channel_id=1, replica_groups=mesh['z'=16,'core'=2,'xy'=16] {'xy'}, dimensions={0} | all-to-all | bytes 524288 | tf_op jit(solution)/shard_map/all_to_all | solution.py:203
  100.7 11.9 %all_to_all.22 = bf16[16,64,128]{2,1,0:T(8,128)(2,1)S(1)} all-to-all(bf16[16,64,128]{2,1,0:T(8,128)(2,1)S(1)} %shard_map.87), channel_id=1, replica_groups=mesh['z'=16,'core'=2,'xy'=16] {'xy'}, dimensions={0} | all-to-all | bytes 524288 | tf_op jit(solution)/shard_map/all_to_all | solution.py:205
  114.4 6.5 %collective-permute-start.8 = (bf16[8,16,512]{2,1,0:T(8,128)(2,1)S(1)}, bf16[8,16,512]{2,1,0:T(8,128)(2,1)S(1)}, u32[]{:S(2)}, u32[]{:S(2)}) collective-permute-start(bf16[8,16,512]{2,1,0:T(8,128)(2,1)S(1)} %get-tuple-element.62), channel_id=1, source_target_pairs={{0,384},{16,144},{32,416},{48,176},{64,448},{80,208},{96,480},{112... | collective-permute-start | bytes 393224 | tf_op jit(solution)/shard_map/ppermute | solution.py:199
  121.0 5.0 %collective-permute-start.9 = (bf16[8,16,512]{2,1,0:T(8,128)(2,1)S(1)}, bf16[8,16,512]{2,1,0:T(8,128)(2,1)S(1)}, u32[]{:S(2)}, u32[]{:S(2)}) collective-permute-start(bf16[8,16,512]{2,1,0:T(8,128)(2,1)S(1)} %get-tuple-element.63), channel_id=1, source_target_pairs={{0,96},{16,432},{32,128},{48,464},{64,160},{80,496},{96,192},{112,... | collective-permute-start | bytes 393224 | tf_op jit(solution)/shard_map/ppermute | solution.py:199
  126.0 3.9 %collective-permute-start.10 = (bf16[8,16,512]{2,1,0:T(8,128)(2,1)S(1)}, bf16[8,16,512]{2,1,0:T(8,128)(2,1)S(1)}, u32[]{:S(2)}, u32[]{:S(2)}) collective-permute-start(bf16[8,16,512]{2,1,0:T(8,128)(2,1)S(1)} %get-tuple-element.64), channel_id=1, source_target_pairs={{0,416},{16,112},{32,448},{48,144},{64,480},{80,176},{96,0},{112,2... | collective-permute-start | bytes 393224 | tf_op jit(solution)/shard_map/ppermute | solution.py:199
  129.8 2.5 %collective-permute-start.11 = (bf16[8,16,512]{2,1,0:T(8,128)(2,1)S(1)}, bf16[8,16,512]{2,1,0:T(8,128)(2,1)S(1)}, u32[]{:S(2)}, u32[]{:S(2)}) collective-permute-start(bf16[8,16,512]{2,1,0:T(8,128)(2,1)S(1)} %get-tuple-element.65), channel_id=1, source_target_pairs={{0,64},{16,464},{32,96},{48,496},{64,128},{80,16},{96,160},{112,48... | collective-permute-start | bytes 393224 | tf_op jit(solution)/shard_map/ppermute | solution.py:199
  132.3 5.5 %collective-permute-start.12 = (bf16[8,16,512]{2,1,0:T(8,128)(2,1)S(1)}, bf16[8,16,512]{2,1,0:T(8,128)(2,1)S(1)}, u32[]{:S(2)}, u32[]{:S(2)}) collective-permute-start(bf16[8,16,512]{2,1,0:T(8,128)(2,1)S(1)} %get-tuple-element.66), channel_id=1, source_target_pairs={{0,448},{16,80},{32,480},{48,112},{64,0},{80,144},{96,32},{112,176... | collective-permute-start | bytes 393224 | tf_op jit(solution)/shard_map/ppermute | solution.py:199
  137.8 2.5 %collective-permute-start.13 = (bf16[8,16,512]{2,1,0:T(8,128)(2,1)S(1)}, bf16[8,16,512]{2,1,0:T(8,128)(2,1)S(1)}, u32[]{:S(2)}, u32[]{:S(2)}) collective-permute-start(bf16[8,16,512]{2,1,0:T(8,128)(2,1)S(1)} %get-tuple-element.67), channel_id=1, source_target_pairs={{0,32},{16,496},{32,64},{48,16},{64,96},{80,48},{96,128},{112,80},... | collective-permute-start | bytes 393224 | tf_op jit(solution)/shard_map/ppermute | solution.py:199
  140.3 4.6 %collective-permute-start.14 = (bf16[8,16,512]{2,1,0:T(8,128)(2,1)S(1)}, bf16[8,16,512]{2,1,0:T(8,128)(2,1)S(1)}, u32[]{:S(2)}, u32[]{:S(2)}) collective-permute-start(bf16[8,16,512]{2,1,0:T(8,128)(2,1)S(1)} %get-tuple-element.68), channel_id=1, source_target_pairs={{0,480},{16,48},{32,0},{48,80},{64,32},{80,112},{96,64},{112,144},... | collective-permute-start | bytes 393224 | tf_op jit(solution)/shard_map/ppermute | solution.py:199
  144.9 3.0 %shard_map.89 = (bf16[1024,512]{1,0:T(8,128)(2,1)}, bf16[1024,512]{1,0:T(8,128)(2,1)}) custom-call(bf16[1024,128]{1,0:T(8,128)(2,1)S(1)} %bitcast.8, bf16[8,16,512]{2,1,0:T(8,128)(2,1)S(1)} %get-tuple-element.53.refs_0_, bf16[8,16,512]{2,1,0:T(8,128)(2,1)S(1)} %collective-permute-done.1.refs_1_, bf16[8,16,512]{2,1,0:T(8,128)(2,1)S(1)} %collective-permute-done.2.refs_2_, ...), custom_call_target="tpu_custom_call" | custom-call | tf_op jit(solution)/shard_map/pallas_call | solution.py:31
  149.6 1.9 collective-permute-start.15
  153.5 37.2 %all_to_all.23.owned = bf16[16,2,16,512]{3,2,1,0:T(8,128)(2,1)S(1)} all-to-all(bf16[16,2,16,512]{3,2,1,0:T(8,128)(2,1)S(1)} %shard_map.91), channel_id=1, replica_groups=mesh['z'=16,'core'=2,'xy'=16] {'z'}, dimensions={0} | all-to-all | bytes 1048576 | tf_op jit(solution)/shard_map/all_to_all | solution.py:193
  (35 shorter events, 11.8 us)
Async XLA Ops:
  0.6 0.9 copy-start.2
  1.5 0.9 copy-start.3
  2.4 47.6 %copy-start.4 = (s32[256]{0:T(256)S(1)}, s32[256]{0:T(256)}, u32[]{:S(2)}) copy-start(s32[256]{0:T(256)} %table.3) | copy-start | bytes 3076
  2.8 81.8 %copy-start = (bf16[1024,512]{1,0:T(8,128)(2,1)S(1)}, bf16[1024,512]{1,0:T(8,128)(2,1)}, u32[]{:S(2)}) copy-start(bf16[1024,512]{1,0:T(8,128)(2,1)} %acts.3) | copy-start | bytes 3145732
  2.8 81.8 %copy-start.1 = (bf16[1024,512]{1,0:T(8,128)(2,1)S(1)}, bf16[1024,512]{1,0:T(8,128)(2,1)}, u32[]{:S(2)}) copy-start(bf16[1024,512]{1,0:T(8,128)(2,1)} %cot.3) | copy-start | bytes 3145732
  46.2 3.8 %collective-permute-start = (bf16[32,16,512]{2,1,0:T(8,128)(2,1)S(1)}, bf16[32,16,512]{2,1,0:T(8,128)(2,1)S(1)}, u32[]{:S(2)}, u32[]{:S(2)}) collective-permute-start(bf16[32,16,512]{2,1,0:T(8,128)(2,1)S(1)} %bitcast.9), channel_id=1, source_target_pairs={{0,16},{16,0},{1,17},{17,1},{2,18},{18,2},{3,19},{19,3},{4,20},{20... | collective-permute-start | bytes 1572872 | tf_op jit(solution)/shard_map/ppermute | solution.py:211
  52.2 21.8 %collective-permute-start.1 = (bf16[8,16,512]{2,1,0:T(8,128)(2,1)S(1)}, bf16[8,16,512]{2,1,0:T(8,128)(2,1)S(1)}, u32[]{:S(2)}, u32[]{:S(2)}) collective-permute-start(bf16[8,16,512]{2,1,0:T(8,128)(2,1)S(1)} %get-tuple-element.46), channel_id=1, source_target_pairs={{0,128},{16,400},{32,160},{48,432},{64,192},{80,464},{96,224},{112... | collective-permute-start | bytes 393224 | tf_op jit(solution)/shard_map/ppermute | solution.py:199
  58.2 17.8 %collective-permute-start.2 = (bf16[8,16,512]{2,1,0:T(8,128)(2,1)S(1)}, bf16[8,16,512]{2,1,0:T(8,128)(2,1)S(1)}, u32[]{:S(2)}, u32[]{:S(2)}) collective-permute-start(bf16[8,16,512]{2,1,0:T(8,128)(2,1)S(1)} %get-tuple-element.47), channel_id=1, source_target_pairs={{0,416},{16,112},{32,448},{48,144},{64,480},{80,176},{96,0},{112,2... | collective-permute-start | bytes 393224 | tf_op jit(solution)/shard_map/ppermute | solution.py:199
  61.3 18.6 %collective-permute-start.3 = (bf16[8,16,512]{2,1,0:T(8,128)(2,1)S(1)}, bf16[8,16,512]{2,1,0:T(8,128)(2,1)S(1)}, u32[]{:S(2)}, u32[]{:S(2)}) collective-permute-start(bf16[8,16,512]{2,1,0:T(8,128)(2,1)S(1)} %get-tuple-element.48), channel_id=1, source_target_pairs={{0,96},{16,432},{32,128},{48,464},{64,160},{80,496},{96,192},{112,... | collective-permute-start | bytes 393224 | tf_op jit(solution)/shard_map/ppermute | solution.py:199
  67.2 12.7 %collective-permute-start.4 = (bf16[8,16,512]{2,1,0:T(8,128)(2,1)S(1)}, bf16[8,16,512]{2,1,0:T(8,128)(2,1)S(1)}, u32[]{:S(2)}, u32[]{:S(2)}) collective-permute-start(bf16[8,16,512]{2,1,0:T(8,128)(2,1)S(1)} %get-tuple-element.49), channel_id=1, source_target_pairs={{0,448},{16,80},{32,480},{48,112},{64,0},{80,144},{96,32},{112,176... | collective-permute-start | bytes 393224 | tf_op jit(solution)/shard_map/ppermute | solution.py:199
  71.2 11.1 %collective-permute-start.5 = (bf16[8,16,512]{2,1,0:T(8,128)(2,1)S(1)}, bf16[8,16,512]{2,1,0:T(8,128)(2,1)S(1)}, u32[]{:S(2)}, u32[]{:S(2)}) collective-permute-start(bf16[8,16,512]{2,1,0:T(8,128)(2,1)S(1)} %get-tuple-element.50), channel_id=1, source_target_pairs={{0,64},{16,464},{32,96},{48,496},{64,128},{80,16},{96,160},{112,48... | collective-permute-start | bytes 393224 | tf_op jit(solution)/shard_map/ppermute | solution.py:199
  74.0 8.3 %collective-permute-start.6 = (bf16[8,16,512]{2,1,0:T(8,128)(2,1)S(1)}, bf16[8,16,512]{2,1,0:T(8,128)(2,1)S(1)}, u32[]{:S(2)}, u32[]{:S(2)}) collective-permute-start(bf16[8,16,512]{2,1,0:T(8,128)(2,1)S(1)} %get-tuple-element.51), channel_id=1, source_target_pairs={{0,480},{16,48},{32,0},{48,80},{64,32},{80,112},{96,64},{112,144},... | collective-permute-start | bytes 393224 | tf_op jit(solution)/shard_map/ppermute | solution.py:199
  76.0 8.7 %collective-permute-start.7 = (bf16[8,16,512]{2,1,0:T(8,128)(2,1)S(1)}, bf16[8,16,512]{2,1,0:T(8,128)(2,1)S(1)}, u32[]{:S(2)}, u32[]{:S(2)}) collective-permute-start(bf16[8,16,512]{2,1,0:T(8,128)(2,1)S(1)} %get-tuple-element.52), channel_id=1, source_target_pairs={{0,32},{16,496},{32,64},{48,16},{64,96},{80,48},{96,128},{112,80},... | collective-permute-start | bytes 393224 | tf_op jit(solution)/shard_map/ppermute | solution.py:199
  114.4 23.4 %collective-permute-start.8 = (bf16[8,16,512]{2,1,0:T(8,128)(2,1)S(1)}, bf16[8,16,512]{2,1,0:T(8,128)(2,1)S(1)}, u32[]{:S(2)}, u32[]{:S(2)}) collective-permute-start(bf16[8,16,512]{2,1,0:T(8,128)(2,1)S(1)} %get-tuple-element.62), channel_id=1, source_target_pairs={{0,384},{16,144},{32,416},{48,176},{64,448},{80,208},{96,480},{112... | collective-permute-start | bytes 393224 | tf_op jit(solution)/shard_map/ppermute | solution.py:199
  121.0 19.3 %collective-permute-start.9 = (bf16[8,16,512]{2,1,0:T(8,128)(2,1)S(1)}, bf16[8,16,512]{2,1,0:T(8,128)(2,1)S(1)}, u32[]{:S(2)}, u32[]{:S(2)}) collective-permute-start(bf16[8,16,512]{2,1,0:T(8,128)(2,1)S(1)} %get-tuple-element.63), channel_id=1, source_target_pairs={{0,96},{16,432},{32,128},{48,464},{64,160},{80,496},{96,192},{112,... | collective-permute-start | bytes 393224 | tf_op jit(solution)/shard_map/ppermute | solution.py:199
  126.0 22.0 %collective-permute-start.10 = (bf16[8,16,512]{2,1,0:T(8,128)(2,1)S(1)}, bf16[8,16,512]{2,1,0:T(8,128)(2,1)S(1)}, u32[]{:S(2)}, u32[]{:S(2)}) collective-permute-start(bf16[8,16,512]{2,1,0:T(8,128)(2,1)S(1)} %get-tuple-element.64), channel_id=1, source_target_pairs={{0,416},{16,112},{32,448},{48,144},{64,480},{80,176},{96,0},{112,2... | collective-permute-start | bytes 393224 | tf_op jit(solution)/shard_map/ppermute | solution.py:199
  129.8 18.1 %collective-permute-start.11 = (bf16[8,16,512]{2,1,0:T(8,128)(2,1)S(1)}, bf16[8,16,512]{2,1,0:T(8,128)(2,1)S(1)}, u32[]{:S(2)}, u32[]{:S(2)}) collective-permute-start(bf16[8,16,512]{2,1,0:T(8,128)(2,1)S(1)} %get-tuple-element.65), channel_id=1, source_target_pairs={{0,64},{16,464},{32,96},{48,496},{64,128},{80,16},{96,160},{112,48... | collective-permute-start | bytes 393224 | tf_op jit(solution)/shard_map/ppermute | solution.py:199
  132.3 15.6 %collective-permute-start.12 = (bf16[8,16,512]{2,1,0:T(8,128)(2,1)S(1)}, bf16[8,16,512]{2,1,0:T(8,128)(2,1)S(1)}, u32[]{:S(2)}, u32[]{:S(2)}) collective-permute-start(bf16[8,16,512]{2,1,0:T(8,128)(2,1)S(1)} %get-tuple-element.66), channel_id=1, source_target_pairs={{0,448},{16,80},{32,480},{48,112},{64,0},{80,144},{96,32},{112,176... | collective-permute-start | bytes 393224 | tf_op jit(solution)/shard_map/ppermute | solution.py:199
  137.8 10.1 %collective-permute-start.13 = (bf16[8,16,512]{2,1,0:T(8,128)(2,1)S(1)}, bf16[8,16,512]{2,1,0:T(8,128)(2,1)S(1)}, u32[]{:S(2)}, u32[]{:S(2)}) collective-permute-start(bf16[8,16,512]{2,1,0:T(8,128)(2,1)S(1)} %get-tuple-element.67), channel_id=1, source_target_pairs={{0,32},{16,496},{32,64},{48,16},{64,96},{80,48},{96,128},{112,80},... | collective-permute-start | bytes 393224 | tf_op jit(solution)/shard_map/ppermute | solution.py:199
  140.3 7.7 %collective-permute-start.14 = (bf16[8,16,512]{2,1,0:T(8,128)(2,1)S(1)}, bf16[8,16,512]{2,1,0:T(8,128)(2,1)S(1)}, u32[]{:S(2)}, u32[]{:S(2)}) collective-permute-start(bf16[8,16,512]{2,1,0:T(8,128)(2,1)S(1)} %get-tuple-element.68), channel_id=1, source_target_pairs={{0,480},{16,48},{32,0},{48,80},{64,32},{80,112},{96,64},{112,144},... | collective-permute-start | bytes 393224 | tf_op jit(solution)/shard_map/ppermute | solution.py:199
  149.6 3.8 %collective-permute-start.15 = (bf16[32,16,512]{2,1,0:T(8,128)(2,1)S(1)}, bf16[32,16,512]{2,1,0:T(8,128)(2,1)S(1)}, u32[]{:S(2)}, u32[]{:S(2)}) collective-permute-start(bf16[32,16,512]{2,1,0:T(8,128)(2,1)S(1)} %get-tuple-element.83), channel_id=1, source_target_pairs={{0,16},{16,0},{1,17},{17,1},{2,18},{18,2},{3,19},{19,3},{4,20},{20... | collective-permute-start | bytes 1572872 | tf_op jit(solution)/shard_map/ppermute | solution.py:232

commit v10 on v6

--- a/solution.py
+++ b/solution.py
@@ -13,6 +13,7 @@
 COPIES = 2
 GROUP = 8
 STEPS = (0, 4, -3, 3, -2, 2, -1, 1)
+FAR = 4
 F32, BF16 = jnp.float32, jnp.bfloat16
 
 VMEM = pl.BlockSpec(memory_space=pltpu.VMEM)
@@ -77,7 +78,8 @@
 
 
 def partner(where, nz, step):
-    return lax.rem(where[0] + (1 - 2 * where[1]) * step + nz, nz)
+    sign = 1 - 2 * where[1] if abs(step) == FAR else 1
+    return lax.rem(where[0] + sign * step + nz, nz)
 
 
 def pick_pieces(nz, table, where, mine, other, *outs):
@@ -195,7 +197,8 @@
     def shift(x, step):
         if step == 0:
             return x
-        pairs = [(z * CORES + c, (z + (step, -step)[c]) % nz * CORES + c) for z in range(nz) for c in range(CORES)]
+        by_core = (step, -step) if abs(step) == FAR else (step, step)
+        pairs = [(z * CORES + c, (z + by_core[c]) % nz * CORES + c) for z in range(nz) for c in range(CORES)]
         return lax.ppermute(x, ("z", "core"), pairs)
 
     def total(part):

time: 194 us -> 197 us (1.015)
  blocking collectives: 109 us -> 112 us
    all_to_all x2, blocking collectives: 80.6 us -> 83.2 us  [over_z(): return lax.all_to_all(x, 'z', 0, 0, tiled=True)]
where the time goes in v10:
time: 197 us; the launch traced here: 196 us
  blocking collectives  112 us (57%)
  starting transfers between devices  61.1 us (31%)
  Pallas kernels  11.2 us (6%)
  waiting for transfers between devices  8.93 us (5%)
    all_to_all x2, blocking collectives, over_z(): return lax.all_to_all(x, 'z', 0, 0, tiled=True)  83.2 us
    ppermute x14, starting transfers between devices, shift(): return lax.ppermute(x, ('z', 'core'), pairs)  57.2 us
    all_to_all x1, blocking collectives, total(): lax.all_to_all(part.reshape(nxy, rows, part.shape[1]), 'xy', 0, 0, tiled=...  16.9 us
    all_to_all x1, blocking collectives, total(): return lax.all_to_all(spread, 'xy', 0, 0, tiled=True).reshape(part.shape)  11.7 us
    pallas_call x9, Pallas kernels, call(): pl.pallas_call(body, out_shape=outs, in_specs=in_specs, out_specs=jax.tre...  11.2 us
    ppermute x14, waiting for transfers between devices, shift(): return lax.ppermute(x, ('z', 'core'), pairs)  5.26 us
  transfers between devices with their start and end apart: 16, of which 4 were waited for; matrix products, arithmetic and copies ran while one was open for 0% of the time, Pallas kernels for 2%

profile of v10, /device:TPU:32, one launch (start us, length us, event | category | flops | bytes accessed | tf_op | source)
XLA Modules:
  0.0 196.0 jit_solution(610338809516537937)
XLA Ops:
  2.8 43.4 %all_to_all.20 = bf16[16,2,16,512]{3,2,1,0:T(8,128)(2,1)S(1)} all-to-all(bf16[16,2,16,512]{3,2,1,0:T(8,128)(2,1)S(1)} %shard_map.84), channel_id=1, replica_groups=mesh['z'=16,'core'=2,'xy'=16] {'z'}, dimensions={0} | all-to-all | bytes 1048576 | tf_op jit(solution)/shard_map/all_to_all | solution.py:195
  46.2 1.9 collective-permute-start
  50.0 2.1 %shard_map.85 = (bf16[8,16,512]{2,1,0:T(8,128)(2,1)S(1)}, bf16[8,16,512]{2,1,0:T(8,128)(2,1)S(1)}, bf16[8,16,512]{2,1,0:T(8,128)(2,1)S(1)}, bf16[8,16,512]{2,1,0...) custom-call(s32[256]{0:T(256)S(1)} %copy-done.4, ...), custom_call_target="tpu_custom_call" | custom-call | tf_op jit(solution)/shard_map/pallas_call | solution.py:32
  52.1 6.0 %collective-permute-start.1 = (bf16[8,16,512]{2,1,0:T(8,128)(2,1)S(1)}, bf16[8,16,512]{2,1,0:T(8,128)(2,1)S(1)}, u32[]{:S(2)}, u32[]{:S(2)}) collective-permute-start(bf16[8,16,512]{2,1,0:T(8,128)(2,1)S(1)} %get-tuple-element.46), channel_id=1, source_target_pairs={{0,128},{16,400},{32,160},{48,432},{64,192},{80,464},{96,224},{112... | collective-permute-start | bytes 393224 | tf_op jit(solution)/shard_map/ppermute | solution.py:202
  58.1 2.9 %collective-permute-start.2 = (bf16[8,16,512]{2,1,0:T(8,128)(2,1)S(1)}, bf16[8,16,512]{2,1,0:T(8,128)(2,1)S(1)}, u32[]{:S(2)}, u32[]{:S(2)}) collective-permute-start(bf16[8,16,512]{2,1,0:T(8,128)(2,1)S(1)} %get-tuple-element.47), channel_id=1, source_target_pairs={{0,416},{16,432},{32,448},{48,464},{64,480},{80,496},{96,0},{112,1... | collective-permute-start | bytes 393224 | tf_op jit(solution)/shard_map/ppermute | solution.py:202
  61.3 5.9 %collective-permute-start.3 = (bf16[8,16,512]{2,1,0:T(8,128)(2,1)S(1)}, bf16[8,16,512]{2,1,0:T(8,128)(2,1)S(1)}, u32[]{:S(2)}, u32[]{:S(2)}) collective-permute-start(bf16[8,16,512]{2,1,0:T(8,128)(2,1)S(1)} %get-tuple-element.48), channel_id=1, source_target_pairs={{0,96},{16,112},{32,128},{48,144},{64,160},{80,176},{96,192},{112,... | collective-permute-start | bytes 393224 | tf_op jit(solution)/shard_map/ppermute | solution.py:202
  67.2 3.9 %collective-permute-start.4 = (bf16[8,16,512]{2,1,0:T(8,128)(2,1)S(1)}, bf16[8,16,512]{2,1,0:T(8,128)(2,1)S(1)}, u32[]{:S(2)}, u32[]{:S(2)}) collective-permute-start(bf16[8,16,512]{2,1,0:T(8,128)(2,1)S(1)} %get-tuple-element.49), channel_id=1, source_target_pairs={{0,448},{16,464},{32,480},{48,496},{64,0},{80,16},{96,32},{112,48}... | collective-permute-start | bytes 393224 | tf_op jit(solution)/shard_map/ppermute | solution.py:202
  71.1 2.8 %collective-permute-start.5 = (bf16[8,16,512]{2,1,0:T(8,128)(2,1)S(1)}, bf16[8,16,512]{2,1,0:T(8,128)(2,1)S(1)}, u32[]{:S(2)}, u32[]{:S(2)}) collective-permute-start(bf16[8,16,512]{2,1,0:T(8,128)(2,1)S(1)} %get-tuple-element.50), channel_id=1, source_target_pairs={{0,64},{16,80},{32,96},{48,112},{64,128},{80,144},{96,160},{112,17... | collective-permute-start | bytes 393224 | tf_op jit(solution)/shard_map/ppermute | solution.py:202
  73.9 1.9 collective-permute-start.6
  75.9 3.9 %collective-permute-start.7 = (bf16[8,16,512]{2,1,0:T(8,128)(2,1)S(1)}, bf16[8,16,512]{2,1,0:T(8,128)(2,1)S(1)}, u32[]{:S(2)}, u32[]{:S(2)}) collective-permute-start(bf16[8,16,512]{2,1,0:T(8,128)(2,1)S(1)} %get-tuple-element.52), channel_id=1, source_target_pairs={{0,32},{16,48},{32,64},{48,80},{64,96},{80,112},{96,128},{112,144}... | collective-permute-start | bytes 393224 | tf_op jit(solution)/shard_map/ppermute | solution.py:202
  79.9 4.4 %collective-permute-done.5.refs_5_ = bf16[8,16,512]{2,1,0:T(8,128)(2,1)S(1)} collective-permute-done((bf16[8,16,512]{2,1,0:T(8,128)(2,1)S(1)}, bf16[8,16,512]{2,1,0:T(8,128)(2,1)S(1)}, u32[]{:S(2)}, u32[]{:S(2)}) %collective-permute-start.5) | collective-permute-done | bytes 131104 | tf_op jit(solution)/shard_map/ppermute | solution.py:202
  85.8 16.9 %all_to_all.21.got = f32[16,64,128]{2,1,0:T(8,128)S(1)} all-to-all(f32[16,64,128]{2,1,0:T(8,128)S(1)} %bitcast.9), channel_id=1, replica_groups=mesh['z'=16,'core'=2,'xy'=16] {'xy'}, dimensions={0} | all-to-all | bytes 1048576 | tf_op jit(solution)/shard_map/all_to_all | solution.py:206
  102.8 11.7 %all_to_all.22 = bf16[16,64,128]{2,1,0:T(8,128)(2,1)S(1)} all-to-all(bf16[16,64,128]{2,1,0:T(8,128)(2,1)S(1)} %shard_map.87), channel_id=1, replica_groups=mesh['z'=16,'core'=2,'xy'=16] {'xy'}, dimensions={0} | all-to-all | bytes 524288 | tf_op jit(solution)/shard_map/all_to_all | solution.py:208
  116.3 6.1 %collective-permute-start.8 = (bf16[8,16,512]{2,1,0:T(8,128)(2,1)S(1)}, bf16[8,16,512]{2,1,0:T(8,128)(2,1)S(1)}, u32[]{:S(2)}, u32[]{:S(2)}) collective-permute-start(bf16[8,16,512]{2,1,0:T(8,128)(2,1)S(1)} %get-tuple-element.62), channel_id=1, source_target_pairs={{0,384},{16,144},{32,416},{48,176},{64,448},{80,208},{96,480},{112... | collective-permute-start | bytes 393224 | tf_op jit(solution)/shard_map/ppermute | solution.py:202
  122.4 4.8 %collective-permute-start.9 = (bf16[8,16,512]{2,1,0:T(8,128)(2,1)S(1)}, bf16[8,16,512]{2,1,0:T(8,128)(2,1)S(1)}, u32[]{:S(2)}, u32[]{:S(2)}) collective-permute-start(bf16[8,16,512]{2,1,0:T(8,128)(2,1)S(1)} %get-tuple-element.63), channel_id=1, source_target_pairs={{0,96},{16,112},{32,128},{48,144},{64,160},{80,176},{96,192},{112,... | collective-permute-start | bytes 393224 | tf_op jit(solution)/shard_map/ppermute | solution.py:202
  127.3 4.0 %collective-permute-start.10 = (bf16[8,16,512]{2,1,0:T(8,128)(2,1)S(1)}, bf16[8,16,512]{2,1,0:T(8,128)(2,1)S(1)}, u32[]{:S(2)}, u32[]{:S(2)}) collective-permute-start(bf16[8,16,512]{2,1,0:T(8,128)(2,1)S(1)} %get-tuple-element.64), channel_id=1, source_target_pairs={{0,416},{16,432},{32,448},{48,464},{64,480},{80,496},{96,0},{112,1... | collective-permute-start | bytes 393224 | tf_op jit(solution)/shard_map/ppermute | solution.py:202
  131.3 2.3 %collective-permute-start.11 = (bf16[8,16,512]{2,1,0:T(8,128)(2,1)S(1)}, bf16[8,16,512]{2,1,0:T(8,128)(2,1)S(1)}, u32[]{:S(2)}, u32[]{:S(2)}) collective-permute-start(bf16[8,16,512]{2,1,0:T(8,128)(2,1)S(1)} %get-tuple-element.65), channel_id=1, source_target_pairs={{0,64},{16,80},{32,96},{48,112},{64,128},{80,144},{96,160},{112,17... | collective-permute-start | bytes 393224 | tf_op jit(solution)/shard_map/ppermute | solution.py:202
  133.6 5.6 %collective-permute-start.12 = (bf16[8,16,512]{2,1,0:T(8,128)(2,1)S(1)}, bf16[8,16,512]{2,1,0:T(8,128)(2,1)S(1)}, u32[]{:S(2)}, u32[]{:S(2)}) collective-permute-start(bf16[8,16,512]{2,1,0:T(8,128)(2,1)S(1)} %get-tuple-element.66), channel_id=1, source_target_pairs={{0,448},{16,464},{32,480},{48,496},{64,0},{80,16},{96,32},{112,48}... | collective-permute-start | bytes 393224 | tf_op jit(solution)/shard_map/ppermute | solution.py:202
  139.3 2.3 %collective-permute-start.13 = (bf16[8,16,512]{2,1,0:T(8,128)(2,1)S(1)}, bf16[8,16,512]{2,1,0:T(8,128)(2,1)S(1)}, u32[]{:S(2)}, u32[]{:S(2)}) collective-permute-start(bf16[8,16,512]{2,1,0:T(8,128)(2,1)S(1)} %get-tuple-element.67), channel_id=1, source_target_pairs={{0,32},{16,48},{32,64},{48,80},{64,96},{80,112},{96,128},{112,144}... | collective-permute-start | bytes 393224 | tf_op jit(solution)/shard_map/ppermute | solution.py:202
  141.6 4.6 %collective-permute-start.14 = (bf16[8,16,512]{2,1,0:T(8,128)(2,1)S(1)}, bf16[8,16,512]{2,1,0:T(8,128)(2,1)S(1)}, u32[]{:S(2)}, u32[]{:S(2)}) collective-permute-start(bf16[8,16,512]{2,1,0:T(8,128)(2,1)S(1)} %get-tuple-element.68), channel_id=1, source_target_pairs={{0,480},{16,496},{32,0},{48,16},{64,32},{80,48},{96,64},{112,80},{... | collective-permute-start | bytes 393224 | tf_op jit(solution)/shard_map/ppermute | solution.py:202
  146.2 3.0 %shard_map.89 = (bf16[1024,512]{1,0:T(8,128)(2,1)}, bf16[1024,512]{1,0:T(8,128)(2,1)}) custom-call(bf16[1024,128]{1,0:T(8,128)(2,1)S(1)} %bitcast.8, bf16[8,16,512]{2,1,0:T(8,128)(2,1)S(1)} %get-tuple-element.53.refs_0_, bf16[8,16,512]{2,1,0:T(8,128)(2,1)S(1)} %collective-permute-done.1.refs_1_, bf16[8,16,512]{2,1,0:T(8,128)(2,1)S(1)} %collective-permute-done.2.refs_2_, ...), custom_call_target="tpu_custom_call" | custom-call | tf_op jit(solution)/shard_map/pallas_call | solution.py:32
  150.9 1.9 collective-permute-start.15
  152.8 1.9 collective-permute-done.15.other
  154.8 39.8 %all_to_all.23.owned = bf16[16,2,16,512]{3,2,1,0:T(8,128)(2,1)S(1)} all-to-all(bf16[16,2,16,512]{3,2,1,0:T(8,128)(2,1)S(1)} %shard_map.91), channel_id=1, replica_groups=mesh['z'=16,'core'=2,'xy'=16] {'z'}, dimensions={0} | all-to-all | bytes 1048576 | tf_op jit(solution)/shard_map/all_to_all | solution.py:195
  (35 shorter events, 10.8 us)
Async XLA Ops:
  0.6 0.9 copy-start.2
  1.5 0.9 copy-start.3
  2.4 47.6 %copy-start.4 = (s32[256]{0:T(256)S(1)}, s32[256]{0:T(256)}, u32[]{:S(2)}) copy-start(s32[256]{0:T(256)} %table.3) | copy-start | bytes 3076
  2.8 82.3 %copy-start = (bf16[1024,512]{1,0:T(8,128)(2,1)S(1)}, bf16[1024,512]{1,0:T(8,128)(2,1)}, u32[]{:S(2)}) copy-start(bf16[1024,512]{1,0:T(8,128)(2,1)} %acts.3) | copy-start | bytes 3145732
  2.8 82.2 %copy-start.1 = (bf16[1024,512]{1,0:T(8,128)(2,1)S(1)}, bf16[1024,512]{1,0:T(8,128)(2,1)}, u32[]{:S(2)}) copy-start(bf16[1024,512]{1,0:T(8,128)(2,1)} %cot.3) | copy-start | bytes 3145732
  46.2 3.8 %collective-permute-start = (bf16[32,16,512]{2,1,0:T(8,128)(2,1)S(1)}, bf16[32,16,512]{2,1,0:T(8,128)(2,1)S(1)}, u32[]{:S(2)}, u32[]{:S(2)}) collective-permute-start(bf16[32,16,512]{2,1,0:T(8,128)(2,1)S(1)} %bitcast.10), channel_id=1, source_target_pairs={{0,16},{16,0},{1,17},{17,1},{2,18},{18,2},{3,19},{19,3},{4,20},{20... | collective-permute-start | bytes 1572872 | tf_op jit(solution)/shard_map/ppermute | solution.py:214
  52.1 21.8 %collective-permute-start.1 = (bf16[8,16,512]{2,1,0:T(8,128)(2,1)S(1)}, bf16[8,16,512]{2,1,0:T(8,128)(2,1)S(1)}, u32[]{:S(2)}, u32[]{:S(2)}) collective-permute-start(bf16[8,16,512]{2,1,0:T(8,128)(2,1)S(1)} %get-tuple-element.46), channel_id=1, source_target_pairs={{0,128},{16,400},{32,160},{48,432},{64,192},{80,464},{96,224},{112... | collective-permute-start | bytes 393224 | tf_op jit(solution)/shard_map/ppermute | solution.py:202
  58.1 17.8 %collective-permute-start.2 = (bf16[8,16,512]{2,1,0:T(8,128)(2,1)S(1)}, bf16[8,16,512]{2,1,0:T(8,128)(2,1)S(1)}, u32[]{:S(2)}, u32[]{:S(2)}) collective-permute-start(bf16[8,16,512]{2,1,0:T(8,128)(2,1)S(1)} %get-tuple-element.47), channel_id=1, source_target_pairs={{0,416},{16,432},{32,448},{48,464},{64,480},{80,496},{96,0},{112,1... | collective-permute-start | bytes 393224 | tf_op jit(solution)/shard_map/ppermute | solution.py:202
  61.3 18.6 %collective-permute-start.3 = (bf16[8,16,512]{2,1,0:T(8,128)(2,1)S(1)}, bf16[8,16,512]{2,1,0:T(8,128)(2,1)S(1)}, u32[]{:S(2)}, u32[]{:S(2)}) collective-permute-start(bf16[8,16,512]{2,1,0:T(8,128)(2,1)S(1)} %get-tuple-element.48), channel_id=1, source_target_pairs={{0,96},{16,112},{32,128},{48,144},{64,160},{80,176},{96,192},{112,... | collective-permute-start | bytes 393224 | tf_op jit(solution)/shard_map/ppermute | solution.py:202
  67.2 12.7 %collective-permute-start.4 = (bf16[8,16,512]{2,1,0:T(8,128)(2,1)S(1)}, bf16[8,16,512]{2,1,0:T(8,128)(2,1)S(1)}, u32[]{:S(2)}, u32[]{:S(2)}) collective-permute-start(bf16[8,16,512]{2,1,0:T(8,128)(2,1)S(1)} %get-tuple-element.49), channel_id=1, source_target_pairs={{0,448},{16,464},{32,480},{48,496},{64,0},{80,16},{96,32},{112,48}... | collective-permute-start | bytes 393224 | tf_op jit(solution)/shard_map/ppermute | solution.py:202
  71.1 13.1 %collective-permute-start.5 = (bf16[8,16,512]{2,1,0:T(8,128)(2,1)S(1)}, bf16[8,16,512]{2,1,0:T(8,128)(2,1)S(1)}, u32[]{:S(2)}, u32[]{:S(2)}) collective-permute-start(bf16[8,16,512]{2,1,0:T(8,128)(2,1)S(1)} %get-tuple-element.50), channel_id=1, source_target_pairs={{0,64},{16,80},{32,96},{48,112},{64,128},{80,144},{96,160},{112,17... | collective-permute-start | bytes 393224 | tf_op jit(solution)/shard_map/ppermute | solution.py:202
  73.9 10.3 %collective-permute-start.6 = (bf16[8,16,512]{2,1,0:T(8,128)(2,1)S(1)}, bf16[8,16,512]{2,1,0:T(8,128)(2,1)S(1)}, u32[]{:S(2)}, u32[]{:S(2)}) collective-permute-start(bf16[8,16,512]{2,1,0:T(8,128)(2,1)S(1)} %get-tuple-element.51), channel_id=1, source_target_pairs={{0,480},{16,496},{32,0},{48,16},{64,32},{80,48},{96,64},{112,80},{... | collective-permute-start | bytes 393224 | tf_op jit(solution)/shard_map/ppermute | solution.py:202
  75.9 9.2 %collective-permute-start.7 = (bf16[8,16,512]{2,1,0:T(8,128)(2,1)S(1)}, bf16[8,16,512]{2,1,0:T(8,128)(2,1)S(1)}, u32[]{:S(2)}, u32[]{:S(2)}) collective-permute-start(bf16[8,16,512]{2,1,0:T(8,128)(2,1)S(1)} %get-tuple-element.52), channel_id=1, source_target_pairs={{0,32},{16,48},{32,64},{48,80},{64,96},{80,112},{96,128},{112,144}... | collective-permute-start | bytes 393224 | tf_op jit(solution)/shard_map/ppermute | solution.py:202
  116.3 23.0 %collective-permute-start.8 = (bf16[8,16,512]{2,1,0:T(8,128)(2,1)S(1)}, bf16[8,16,512]{2,1,0:T(8,128)(2,1)S(1)}, u32[]{:S(2)}, u32[]{:S(2)}) collective-permute-start(bf16[8,16,512]{2,1,0:T(8,128)(2,1)S(1)} %get-tuple-element.62), channel_id=1, source_target_pairs={{0,384},{16,144},{32,416},{48,176},{64,448},{80,208},{96,480},{112... | collective-permute-start | bytes 393224 | tf_op jit(solution)/shard_map/ppermute | solution.py:202
  122.4 19.2 %collective-permute-start.9 = (bf16[8,16,512]{2,1,0:T(8,128)(2,1)S(1)}, bf16[8,16,512]{2,1,0:T(8,128)(2,1)S(1)}, u32[]{:S(2)}, u32[]{:S(2)}) collective-permute-start(bf16[8,16,512]{2,1,0:T(8,128)(2,1)S(1)} %get-tuple-element.63), channel_id=1, source_target_pairs={{0,96},{16,112},{32,128},{48,144},{64,160},{80,176},{96,192},{112,... | collective-permute-start | bytes 393224 | tf_op jit(solution)/shard_map/ppermute | solution.py:202
  127.3 22.0 %collective-permute-start.10 = (bf16[8,16,512]{2,1,0:T(8,128)(2,1)S(1)}, bf16[8,16,512]{2,1,0:T(8,128)(2,1)S(1)}, u32[]{:S(2)}, u32[]{:S(2)}) collective-permute-start(bf16[8,16,512]{2,1,0:T(8,128)(2,1)S(1)} %get-tuple-element.64), channel_id=1, source_target_pairs={{0,416},{16,432},{32,448},{48,464},{64,480},{80,496},{96,0},{112,1... | collective-permute-start | bytes 393224 | tf_op jit(solution)/shard_map/ppermute | solution.py:202
  131.3 18.0 %collective-permute-start.11 = (bf16[8,16,512]{2,1,0:T(8,128)(2,1)S(1)}, bf16[8,16,512]{2,1,0:T(8,128)(2,1)S(1)}, u32[]{:S(2)}, u32[]{:S(2)}) collective-permute-start(bf16[8,16,512]{2,1,0:T(8,128)(2,1)S(1)} %get-tuple-element.65), channel_id=1, source_target_pairs={{0,64},{16,80},{32,96},{48,112},{64,128},{80,144},{96,160},{112,17... | collective-permute-start | bytes 393224 | tf_op jit(solution)/shard_map/ppermute | solution.py:202
  133.6 15.6 %collective-permute-start.12 = (bf16[8,16,512]{2,1,0:T(8,128)(2,1)S(1)}, bf16[8,16,512]{2,1,0:T(8,128)(2,1)S(1)}, u32[]{:S(2)}, u32[]{:S(2)}) collective-permute-start(bf16[8,16,512]{2,1,0:T(8,128)(2,1)S(1)} %get-tuple-element.66), channel_id=1, source_target_pairs={{0,448},{16,464},{32,480},{48,496},{64,0},{80,16},{96,32},{112,48}... | collective-permute-start | bytes 393224 | tf_op jit(solution)/shard_map/ppermute | solution.py:202
  139.3 10.0 %collective-permute-start.13 = (bf16[8,16,512]{2,1,0:T(8,128)(2,1)S(1)}, bf16[8,16,512]{2,1,0:T(8,128)(2,1)S(1)}, u32[]{:S(2)}, u32[]{:S(2)}) collective-permute-start(bf16[8,16,512]{2,1,0:T(8,128)(2,1)S(1)} %get-tuple-element.67), channel_id=1, source_target_pairs={{0,32},{16,48},{32,64},{48,80},{64,96},{80,112},{96,128},{112,144}... | collective-permute-start | bytes 393224 | tf_op jit(solution)/shard_map/ppermute | solution.py:202
  141.6 7.7 %collective-permute-start.14 = (bf16[8,16,512]{2,1,0:T(8,128)(2,1)S(1)}, bf16[8,16,512]{2,1,0:T(8,128)(2,1)S(1)}, u32[]{:S(2)}, u32[]{:S(2)}) collective-permute-start(bf16[8,16,512]{2,1,0:T(8,128)(2,1)S(1)} %get-tuple-element.68), channel_id=1, source_target_pairs={{0,480},{16,496},{32,0},{48,16},{64,32},{80,48},{96,64},{112,80},{... | collective-permute-start | bytes 393224 | tf_op jit(solution)/shard_map/ppermute | solution.py:202
  150.9 3.8 %collective-permute-start.15 = (bf16[32,16,512]{2,1,0:T(8,128)(2,1)S(1)}, bf16[32,16,512]{2,1,0:T(8,128)(2,1)S(1)}, u32[]{:S(2)}, u32[]{:S(2)}) collective-permute-start(bf16[32,16,512]{2,1,0:T(8,128)(2,1)S(1)} %get-tuple-element.83), channel_id=1, source_target_pairs={{0,16},{16,0},{1,17},{17,1},{2,18},{18,2},{3,19},{19,3},{4,20},{20... | collective-permute-start | bytes 1572872 | tf_op jit(solution)/shard_map/ppermute | solution.py:235
